TPU v7x, 128 devices: a whole 4x4x4 slice. The times are simulated.
128 devices in a mesh: gx: 8 (over z, core), gy: 16 (over x, y).
Axes of the slice: x: 4, y: 4, z: 4, core: 2. Of those that a mesh axis runs over, the one named last changes fastest.
Arguments:
- displacement: float32 [3, 256, 5, 2048], P(None, 'gx', None, 'gy'), may hold values from -5 to 5
- velocity: float32 [3, 256, 5, 2048], P(None, 'gx', None, 'gy'), may hold values from -4 to 4
- stiffness: float32 [256, 5, 2048], P('gx', None, 'gy'), may hold values from 0.5 to 2
- inverse_mass: float32 [256, 5, 2048], P('gx', None, 'gy'), may hold values from 0.5 to 2
- facing: int32 [256, 16, 8], P('gx', 'gy'), may hold values from 0 to 4095, as said below
Outputs:
- final_displacement: float32 [3, 256, 5, 2048], P(None, 'gx', None, 'gy')
- final_velocity: float32 [3, 256, 5, 2048], P(None, 'gx', None, 'gy')
Inputs may be any that keep to these rules, and one draw needn't show every extreme that they name: facing[x, j, k] names block x' * 16 + j'. For each aligned run of 32 rows x and each j, the 256 entries name blocks with each pair (x' // 32, j') exactly 2 times; repeats are allowed.
All inputs are finite; a program needn't handle non-finite values.
Results may differ from a plain program's by a relative error of at most 0.0001.
Values sent between devices are 32-bit elements; how exact they have to be, the bound alone decides.
No kernel may reach another device: no remote copies, remote signals or barrier semaphores. Data moves between devices by JAX's collectives and lax.ppermute only.
A program may use at most 64 MiB of HBM per device.

v0:
```python
import jax
import jax.numpy as jnp
import numpy as np
from jax import lax
from jax.experimental import pallas as pl
from jax.experimental.pallas import tpu as pltpu
from jax.sharding import PartitionSpec as P

STEPS = 2
AXES = ("gx", "gy")
NODES = 128
ROWS = 32
DEPTH = 5
FACES = 8
ENTRIES = ROWS * FACES
UNROLL = 4

time_step = 0.2
stiff_coef = 4.0 / (8.0 * NODES)
damp_coef = 1.0 / (8.0 * NODES)
exponent_scale = float(np.sqrt(np.log2(np.e) / 2.0))
frame_extent = 4.0

f32 = jnp.float32
bf16 = jnp.bfloat16
PARAMS = pltpu.CompilerParams(vmem_limit_bytes=48 * 1024 * 1024)


def sublanes(shape):
    return lax.broadcasted_iota(jnp.int32, shape, 0)


def lanes(shape):
    return lax.broadcasted_iota(jnp.int32, shape, 1)


def split3(value):
    high = value.astype(bf16).astype(f32)
    rest = value - high
    middle = rest.astype(bf16).astype(f32)
    return high, middle, rest - middle


def frame_tile():
    shape = (8, NODES)
    place = (lanes(shape).astype(f32) - (NODES - 1) / 2.0) * (frame_extent / NODES)
    return jnp.where(sublanes(shape) == 1, place, 0.0)


def tile_constants():
    row = sublanes((8, NODES))
    return frame_tile(), (row < 3).astype(f32), (row == 3).astype(f32), (row == 4).astype(f32)


def tile_parts(disp, vel, consts):
    frame, first3, row3, _ = consts
    place = disp + frame
    scaled = (place * exponent_scale) * first3
    half = 0.5 * jnp.sum(scaled * scaled, axis=0, keepdims=True)
    potential = (stiff_coef * place - damp_coef * vel) * first3 + row3
    return scaled, half, potential


def far_factor(scaled, half, consts):
    h, m, l = split3(scaled + half * consts[2] + consts[3])
    return jnp.concatenate([h, m, h, m, l, h], axis=0).astype(bf16)


def near_factor(scaled, half, consts):
    h, m, l = split3(scaled - consts[2] - half * consts[3])
    return jnp.concatenate([h, h, m, m, h, l], axis=0).astype(bf16)


def packed_potential(potential):
    h, m, l = split3(potential)
    return jnp.concatenate([h + pltpu.roll(m, 4, 0), l], axis=0).astype(bf16)


def fold(total):
    total = total[:8] + total[8:]
    return total + pltpu.roll(total, 4, 0)


def request_kernel(facing_ref, disp_ref, vel_ref, send_ref, slot_ref, surf_ref, count_ref):
    def clear(i, carry):
        count_ref[i] = 0
        return carry

    lax.fori_loop(0, NODES, clear, 0, unroll=16)
    zero = jnp.zeros((ROWS, NODES), f32)
    for c in range(3):
        surf_ref[:, c, :] = disp_ref[c]
        surf_ref[:, 3 + c, :] = vel_ref[c]
        if c < 2:
            surf_ref[:, 6 + c, :] = zero
    row6 = (sublanes((8, NODES)) == 6).astype(f32)

    def visit(b, carry):
        tile = surf_ref[b]
        for k in range(FACES):
            name = facing_ref[k, b]
            block = lax.shift_right_logical(name, 4)
            owner = lax.shift_left(lax.shift_right_logical(block, 5), 4) | (name & 15)
            used = count_ref[owner]
            count_ref[owner] = used + 1
            slot = 2 * owner + used
            slot_ref[b * FACES + k] = slot
            send_ref[slot] = tile + row6 * jnp.full((8, NODES), block & 31, jnp.int32).astype(f32)
        return carry

    lax.fori_loop(0, ROWS, visit, 0)


def edge_rows(value, x):
    return [value[c, z, x : x + 1, :] for c in range(value.shape[0]) for z in range(DEPTH)]


def edge_kernel(with_stiff, disp_ref, stiff_ref, last_ref, low_row, high_row, low_col, high_col, masked_ref):
    shape = (ROWS, NODES)
    lane = lanes(shape)
    if with_stiff:
        row = sublanes(shape)
        keep = ((row < ROWS - 1) | (last_ref[0] == 0)) & ((lane < NODES - 1) | (last_ref[1] == 0))
        for z in range(DEPTH):
            if z < DEPTH - 1:
                masked_ref[z] = jnp.where(keep, stiff_ref[z], 0.0)
            else:
                masked_ref[z] = jnp.zeros(shape, f32)
    low = jnp.zeros(shape, f32)
    high = jnp.zeros(shape, f32)
    low_row[...] = jnp.zeros((24, NODES), f32)
    high_row[...] = jnp.zeros((24, NODES), f32)
    for c in range(4 if with_stiff else 3):
        for z in range(DEPTH):
            at = c * DEPTH + z
            value = disp_ref[c, z] if c < 3 else masked_ref[z]
            low_row[at : at + 1, :] = value[0:1, :]
            high_row[at : at + 1, :] = value[ROWS - 1 :, :]
            low = jnp.where(lane == at, pltpu.roll(value, at, 1) if at else value, low)
            high = jnp.where(lane == at, pltpu.roll(value, at + 1, 1), high)
    low_col[...] = low
    high_col[...] = high


def extended(center, above, below):
    row = sublanes((8, NODES))
    tail = jnp.where(row == 0, below, jnp.where(row == 7, above, 0.0))
    return jnp.concatenate([center, tail], axis=0)


def force_kernel(with_stiff, disp_ref, stiff_ref, row_lo, row_hi, col_lo, col_hi, c_ll, c_hl, c_lh, c_hh, *rest):
    if with_stiff:
        surf_ref, force_ref, wide_ref, node_ref, near_ref, pot_ref, exact_ref = rest
    else:
        wide_in, node_in, surf_ref, force_ref, near_ref, pot_ref, exact_ref = rest
    wide = (ROWS + 8, NODES)
    lane = lanes(wide)
    last = lane == NODES - 1
    left = extended(col_lo[...], c_ll[7:8, :], c_hl[0:1, :])
    right = extended(col_hi[...], c_lh[7:8, :], c_hh[0:1, :])

    def own(c, z):
        value = disp_ref[c, z] if c < 3 else stiff_ref[z]
        at = c * DEPTH + z
        return extended(value, row_lo[at : at + 1, :], row_hi[at : at + 1, :])

    def at_last(cols, at):
        return pltpu.roll(cols, NODES - 1 - at, 1)

    def spread(main, side):
        main = main + pltpu.roll(main, 1, 0)
        side = side + pltpu.roll(side, 1, 0)
        return main + pltpu.roll(jnp.where(last, side, main), 1, 1)

    stiff = []
    if with_stiff:
        total = None
        for z in range(DEPTH - 1):
            main = own(3, z)
            side = at_last(left, 3 * DEPTH + z)
            wide_ref[z, 0] = main
            wide_ref[z, 1] = side
            stiff.append((main * 0.125, side * 0.125))
            out = spread(main, side)[:ROWS]
            node_ref[z] = out if total is None else total + out
            total = out
        node_ref[DEPTH - 1] = total
        node = node_ref
    else:
        for z in range(DEPTH - 1):
            stiff.append((wide_in[z, 0] * 0.125, wide_in[z, 1] * 0.125))
        node = node_in
    for c in range(3):
        boxes = []
        for z in range(DEPTH):
            value = own(c, z)
            turned = pltpu.roll(value, NODES - 1, 1)
            main = value + jnp.where(last, at_last(right, c * DEPTH + z), turned)
            side = at_last(left, c * DEPTH + z) + turned
            boxes.append((main, side))
        total = None
        for z in range(DEPTH):
            out = None
            if z < DEPTH - 1:
                main = boxes[z][0] + boxes[z + 1][0]
                side = boxes[z][1] + boxes[z + 1][1]
                main = main + pltpu.roll(main, ROWS + 7, 0)
                side = side + pltpu.roll(side, ROWS + 7, 0)
                out = spread(main * stiff[z][0], side * stiff[z][1])[:ROWS]
                pull = out if total is None else total + out
            else:
                pull = total
            total = out
            force_ref[c, z] = pull - disp_ref[c, z] * node[z]

    consts = tile_constants()
    unit = (lanes((NODES, NODES)) == sublanes((NODES, NODES))).astype(bf16)

    def table(b, carry):
        tile = surf_ref[b]
        scaled, half, potential = tile_parts(tile, pltpu.roll(tile, 5, 0), consts)
        near = near_factor(scaled, half, consts)
        turned = lax.dot_general(unit, near, (((1,), (1,)), ((), ())), preferred_element_type=f32)
        near_ref[b] = turned.astype(bf16)
        pot_ref[b] = packed_potential(potential)
        exact_ref[b] = potential
        return carry

    lax.fori_loop(0, ROWS, table, 0, unroll=4)


def contact_kernel(moved, row_ref, *rest):
    if moved:
        recv_ref, vel_ref, near_ref, pot_ref, out_ref, loc_ref = rest
    else:
        recv_ref, near_ref, pot_ref, out_ref, loc_ref = rest
    loc_ref[...] = jnp.zeros((ROWS, 8, NODES), f32)
    consts = tile_constants()

    def visit(step, carry):
        for j in range(UNROLL):
            e = step * UNROLL + j
            tile = recv_ref[e]
            if moved:
                vel = jnp.concatenate([vel_ref[e], jnp.zeros((4, NODES), f32)], axis=0)
                disp = tile + time_step * vel
            else:
                vel = pltpu.roll(tile, 5, 0)
                disp = tile
            scaled, half, potential = tile_parts(disp, vel, consts)
            far = far_factor(scaled, half, consts)
            far_pot = packed_potential(potential)
            r = row_ref[e]
            weight = jnp.exp2(jnp.dot(near_ref[r], far, preferred_element_type=f32))
            high = weight.astype(bf16)
            low = (weight - high.astype(f32)).astype(bf16)
            near_pot = pot_ref[r]
            pulled = fold(
                jnp.dot(
                    jnp.concatenate([near_pot, near_pot], axis=1),
                    jnp.concatenate([high, low], axis=0),
                    preferred_element_type=f32,
                )
            )
            out_ref[e] = (pulled[3:4] * potential - pulled)[:4]
            pushed = lax.dot_general(
                jnp.concatenate([far_pot, far_pot], axis=1),
                jnp.concatenate([high, low], axis=1),
                (((1,), (1,)), ((), ())),
                preferred_element_type=f32,
            )
            loc_ref[r] += pushed[:8] + pushed[8:]
        return carry

    lax.fori_loop(0, ENTRIES // UNROLL, visit, 0)


def update_kernel(
    final, slot_ref, ret_ref, loc_ref, exact_ref, force_ref, disp_ref, vel_ref, mass_ref, new_disp, new_vel, *rest
):
    if final:
        (sum_ref,) = rest
    else:
        send_ref, surf_ref, sum_ref = rest

    def gather(b, carry):
        total = loc_ref[b]
        total = total + pltpu.roll(total, 4, 0)
        acc = (total[3:4] * exact_ref[b] - total)[:4]
        for k in range(FACES):
            acc = acc + ret_ref[slot_ref[b * FACES + k]]
        sum_ref[b] = acc
        return carry

    lax.fori_loop(0, ROWS, gather, 0, unroll=4)
    if not final:
        for c in range(2):
            surf_ref[:, 6 + c, :] = jnp.zeros((ROWS, NODES), f32)
    for z in range(DEPTH):
        mass = time_step * mass_ref[z]
        for c in range(3):
            force = force_ref[c, z]
            if z == DEPTH - 1:
                force = force + sum_ref[:, c, :]
            vel = vel_ref[c, z] + mass * force
            disp = disp_ref[c, z] + time_step * vel
            new_vel[c, z] = vel
            new_disp[c, z] = disp
            if z == DEPTH - 1 and not final:
                surf_ref[:, c, :] = disp
                surf_ref[:, 3 + c, :] = vel
    if final:
        return

    def scatter(b, carry):
        tile = pltpu.roll(surf_ref[b], 5, 0)[:4]
        for k in range(FACES):
            send_ref[slot_ref[b * FACES + k]] = tile
        return carry

    lax.fori_loop(0, ROWS, scatter, 0, unroll=4)


VMEM = pl.BlockSpec(memory_space=pltpu.VMEM)
SMEM = pl.BlockSpec(memory_space=pltpu.SMEM)


def struct(*shape, dtype=f32):
    return jax.ShapeDtypeStruct(shape, dtype)


def shifted(value, count_gx, count_gy, dx, dy):
    pairs = []
    for x in range(count_gx):
        for y in range(count_gy):
            if 0 <= x + dx < count_gx and 0 <= y + dy < count_gy:
                pairs.append((x * count_gy + y, (x + dx) * count_gy + y + dy))
    return lax.ppermute(value, AXES, pairs)


def halo(edges, count_gx, count_gy):
    low_row, high_row, low_col, high_col = edges

    def go(value, dx, dy):
        return shifted(value, count_gx, count_gy, dx, dy)

    return (
        go(high_row, 1, 0),
        go(low_row, -1, 0),
        go(high_col, 0, 1),
        go(low_col, 0, -1),
        go(high_col[ROWS - 8 :], 1, 1),
        go(high_col[:8], -1, 1),
        go(low_col[ROWS - 8 :], 1, -1),
        go(low_col[:8], -1, -1),
    )


def local(displacement, velocity, stiffness, inverse_mass, facing):
    count_gx = lax.axis_size("gx")
    count_gy = lax.axis_size("gy")
    disp = displacement.transpose(0, 2, 1, 3)
    vel = velocity.transpose(0, 2, 1, 3)
    stiff = stiffness.transpose(1, 0, 2)
    mass = inverse_mass.transpose(1, 0, 2)
    faces = facing.transpose(1, 2, 0).reshape(FACES, ROWS)
    ends = jnp.stack(
        [
            (lax.axis_index("gx") == count_gx - 1).astype(jnp.int32),
            (lax.axis_index("gy") == count_gy - 1).astype(jnp.int32),
        ]
    )
    plane = (3, 1, ROWS, NODES)
    top = pl.BlockSpec((3, None, ROWS, NODES), lambda i: (0, DEPTH - 1, 0, 0))
    send, slots, surf = pl.pallas_call(
        request_kernel,
        grid=(1,),
        in_specs=[SMEM, top, top],
        out_specs=[VMEM, SMEM, VMEM],
        out_shape=[struct(ENTRIES, 8, NODES), struct(ENTRIES, dtype=jnp.int32), struct(ROWS, 8, NODES)],
        scratch_shapes=[pltpu.SMEM((NODES,), jnp.int32)],
        compiler_params=PARAMS,
        name="request",
    )(faces, disp, vel)
    first_recv = lax.all_to_all(send, AXES, 0, 0, tiled=True)
    wide = node = None
    edge_shapes = [struct(24, NODES), struct(24, NODES), struct(ROWS, NODES), struct(ROWS, NODES)]
    table_shapes = [
        struct(ROWS, NODES, 48, dtype=bf16),
        struct(ROWS, 16, NODES, dtype=bf16),
        struct(ROWS, 8, NODES),
    ]
    force_shape = [struct(3, DEPTH, ROWS, NODES)]
    for step in range(STEPS):
        if step == 0:
            *edges, masked = pl.pallas_call(
                lambda d, s, e, *outs: edge_kernel(True, d, s, e, *outs),
                in_specs=[VMEM, VMEM, SMEM],
                out_specs=[VMEM] * 5,
                out_shape=edge_shapes + [struct(DEPTH, ROWS, NODES)],
                compiler_params=PARAMS,
                name="edges_first",
            )(disp, stiff, ends)
            around = halo(edges, count_gx, count_gy)
            force, wide, node, near, pot, exact = pl.pallas_call(
                lambda *refs: force_kernel(True, *refs),
                in_specs=[VMEM] * 11,
                out_specs=[VMEM] * 6,
                out_shape=force_shape
                + [struct(DEPTH - 1, 2, ROWS + 8, NODES), struct(DEPTH, ROWS, NODES)]
                + table_shapes,
                compiler_params=PARAMS,
                name="force_first",
            )(disp, masked, *around, surf)
            rows = first_recv[:, 6, 0].astype(jnp.int32)
            extra = ()
        else:
            edges = pl.pallas_call(
                lambda d, *outs: edge_kernel(False, d, None, None, *outs, None),
                in_specs=[VMEM],
                out_specs=[VMEM] * 4,
                out_shape=edge_shapes,
                compiler_params=PARAMS,
                name="edges_next",
            )(disp)
            around = halo(edges, count_gx, count_gy)
            force, near, pot, exact = pl.pallas_call(
                lambda d, *refs: force_kernel(False, d, None, *refs),
                in_specs=[VMEM] * 12,
                out_specs=[VMEM] * 4,
                out_shape=force_shape + table_shapes,
                compiler_params=PARAMS,
                name="force_next",
            )(disp, *around, wide, node, surf)
            extra = (lax.all_to_all(send, AXES, 0, 0, tiled=True),)
        moved = step > 0
        action, reaction = pl.pallas_call(
            lambda *refs, moved=moved: contact_kernel(moved, *refs),
            in_specs=[SMEM] + [VMEM] * (3 + len(extra)),
            out_specs=[VMEM] * 2,
            out_shape=[struct(ENTRIES, 4, NODES), struct(ROWS, 8, NODES)],
            compiler_params=PARAMS,
            name="contact",
        )(rows, first_recv, *extra, near, pot)
        returned = lax.all_to_all(action, AXES, 0, 0, tiled=True)
        final = step == STEPS - 1
        outs = [struct(3, DEPTH, ROWS, NODES), struct(3, DEPTH, ROWS, NODES)]
        if not final:
            outs += [struct(ENTRIES, 4, NODES), struct(ROWS, 8, NODES)]
        disp, vel, *rest = pl.pallas_call(
            lambda *refs, final=final: update_kernel(final, *refs),
            in_specs=[SMEM] + [VMEM] * 7,
            out_specs=[VMEM] * len(outs),
            out_shape=outs,
            scratch_shapes=[pltpu.VMEM((ROWS, 4, NODES), f32)],
            compiler_params=PARAMS,
            name="update",
        )(slots, returned, reaction, exact, force, disp, vel, mass)
        if not final:
            send, surf = rest
    return disp.transpose(0, 2, 1, 3), vel.transpose(0, 2, 1, 3)


def solution(mesh):
    in_specs = (
        P(None, "gx", None, "gy"),
        P(None, "gx", None, "gy"),
        P("gx", None, "gy"),
        P("gx", None, "gy"),
        P("gx", "gy", None),
    )
    out_specs = (P(None, "gx", None, "gy"), P(None, "gx", None, "gy"))
    return jax.shard_map(local, mesh=mesh, in_specs=in_specs, out_specs=out_specs, check_vma=False)
```

profile of v0, /device:TPU:7, one launch (start us, length us, event | category | flops | bytes accessed | tf_op | source)
XLA Modules:
  0.0 229.5 jit_solution(12620261781271657033)
XLA Ops:
  3.2 3.2 %request.1 = (f32[256,8,128]{2,1,0:T(8,128)}, s32[256]{0:T(256)S(1)}, f32[32,8,128]{2,1,0:T(8,128)S(1)}) custom-call(s32[8,32]{1,0:T(8,128)S(1)} %bitcast.20, f32[3,5,32,128]{3,2,1,0:T(8,128)S(1)} %bitcast.11, f32[3,5,32,128]{3,2,1,0:T(8,128)S(1)} %bitcast.15), custom_call_target="tpu_custom_call" | custom-call | tf_op jit(solution)/shard_map/request/pallas_call | solution.py:375
  6.5 10.8 %all-to-all-start = ((f32[256,8,128]{2,1,0:T(8,128)}), f32[256,8,128]{2,1,0:T(8,128)S(1)}, u32[]{:S(2)}, u32[]{:S(2)}) async-start(f32[256,8,128]{2,1,0:T(8,128)} %get-tuple-element.35), calls=%async_computation | async-start | bytes 2097152 | tf_op jit(solution)/shard_map/all_to_all | solution.py:385
  18.1 4.9 %collective-permute-start.7 = (f32[8,128]{1,0:T(8,128)S(1)}, f32[8,128]{1,0:T(8,128)S(1)}, u32[]{:S(2)}, u32[]{:S(2)}) collective-permute-start(f32[8,128]{1,0:T(8,128)S(1)} %get-tuple-element.70), channel_id=1, source_target_pairs={{17,0},{18,1},{19,2},{20,3},{21,4},{22,5},{23,6},{24,7},{25,8},{26... | collective-permute-start | bytes 12296 | tf_op jit(solution)/shard_map/ppermute | solution.py:338
  23.1 2.4 %collective-permute-start.3 = (f32[32,128]{1,0:T(8,128)S(1)}, f32[32,128]{1,0:T(8,128)S(1)}, u32[]{:S(2)}, u32[]{:S(2)}) collective-permute-start(f32[32,128]{1,0:T(8,128)S(1)} %get-tuple-element.40), channel_id=1, source_target_pairs={{1,0},{2,1},{3,2},{4,3},{5,4},{6,5},{7,6},{8,7},{9,8},{10,9},{11,1... | collective-permute-start | bytes 49160 | tf_op jit(solution)/shard_map/ppermute | solution.py:338
  25.5 3.4 %collective-permute-start.6 = (f32[8,128]{1,0:T(8,128)S(1)}, f32[8,128]{1,0:T(8,128)S(1)}, u32[]{:S(2)}, u32[]{:S(2)}) collective-permute-start(f32[8,128]{1,0:T(8,128)S(1)} %get-tuple-element.71), channel_id=1, source_target_pairs={{1,16},{2,17},{3,18},{4,19},{5,20},{6,21},{7,22},{8,23},{9,24},{10... | collective-permute-start | bytes 12296 | tf_op jit(solution)/shard_map/ppermute | solution.py:338
  28.9 2.4 %collective-permute-start = (f32[24,128]{1,0:T(8,128)S(1)}, f32[24,128]{1,0:T(8,128)S(1)}, u32[]{:S(2)}, u32[]{:S(2)}) collective-permute-start(f32[24,128]{1,0:T(8,128)S(1)} %get-tuple-element.37), channel_id=1, source_target_pairs={{0,16},{1,17},{2,18},{3,19},{4,20},{5,21},{6,22},{7,23},{8,24},{9,... | collective-permute-start | bytes 36872 | tf_op jit(solution)/shard_map/ppermute | solution.py:338
  33.2 3.1 %collective-permute-start.2 = (f32[32,128]{1,0:T(8,128)S(1)}, f32[32,128]{1,0:T(8,128)S(1)}, u32[]{:S(2)}, u32[]{:S(2)}) collective-permute-start(f32[32,128]{1,0:T(8,128)S(1)} %get-tuple-element.39), channel_id=1, source_target_pairs={{0,1},{1,2},{2,3},{3,4},{4,5},{5,6},{6,7},{7,8},{8,9},{9,10},{10,1... | collective-permute-start | bytes 49160 | tf_op jit(solution)/shard_map/ppermute | solution.py:338
  36.4 2.4 %collective-permute-start.5 = (f32[8,128]{1,0:T(8,128)S(1)}, f32[8,128]{1,0:T(8,128)S(1)}, u32[]{:S(2)}, u32[]{:S(2)}) collective-permute-start(f32[8,128]{1,0:T(8,128)S(1)} %get-tuple-element.72), channel_id=1, source_target_pairs={{16,1},{17,2},{18,3},{19,4},{20,5},{21,6},{22,7},{23,8},{24,9},{25... | collective-permute-start | bytes 12296 | tf_op jit(solution)/shard_map/ppermute | solution.py:338
  38.8 5.5 %collective-permute-done.5.refs_7_ = f32[8,128]{1,0:T(8,128)S(1)} collective-permute-done((f32[8,128]{1,0:T(8,128)S(1)}, f32[8,128]{1,0:T(8,128)S(1)}, u32[]{:S(2)}, u32[]{:S(2)}) %collective-permute-start.5) | collective-permute-done | bytes 4128 | tf_op jit(solution)/shard_map/ppermute | solution.py:338
  46.2 5.1 %collective-permute-done.4.refs_6_ = f32[8,128]{1,0:T(8,128)S(1)} collective-permute-done((f32[8,128]{1,0:T(8,128)S(1)}, f32[8,128]{1,0:T(8,128)S(1)}, u32[]{:S(2)}, u32[]{:S(2)}) %collective-permute-start.4) | collective-permute-done | bytes 4128 | tf_op jit(solution)/shard_map/ppermute | solution.py:338
  54.1 4.6 %fusion.refs_0_ = s32[256]{0:T(256)S(1)} fusion(f32[256,8,128]{2,1,0:T(8,128)S(1)} %all-to-all-done.refs_1_), kind=kLoop, calls=%fused_computation.1 | loop fusion | flops 256 | bytes 2048 | tf_op jit(solution)/shard_map/convert_element_type | solution.py:415
  58.8 41.7 %contact.2 = (f32[256,4,128]{2,1,0:T(4,128)S(1)}, f32[32,8,128]{2,1,0:T(8,128)S(1)}) custom-call(s32[256]{0:T(256)S(1)} %fusion.refs_0_, f32[256,8,128]{2,1,0:T(8,128)S(1)} %all-to-all-done.refs_1_, bf16[32,128,48]{2,1,0:T(8,128)(2,1)S(1)} %get-tuple-element.42.refs_2_, bf16[32,16,128]{2,1,0:T(8,128)(2,1)S(1)} %get-tuple-element.43.refs_3_), custom_call_target="tpu_custom_call" | custom-call | tf_op jit(solution)/shard_map/contact/pallas_call | solution.py:437
  100.5 19.4 %all_to_all.20.refs_1_ = f32[256,4,128]{2,1,0:T(4,128)S(1)} all-to-all(f32[256,4,128]{2,1,0:T(4,128)S(1)} %get-tuple-element.44), channel_id=1, replica_groups=mesh['gx'=8,'gy'=16] {'gx','gy'}, dimensions={0} | all-to-all | bytes 1048576 | tf_op jit(solution)/shard_map/all_to_all | solution.py:445
  122.7 5.9 %all-to-all-start.2 = ((f32[256,4,128]{2,1,0:T(4,128)}), f32[256,4,128]{2,1,0:T(4,128)S(1)}, u32[]{:S(2)}, u32[]{:S(2)}) async-start(f32[256,4,128]{2,1,0:T(4,128)} %get-tuple-element.48), calls=%async_computation.2 | async-start | bytes 1048576 | tf_op jit(solution)/shard_map/all_to_all | solution.py:435
  128.8 5.0 %collective-permute-start.15 = (f32[8,128]{1,0:T(8,128)S(1)}, f32[8,128]{1,0:T(8,128)S(1)}, u32[]{:S(2)}, u32[]{:S(2)}) collective-permute-start(f32[8,128]{1,0:T(8,128)S(1)} %get-tuple-element.66), channel_id=1, source_target_pairs={{17,0},{18,1},{19,2},{20,3},{21,4},{22,5},{23,6},{24,7},{25,8},{26... | collective-permute-start | bytes 12296 | tf_op jit(solution)/shard_map/ppermute | solution.py:338
  133.9 2.4 %collective-permute-start.11 = (f32[32,128]{1,0:T(8,128)S(1)}, f32[32,128]{1,0:T(8,128)S(1)}, u32[]{:S(2)}, u32[]{:S(2)}) collective-permute-start(f32[32,128]{1,0:T(8,128)S(1)} %get-tuple-element.53), channel_id=1, source_target_pairs={{1,0},{2,1},{3,2},{4,3},{5,4},{6,5},{7,6},{8,7},{9,8},{10,9},{11,1... | collective-permute-start | bytes 49160 | tf_op jit(solution)/shard_map/ppermute | solution.py:338
  136.3 3.4 %collective-permute-start.14 = (f32[8,128]{1,0:T(8,128)S(1)}, f32[8,128]{1,0:T(8,128)S(1)}, u32[]{:S(2)}, u32[]{:S(2)}) collective-permute-start(f32[8,128]{1,0:T(8,128)S(1)} %get-tuple-element.67), channel_id=1, source_target_pairs={{1,16},{2,17},{3,18},{4,19},{5,20},{6,21},{7,22},{8,23},{9,24},{10... | collective-permute-start | bytes 12296 | tf_op jit(solution)/shard_map/ppermute | solution.py:338
  139.7 2.4 %collective-permute-start.8 = (f32[24,128]{1,0:T(8,128)S(1)}, f32[24,128]{1,0:T(8,128)S(1)}, u32[]{:S(2)}, u32[]{:S(2)}) collective-permute-start(f32[24,128]{1,0:T(8,128)S(1)} %get-tuple-element.50), channel_id=1, source_target_pairs={{0,16},{1,17},{2,18},{3,19},{4,20},{5,21},{6,22},{7,23},{8,24},{9,... | collective-permute-start | bytes 36872 | tf_op jit(solution)/shard_map/ppermute | solution.py:338
  144.0 3.2 %collective-permute-start.10 = (f32[32,128]{1,0:T(8,128)S(1)}, f32[32,128]{1,0:T(8,128)S(1)}, u32[]{:S(2)}, u32[]{:S(2)}) collective-permute-start(f32[32,128]{1,0:T(8,128)S(1)} %get-tuple-element.52), channel_id=1, source_target_pairs={{0,1},{1,2},{2,3},{3,4},{4,5},{5,6},{6,7},{7,8},{8,9},{9,10},{10,1... | collective-permute-start | bytes 49160 | tf_op jit(solution)/shard_map/ppermute | solution.py:338
  147.2 2.4 %collective-permute-start.13 = (f32[8,128]{1,0:T(8,128)S(1)}, f32[8,128]{1,0:T(8,128)S(1)}, u32[]{:S(2)}, u32[]{:S(2)}) collective-permute-start(f32[8,128]{1,0:T(8,128)S(1)} %get-tuple-element.68), channel_id=1, source_target_pairs={{16,1},{17,2},{18,3},{19,4},{20,5},{21,6},{22,7},{23,8},{24,9},{25... | collective-permute-start | bytes 12296 | tf_op jit(solution)/shard_map/ppermute | solution.py:338
  149.6 5.5 %collective-permute-done.13.refs_5_ = f32[8,128]{1,0:T(8,128)S(1)} collective-permute-done((f32[8,128]{1,0:T(8,128)S(1)}, f32[8,128]{1,0:T(8,128)S(1)}, u32[]{:S(2)}, u32[]{:S(2)}) %collective-permute-start.13) | collective-permute-done | bytes 4128 | tf_op jit(solution)/shard_map/ppermute | solution.py:338
  157.1 5.1 %collective-permute-done.12.refs_4_ = f32[8,128]{1,0:T(8,128)S(1)} collective-permute-done((f32[8,128]{1,0:T(8,128)S(1)}, f32[8,128]{1,0:T(8,128)S(1)}, u32[]{:S(2)}, u32[]{:S(2)}) %collective-permute-start.12) | collective-permute-done | bytes 4128 | tf_op jit(solution)/shard_map/ppermute | solution.py:338
  166.5 41.9 %contact.3 = (f32[256,4,128]{2,1,0:T(4,128)S(1)}, f32[32,8,128]{2,1,0:T(8,128)S(1)}) custom-call(s32[256]{0:T(256)S(1)} %fusion.refs_0_, f32[256,8,128]{2,1,0:T(8,128)S(1)} %all-to-all-done.refs_1_, f32[256,4,128]{2,1,0:T(4,128)S(1)} %all-to-all-done.2.refs_2_, bf16[32,128,48]{2,1,0:T(8,128)(2,1)S(1)} %get-tuple-element.57.refs_3_, ...), custom_call_target="tpu_custom_call" | custom-call | tf_op jit(solution)/shard_map/contact/pallas_call | solution.py:437
  208.4 19.4 %all_to_all.21.refs_1_ = f32[256,4,128]{2,1,0:T(4,128)S(1)} all-to-all(f32[256,4,128]{2,1,0:T(4,128)S(1)} %get-tuple-element.59), channel_id=1, replica_groups=mesh['gx'=8,'gy'=16] {'gx','gy'}, dimensions={0} | all-to-all | bytes 1048576 | tf_op jit(solution)/shard_map/all_to_all | solution.py:445
  (59 shorter events, 22.9 us)
Async XLA Ops:
  6.4 10.9 %copy-start.1 = (f32[3,32,5,128]{3,1,2,0:T(8,128)S(1)}, f32[3,32,5,128]{3,1,2,0:T(8,128)}, u32[]{:S(2)}) copy-start(f32[3,32,5,128]{3,1,2,0:T(8,128)} %param.5) | copy-start | bytes 737284
  6.5 47.7 %all-to-all-start = ((f32[256,8,128]{2,1,0:T(8,128)}), f32[256,8,128]{2,1,0:T(8,128)S(1)}, u32[]{:S(2)}, u32[]{:S(2)}) async-start(f32[256,8,128]{2,1,0:T(8,128)} %get-tuple-element.35), calls=%async_computation | async-start | bytes 2097152 | tf_op jit(solution)/shard_map/all_to_all | solution.py:385
  18.1 15.1 %collective-permute-start.7 = (f32[8,128]{1,0:T(8,128)S(1)}, f32[8,128]{1,0:T(8,128)S(1)}, u32[]{:S(2)}, u32[]{:S(2)}) collective-permute-start(f32[8,128]{1,0:T(8,128)S(1)} %get-tuple-element.70), channel_id=1, source_target_pairs={{17,0},{18,1},{19,2},{20,3},{21,4},{22,5},{23,6},{24,7},{25,8},{26... | collective-permute-start | bytes 12296 | tf_op jit(solution)/shard_map/ppermute | solution.py:338
  23.1 28.3 %collective-permute-start.3 = (f32[32,128]{1,0:T(8,128)S(1)}, f32[32,128]{1,0:T(8,128)S(1)}, u32[]{:S(2)}, u32[]{:S(2)}) collective-permute-start(f32[32,128]{1,0:T(8,128)S(1)} %get-tuple-element.40), channel_id=1, source_target_pairs={{1,0},{2,1},{3,2},{4,3},{5,4},{6,5},{7,6},{8,7},{9,8},{10,9},{11,1... | collective-permute-start | bytes 49160 | tf_op jit(solution)/shard_map/ppermute | solution.py:338
  25.5 10.9 %collective-permute-start.6 = (f32[8,128]{1,0:T(8,128)S(1)}, f32[8,128]{1,0:T(8,128)S(1)}, u32[]{:S(2)}, u32[]{:S(2)}) collective-permute-start(f32[8,128]{1,0:T(8,128)S(1)} %get-tuple-element.71), channel_id=1, source_target_pairs={{1,16},{2,17},{3,18},{4,19},{5,20},{6,21},{7,22},{8,23},{9,24},{10... | collective-permute-start | bytes 12296 | tf_op jit(solution)/shard_map/ppermute | solution.py:338
  28.9 22.5 %collective-permute-start = (f32[24,128]{1,0:T(8,128)S(1)}, f32[24,128]{1,0:T(8,128)S(1)}, u32[]{:S(2)}, u32[]{:S(2)}) collective-permute-start(f32[24,128]{1,0:T(8,128)S(1)} %get-tuple-element.37), channel_id=1, source_target_pairs={{0,16},{1,17},{2,18},{3,19},{4,20},{5,21},{6,22},{7,23},{8,24},{9,... | collective-permute-start | bytes 36872 | tf_op jit(solution)/shard_map/ppermute | solution.py:338
  31.3 20.1 %collective-permute-start.1 = (f32[24,128]{1,0:T(8,128)S(1)}, f32[24,128]{1,0:T(8,128)S(1)}, u32[]{:S(2)}, u32[]{:S(2)}) collective-permute-start(f32[24,128]{1,0:T(8,128)S(1)} %get-tuple-element.38), channel_id=1, source_target_pairs={{16,0},{17,1},{18,2},{19,3},{20,4},{21,5},{22,6},{23,7},{24,8},{25... | collective-permute-start | bytes 36872 | tf_op jit(solution)/shard_map/ppermute | solution.py:338
  33.2 18.1 %collective-permute-start.2 = (f32[32,128]{1,0:T(8,128)S(1)}, f32[32,128]{1,0:T(8,128)S(1)}, u32[]{:S(2)}, u32[]{:S(2)}) collective-permute-start(f32[32,128]{1,0:T(8,128)S(1)} %get-tuple-element.39), channel_id=1, source_target_pairs={{0,1},{1,2},{2,3},{3,4},{4,5},{5,6},{6,7},{7,8},{8,9},{9,10},{10,1... | collective-permute-start | bytes 49160 | tf_op jit(solution)/shard_map/ppermute | solution.py:338
  36.4 7.9 %collective-permute-start.5 = (f32[8,128]{1,0:T(8,128)S(1)}, f32[8,128]{1,0:T(8,128)S(1)}, u32[]{:S(2)}, u32[]{:S(2)}) collective-permute-start(f32[8,128]{1,0:T(8,128)S(1)} %get-tuple-element.72), channel_id=1, source_target_pairs={{16,1},{17,2},{18,3},{19,4},{20,5},{21,6},{22,7},{23,8},{24,9},{25... | collective-permute-start | bytes 12296 | tf_op jit(solution)/shard_map/ppermute | solution.py:338
  44.3 7.0 %collective-permute-start.4 = (f32[8,128]{1,0:T(8,128)S(1)}, f32[8,128]{1,0:T(8,128)S(1)}, u32[]{:S(2)}, u32[]{:S(2)}) collective-permute-start(f32[8,128]{1,0:T(8,128)S(1)} %get-tuple-element.73), channel_id=1, source_target_pairs={{0,17},{1,18},{2,19},{3,20},{4,21},{5,22},{6,23},{7,24},{8,25},{9,... | collective-permute-start | bytes 12296 | tf_op jit(solution)/shard_map/ppermute | solution.py:338
  100.5 19.4 %copy-start.3 = (f32[3,32,5,128]{3,1,2,0:T(8,128)S(1)}, f32[3,32,5,128]{3,1,2,0:T(8,128)}, u32[]{:S(2)}) copy-start(f32[3,32,5,128]{3,1,2,0:T(8,128)} %param.6) | copy-start | bytes 737284
  100.5 19.4 %copy-start.4 = (f32[32,5,128]{2,0,1:T(8,128)S(1)}, f32[32,5,128]{2,0,1:T(8,128)}, u32[]{:S(2)}) copy-start(f32[32,5,128]{2,0,1:T(8,128)} %param.8) | copy-start | bytes 245764
  122.7 42.8 %all-to-all-start.2 = ((f32[256,4,128]{2,1,0:T(4,128)}), f32[256,4,128]{2,1,0:T(4,128)S(1)}, u32[]{:S(2)}, u32[]{:S(2)}) async-start(f32[256,4,128]{2,1,0:T(4,128)} %get-tuple-element.48), calls=%async_computation.2 | async-start | bytes 1048576 | tf_op jit(solution)/shard_map/all_to_all | solution.py:435
  128.6 33.6 %copy-start.6 = (f32[4,2,40,128]{3,2,1,0:T(8,128)S(1)}, f32[4,2,40,128]{3,2,1,0:T(8,128)}, u32[]{:S(2)}) copy-start(f32[4,2,40,128]{3,2,1,0:T(8,128)} %copy-done.5) | copy-start | bytes 491524
  128.6 33.6 %copy-start.10 = (f32[32,8,128]{2,1,0:T(8,128)S(1)}, f32[32,8,128]{2,1,0:T(8,128)}, u32[]{:S(2)}) copy-start(f32[32,8,128]{2,1,0:T(8,128)} %copy-done.9) | copy-start | bytes 393220
  128.8 15.2 %collective-permute-start.15 = (f32[8,128]{1,0:T(8,128)S(1)}, f32[8,128]{1,0:T(8,128)S(1)}, u32[]{:S(2)}, u32[]{:S(2)}) collective-permute-start(f32[8,128]{1,0:T(8,128)S(1)} %get-tuple-element.66), channel_id=1, source_target_pairs={{17,0},{18,1},{19,2},{20,3},{21,4},{22,5},{23,6},{24,7},{25,8},{26... | collective-permute-start | bytes 12296 | tf_op jit(solution)/shard_map/ppermute | solution.py:338
  133.9 28.3 %collective-permute-start.11 = (f32[32,128]{1,0:T(8,128)S(1)}, f32[32,128]{1,0:T(8,128)S(1)}, u32[]{:S(2)}, u32[]{:S(2)}) collective-permute-start(f32[32,128]{1,0:T(8,128)S(1)} %get-tuple-element.53), channel_id=1, source_target_pairs={{1,0},{2,1},{3,2},{4,3},{5,4},{6,5},{7,6},{8,7},{9,8},{10,9},{11,1... | collective-permute-start | bytes 49160 | tf_op jit(solution)/shard_map/ppermute | solution.py:338
  136.3 10.9 %collective-permute-start.14 = (f32[8,128]{1,0:T(8,128)S(1)}, f32[8,128]{1,0:T(8,128)S(1)}, u32[]{:S(2)}, u32[]{:S(2)}) collective-permute-start(f32[8,128]{1,0:T(8,128)S(1)} %get-tuple-element.67), channel_id=1, source_target_pairs={{1,16},{2,17},{3,18},{4,19},{5,20},{6,21},{7,22},{8,23},{9,24},{10... | collective-permute-start | bytes 12296 | tf_op jit(solution)/shard_map/ppermute | solution.py:338
  139.7 22.5 %collective-permute-start.8 = (f32[24,128]{1,0:T(8,128)S(1)}, f32[24,128]{1,0:T(8,128)S(1)}, u32[]{:S(2)}, u32[]{:S(2)}) collective-permute-start(f32[24,128]{1,0:T(8,128)S(1)} %get-tuple-element.50), channel_id=1, source_target_pairs={{0,16},{1,17},{2,18},{3,19},{4,20},{5,21},{6,22},{7,23},{8,24},{9,... | collective-permute-start | bytes 36872 | tf_op jit(solution)/shard_map/ppermute | solution.py:338
  142.1 20.1 %collective-permute-start.9 = (f32[24,128]{1,0:T(8,128)S(1)}, f32[24,128]{1,0:T(8,128)S(1)}, u32[]{:S(2)}, u32[]{:S(2)}) collective-permute-start(f32[24,128]{1,0:T(8,128)S(1)} %get-tuple-element.51), channel_id=1, source_target_pairs={{16,0},{17,1},{18,2},{19,3},{20,4},{21,5},{22,6},{23,7},{24,8},{25... | collective-permute-start | bytes 36872 | tf_op jit(solution)/shard_map/ppermute | solution.py:338
  144.0 18.1 %collective-permute-start.10 = (f32[32,128]{1,0:T(8,128)S(1)}, f32[32,128]{1,0:T(8,128)S(1)}, u32[]{:S(2)}, u32[]{:S(2)}) collective-permute-start(f32[32,128]{1,0:T(8,128)S(1)} %get-tuple-element.52), channel_id=1, source_target_pairs={{0,1},{1,2},{2,3},{3,4},{4,5},{5,6},{6,7},{7,8},{8,9},{9,10},{10,1... | collective-permute-start | bytes 49160 | tf_op jit(solution)/shard_map/ppermute | solution.py:338
  147.2 7.9 %collective-permute-start.13 = (f32[8,128]{1,0:T(8,128)S(1)}, f32[8,128]{1,0:T(8,128)S(1)}, u32[]{:S(2)}, u32[]{:S(2)}) collective-permute-start(f32[8,128]{1,0:T(8,128)S(1)} %get-tuple-element.68), channel_id=1, source_target_pairs={{16,1},{17,2},{18,3},{19,4},{20,5},{21,6},{22,7},{23,8},{24,9},{25... | collective-permute-start | bytes 12296 | tf_op jit(solution)/shard_map/ppermute | solution.py:338
  155.1 7.0 %collective-permute-start.12 = (f32[8,128]{1,0:T(8,128)S(1)}, f32[8,128]{1,0:T(8,128)S(1)}, u32[]{:S(2)}, u32[]{:S(2)}) collective-permute-start(f32[8,128]{1,0:T(8,128)S(1)} %get-tuple-element.69), channel_id=1, source_target_pairs={{0,17},{1,18},{2,19},{3,20},{4,21},{5,22},{6,23},{7,24},{8,25},{9,... | collective-permute-start | bytes 12296 | tf_op jit(solution)/shard_map/ppermute | solution.py:338
  208.4 19.4 %copy-start.12 = (f32[32,8,128]{2,1,0:T(8,128)S(1)}, f32[32,8,128]{2,1,0:T(8,128)}, u32[]{:S(2)}) copy-start(f32[32,8,128]{2,1,0:T(8,128)} %copy-done.11) | copy-start | bytes 393220
  (9 other events, 17.0 us)
where the time goes:
time: 232 us; the launch traced here: 230 us
  Pallas kernels  95.8 us (41%)
  starting transfers between devices  61.7 us (27%)
  blocking collectives  38.8 us (17%)
  waiting for transfers between devices  21.3 us (9%)
  local copies, waits for them, and re-layouts  6.15 us (3%)
  other arithmetic  4.7 us (2%)
    pallas_call x2, Pallas kernels, local(): pl.pallas_call(lambda *refs, moved=moved: contact_kernel(moved, *refs), i...  83.6 us
    ppermute x16, starting transfers between devices, shifted(): return lax.ppermute(value, AXES, pairs)  45.1 us
    all_to_all x2, blocking collectives, local(): returned = lax.all_to_all(action, AXES, 0, 0, tiled=True)  38.8 us
    ppermute x16, waiting for transfers between devices, shifted(): return lax.ppermute(value, AXES, pairs)  21.3 us
    all_to_all x1, starting transfers between devices, local(): first_recv = lax.all_to_all(send, AXES, 0, 0, tiled=True)  10.8 us
    unnamed x30, local copies, waits for them, and re-layouts  6.14 us
    all_to_all x1, starting transfers between devices, local(): extra = (lax.all_to_all(send, AXES, 0, 0, tiled=True),)  5.87 us
  transfers between devices with their start and end apart: 18, of which 4 were waited for; matrix products, arithmetic and copies ran while one was open for 0% of the time, Pallas kernels for 2%

commit v1 on v0

--- a/solution.py
+++ b/solution.py
@@ -13,7 +13,8 @@
 DEPTH = 5
 FACES = 8
 ENTRIES = ROWS * FACES
-UNROLL = 4
+UNROLL = 64
+LAG = 7
 
 time_step = 0.2
 stiff_coef = 4.0 / (8.0 * NODES)
@@ -81,16 +82,26 @@
     return total + pltpu.roll(total, 4, 0)
 
 
-def request_kernel(facing_ref, disp_ref, vel_ref, send_ref, slot_ref, surf_ref, count_ref):
+def request_kernel(facing_hbm, disp_hbm, vel_hbm, send_ref, slot_ref, surf_ref, facing_ref, top_ref, count_ref, sems):
+    copies = [
+        pltpu.make_async_copy(disp_hbm.at[:, DEPTH - 1], top_ref.at[0], sems.at[0]),
+        pltpu.make_async_copy(vel_hbm.at[:, DEPTH - 1], top_ref.at[1], sems.at[1]),
+        pltpu.make_async_copy(facing_hbm, facing_ref, sems.at[2]),
+    ]
+    for copy in copies:
+        copy.start()
+
     def clear(i, carry):
         count_ref[i] = 0
         return carry
 
     lax.fori_loop(0, NODES, clear, 0, unroll=16)
+    for copy in copies:
+        copy.wait()
     zero = jnp.zeros((ROWS, NODES), f32)
     for c in range(3):
-        surf_ref[:, c, :] = disp_ref[c]
-        surf_ref[:, 3 + c, :] = vel_ref[c]
+        surf_ref[:, c, :] = top_ref[0, c]
+        surf_ref[:, 3 + c, :] = top_ref[1, c]
         if c < 2:
             surf_ref[:, 6 + c, :] = zero
     row6 = (sublanes((8, NODES)) == 6).astype(f32)
@@ -115,7 +126,29 @@
     return [value[c, z, x : x + 1, :] for c in range(value.shape[0]) for z in range(DEPTH)]
 
 
-def edge_kernel(with_stiff, disp_ref, stiff_ref, last_ref, low_row, high_row, low_col, high_col, masked_ref):
+def table_kernel(surf_ref, near_ref, pot_ref, exact_ref):
+    consts = tile_constants()
+    unit = (lanes((NODES, NODES)) == sublanes((NODES, NODES))).astype(bf16)
+
+    def table(b, carry):
+        tile = surf_ref[b]
+        scaled, half, potential = tile_parts(tile, pltpu.roll(tile, 5, 0), consts)
+        near = near_factor(scaled, half, consts)
+        turned = lax.dot_general(unit, near, (((1,), (1,)), ((), ())), preferred_element_type=f32)
+        near_ref[b] = turned.astype(bf16)
+        pot_ref[b] = packed_potential(potential)
+        exact_ref[b] = potential
+        return carry
+
+    lax.fori_loop(0, ROWS, table, 0, unroll=4)
+
+
+def edge_kernel(with_stiff, *refs):
+    if with_stiff:
+        last_ref, disp_ref, surf_ref, stiff_ref, *refs = refs
+        low_row, high_row, low_col, high_col, near_ref, pot_ref, exact_ref, masked_ref = refs
+    else:
+        disp_ref, surf_ref, low_row, high_row, low_col, high_col, near_ref, pot_ref, exact_ref = refs
     shape = (ROWS, NODES)
     lane = lanes(shape)
     if with_stiff:
@@ -140,6 +173,7 @@
             high = jnp.where(lane == at, pltpu.roll(value, at + 1, 1), high)
     low_col[...] = low
     high_col[...] = high
+    table_kernel(surf_ref, near_ref, pot_ref, exact_ref)
 
 
 def extended(center, above, below):
@@ -148,16 +182,16 @@
     return jnp.concatenate([center, tail], axis=0)
 
 
-def force_kernel(with_stiff, disp_ref, stiff_ref, row_lo, row_hi, col_lo, col_hi, c_ll, c_hl, c_lh, c_hh, *rest):
+def force_kernel(with_stiff, disp_ref, *refs):
     if with_stiff:
-        surf_ref, force_ref, wide_ref, node_ref, near_ref, pot_ref, exact_ref = rest
+        stiff_ref, row_lo, row_hi, col_lo, col_hi, force_ref, wide_ref, node_ref = refs
     else:
-        wide_in, node_in, surf_ref, force_ref, near_ref, pot_ref, exact_ref = rest
+        wide_in, node_in, row_lo, row_hi, col_lo, col_hi, force_ref = refs
     wide = (ROWS + 8, NODES)
     lane = lanes(wide)
     last = lane == NODES - 1
-    left = extended(col_lo[...], c_ll[7:8, :], c_hl[0:1, :])
-    right = extended(col_hi[...], c_lh[7:8, :], c_hh[0:1, :])
+    left = extended(col_lo[...], row_lo[24:25, :], row_hi[24:25, :])
+    right = extended(col_hi[...], row_lo[25:26, :], row_hi[25:26, :])
 
     def own(c, z):
         value = disp_ref[c, z] if c < 3 else stiff_ref[z]
@@ -213,63 +247,90 @@
             total = out
             force_ref[c, z] = pull - disp_ref[c, z] * node[z]
 
-    consts = tile_constants()
-    unit = (lanes((NODES, NODES)) == sublanes((NODES, NODES))).astype(bf16)
-
-    def table(b, carry):
-        tile = surf_ref[b]
-        scaled, half, potential = tile_parts(tile, pltpu.roll(tile, 5, 0), consts)
-        near = near_factor(scaled, half, consts)
-        turned = lax.dot_general(unit, near, (((1,), (1,)), ((), ())), preferred_element_type=f32)
-        near_ref[b] = turned.astype(bf16)
-        pot_ref[b] = packed_potential(potential)
-        exact_ref[b] = potential
-        return carry
-
-    lax.fori_loop(0, ROWS, table, 0, unroll=4)
-
-
-def contact_kernel(moved, row_ref, *rest):
+
+def entry_rows(recv_ref, turn_ref, row_ref, sem):
+    shape = (NODES, NODES)
+    diagonal = lanes(shape) == sublanes(shape)
+    for half in range(ENTRIES // NODES):
+        held = recv_ref[half * NODES : (half + 1) * NODES, 6, :]
+        picked = jnp.sum(jnp.where(diagonal, held, 0.0), axis=0, keepdims=True)
+        turn_ref[half : half + 1, :] = picked.astype(jnp.int32)
+    copy = pltpu.make_async_copy(turn_ref, row_ref, sem)
+    copy.start()
+    copy.wait()
+
+
+def contact_kernel(moved, *refs):
     if moved:
-        recv_ref, vel_ref, near_ref, pot_ref, out_ref, loc_ref = rest
+        row_in, recv_ref, vel_ref, near_ref, pot_ref, *refs = refs
     else:
-        recv_ref, near_ref, pot_ref, out_ref, loc_ref = rest
+        recv_ref, near_ref, pot_ref, *refs = refs
+    low_row, high_row, col_lo, col_hi, *refs = refs
+    if moved:
+        out_ref, loc_ref, low_out, high_out = refs
+        row_ref = row_in
+    else:
+        out_ref, loc_ref, low_out, high_out, row_ref, turn_ref, sem = refs
+        entry_rows(recv_ref, turn_ref, row_ref, sem)
+    for side, edge, at in ((low_out, low_row, 0), (high_out, high_row, ROWS - 1)):
+        side[:24] = edge[...]
+        side[24:25] = col_lo[at : at + 1, :]
+        side[25:26] = col_hi[at : at + 1, :]
+        side[26:] = jnp.zeros((ROWS - 26, NODES), f32)
     loc_ref[...] = jnp.zeros((ROWS, 8, NODES), f32)
     consts = tile_constants()
 
     def visit(step, carry):
-        for j in range(UNROLL):
-            e = step * UNROLL + j
-            tile = recv_ref[e]
+        entries = [step * UNROLL + j for j in range(UNROLL)]
+        first = step * UNROLL
+        row = [row_ref[first // NODES, first % NODES + j] for j in range(UNROLL)]
+        held = {}
+
+        def weigh(j):
+            tile = recv_ref[entries[j]]
             if moved:
-                vel = jnp.concatenate([vel_ref[e], jnp.zeros((4, NODES), f32)], axis=0)
+                vel = jnp.concatenate([vel_ref[entries[j]], jnp.zeros((4, NODES), f32)], axis=0)
                 disp = tile + time_step * vel
             else:
                 vel = pltpu.roll(tile, 5, 0)
                 disp = tile
             scaled, half, potential = tile_parts(disp, vel, consts)
             far = far_factor(scaled, half, consts)
-            far_pot = packed_potential(potential)
-            r = row_ref[e]
-            weight = jnp.exp2(jnp.dot(near_ref[r], far, preferred_element_type=f32))
+            exponent = jnp.dot(near_ref[row[j]], far, preferred_element_type=f32)
+            held[j] = exponent, packed_potential(potential), potential
+
+        def reduce(j):
+            exponent, far_pot, potential = held[j]
+            weight = jnp.exp2(exponent)
             high = weight.astype(bf16)
             low = (weight - high.astype(f32)).astype(bf16)
-            near_pot = pot_ref[r]
-            pulled = fold(
-                jnp.dot(
-                    jnp.concatenate([near_pot, near_pot], axis=1),
-                    jnp.concatenate([high, low], axis=0),
-                    preferred_element_type=f32,
-                )
+            near_pot = pot_ref[row[j]]
+            pulled = jnp.dot(
+                jnp.concatenate([near_pot, near_pot], axis=1),
+                jnp.concatenate([high, low], axis=0),
+                preferred_element_type=f32,
             )
-            out_ref[e] = (pulled[3:4] * potential - pulled)[:4]
             pushed = lax.dot_general(
                 jnp.concatenate([far_pot, far_pot], axis=1),
                 jnp.concatenate([high, low], axis=1),
                 (((1,), (1,)), ((), ())),
                 preferred_element_type=f32,
             )
-            loc_ref[r] += pushed[:8] + pushed[8:]
+            held[j] = pulled, pushed, potential
+
+        def store(j):
+            pulled, pushed, potential = held.pop(j)
+            pulled = fold(pulled)
+            out_ref[entries[j]] = (pulled[3:4] * potential - pulled)[:4]
+            loc_ref[row[j]] += pushed[:8] + pushed[8:]
+
+        for t in range(UNROLL + LAG + 1):
+            if t < UNROLL:
+                weigh(t)
+            if 0 <= t - LAG < UNROLL:
+                reduce(t - LAG)
+            if 0 <= t - LAG - 1 < UNROLL:
+                store(t - LAG - 1)
         return carry
 
     lax.fori_loop(0, ENTRIES // UNROLL, visit, 0)
@@ -323,6 +384,7 @@
 
 VMEM = pl.BlockSpec(memory_space=pltpu.VMEM)
 SMEM = pl.BlockSpec(memory_space=pltpu.SMEM)
+ANY = pl.BlockSpec(memory_space=pl.ANY)
 
 
 def struct(*shape, dtype=f32):
@@ -336,24 +398,6 @@
             if 0 <= x + dx < count_gx and 0 <= y + dy < count_gy:
                 pairs.append((x * count_gy + y, (x + dx) * count_gy + y + dy))
     return lax.ppermute(value, AXES, pairs)
-
-
-def halo(edges, count_gx, count_gy):
-    low_row, high_row, low_col, high_col = edges
-
-    def go(value, dx, dy):
-        return shifted(value, count_gx, count_gy, dx, dy)
-
-    return (
-        go(high_row, 1, 0),
-        go(low_row, -1, 0),
-        go(high_col, 0, 1),
-        go(low_col, 0, -1),
-        go(high_col[ROWS - 8 :], 1, 1),
-        go(high_col[:8], -1, 1),
-        go(low_col[ROWS - 8 :], 1, -1),
-        go(low_col[:8], -1, -1),
-    )
 
 
 def local(displacement, velocity, stiffness, inverse_mass, facing):
@@ -370,79 +414,102 @@
             (lax.axis_index("gy") == count_gy - 1).astype(jnp.int32),
         ]
     )
-    plane = (3, 1, ROWS, NODES)
-    top = pl.BlockSpec((3, None, ROWS, NODES), lambda i: (0, DEPTH - 1, 0, 0))
     send, slots, surf = pl.pallas_call(
         request_kernel,
-        grid=(1,),
-        in_specs=[SMEM, top, top],
+        in_specs=[ANY] * 3,
         out_specs=[VMEM, SMEM, VMEM],
         out_shape=[struct(ENTRIES, 8, NODES), struct(ENTRIES, dtype=jnp.int32), struct(ROWS, 8, NODES)],
-        scratch_shapes=[pltpu.SMEM((NODES,), jnp.int32)],
+        scratch_shapes=[
+            pltpu.SMEM((FACES, ROWS), jnp.int32),
+            pltpu.VMEM((2, 3, ROWS, NODES), f32),
+            pltpu.SMEM((NODES,), jnp.int32),
+            pltpu.SemaphoreType.DMA((3,)),
+        ],
         compiler_params=PARAMS,
         name="request",
     )(faces, disp, vel)
-    first_recv = lax.all_to_all(send, AXES, 0, 0, tiled=True)
-    wide = node = None
-    edge_shapes = [struct(24, NODES), struct(24, NODES), struct(ROWS, NODES), struct(ROWS, NODES)]
-    table_shapes = [
+    wide = node = rows = first_recv = masked = None
+    edge_shapes = [
+        struct(24, NODES),
+        struct(24, NODES),
+        struct(ROWS, NODES),
+        struct(ROWS, NODES),
         struct(ROWS, NODES, 48, dtype=bf16),
         struct(ROWS, 16, NODES, dtype=bf16),
         struct(ROWS, 8, NODES),
     ]
     force_shape = [struct(3, DEPTH, ROWS, NODES)]
+
+    def go(value, dx, dy):
+        return shifted(value, count_gx, count_gy, dx, dy)
+
     for step in range(STEPS):
-        if step == 0:
-            *edges, masked = pl.pallas_call(
-                lambda d, s, e, *outs: edge_kernel(True, d, s, e, *outs),
-                in_specs=[VMEM, VMEM, SMEM],
-                out_specs=[VMEM] * 5,
+        moved = step > 0
+        recv = lax.all_to_all(send, AXES, 0, 0, tiled=True)
+        if moved:
+            outs = pl.pallas_call(
+                lambda *refs: edge_kernel(False, *refs),
+                in_specs=[VMEM] * 2,
+                out_specs=[VMEM] * 7,
+                out_shape=edge_shapes,
+                compiler_params=PARAMS,
+                name="edges_next",
+            )(disp, surf)
+        else:
+            *outs, masked = pl.pallas_call(
+                lambda *refs: edge_kernel(True, *refs),
+                in_specs=[SMEM] + [VMEM] * 3,
+                out_specs=[VMEM] * 8,
                 out_shape=edge_shapes + [struct(DEPTH, ROWS, NODES)],
                 compiler_params=PARAMS,
                 name="edges_first",
-            )(disp, stiff, ends)
-            around = halo(edges, count_gx, count_gy)
-            force, wide, node, near, pot, exact = pl.pallas_call(
+            )(ends, disp, surf, stiff)
+        low_row, high_row, low_col, high_col, near, pot, exact = outs
+        col_lo = go(high_col, 0, 1)
+        col_hi = go(low_col, 0, -1)
+        shapes = [struct(ENTRIES, 4, NODES), struct(ROWS, 8, NODES), struct(ROWS, NODES), struct(ROWS, NODES)]
+        edges = (low_row, high_row, col_lo, col_hi)
+        if moved:
+            action, reaction, low_out, high_out = pl.pallas_call(
+                lambda *refs: contact_kernel(True, *refs),
+                in_specs=[SMEM] + [VMEM] * 8,
+                out_specs=[VMEM] * 4,
+                out_shape=shapes,
+                compiler_params=PARAMS,
+                name="contact_next",
+            )(rows, first_recv, recv, near, pot, *edges)
+        else:
+            first_recv = recv
+            action, reaction, low_out, high_out, rows = pl.pallas_call(
+                lambda *refs: contact_kernel(False, *refs),
+                in_specs=[VMEM] * 7,
+                out_specs=[VMEM] * 4 + [SMEM],
+                out_shape=shapes + [struct(ENTRIES // NODES, NODES, dtype=jnp.int32)],
+                scratch_shapes=[pltpu.VMEM((ENTRIES // NODES, NODES), jnp.int32), pltpu.SemaphoreType.DMA(())],
+                compiler_params=PARAMS,
+                name="contact_first",
+            )(recv, near, pot, *edges)
+        returned = lax.all_to_all(action, AXES, 0, 0, tiled=True)
+        row_lo = go(high_out, 1, 0)
+        row_hi = go(low_out, -1, 0)
+        if moved:
+            (force,) = pl.pallas_call(
+                lambda *refs: force_kernel(False, *refs),
+                in_specs=[VMEM] * 7,
+                out_specs=[VMEM],
+                out_shape=force_shape,
+                compiler_params=PARAMS,
+                name="force_next",
+            )(disp, wide, node, row_lo, row_hi, col_lo, col_hi)
+        else:
+            force, wide, node = pl.pallas_call(
                 lambda *refs: force_kernel(True, *refs),
-                in_specs=[VMEM] * 11,
-                out_specs=[VMEM] * 6,
-                out_shape=force_shape
-                + [struct(DEPTH - 1, 2, ROWS + 8, NODES), struct(DEPTH, ROWS, NODES)]
-                + table_shapes,
+                in_specs=[VMEM] * 6,
+                out_specs=[VMEM] * 3,
+                out_shape=force_shape + [struct(DEPTH - 1, 2, ROWS + 8, NODES), struct(DEPTH, ROWS, NODES)],
                 compiler_params=PARAMS,
                 name="force_first",
-            )(disp, masked, *around, surf)
-            rows = first_recv[:, 6, 0].astype(jnp.int32)
-            extra = ()
-        else:
-            edges = pl.pallas_call(
-                lambda d, *outs: edge_kernel(False, d, None, None, *outs, None),
-                in_specs=[VMEM],
-                out_specs=[VMEM] * 4,
-                out_shape=edge_shapes,
-                compiler_params=PARAMS,
-                name="edges_next",
-            )(disp)
-            around = halo(edges, count_gx, count_gy)
-            force, near, pot, exact = pl.pallas_call(
-                lambda d, *refs: force_kernel(False, d, None, *refs),
-                in_specs=[VMEM] * 12,
-                out_specs=[VMEM] * 4,
-                out_shape=force_shape + table_shapes,
-                compiler_params=PARAMS,
-                name="force_next",
-            )(disp, *around, wide, node, surf)
-            extra = (lax.all_to_all(send, AXES, 0, 0, tiled=True),)
-        moved = step > 0
-        action, reaction = pl.pallas_call(
-            lambda *refs, moved=moved: contact_kernel(moved, *refs),
-            in_specs=[SMEM] + [VMEM] * (3 + len(extra)),
-            out_specs=[VMEM] * 2,
-            out_shape=[struct(ENTRIES, 4, NODES), struct(ROWS, 8, NODES)],
-            compiler_params=PARAMS,
-            name="contact",
-        )(rows, first_recv, *extra, near, pot)
-        returned = lax.all_to_all(action, AXES, 0, 0, tiled=True)
+            )(disp, masked, row_lo, row_hi, col_lo, col_hi)
         final = step == STEPS - 1
         outs = [struct(3, DEPTH, ROWS, NODES), struct(3, DEPTH, ROWS, NODES)]
         if not final:

time: 232 us -> 126 us (0.54)
  Pallas kernels: 95.8 us -> 31.7 us
  blocking collectives: 38.8 us -> 0 us
  other arithmetic: 4.7 us -> 0.08 us
  local copies, waits for them, and re-layouts: 6.15 us -> 8.79 us
    pallas_call x6, Pallas kernels: 89.8 us -> 27.2 us  [the longest x1 10.3 us: local(): pl.pallas_call(lambda *refs: contact_kernel(False, *refs), in_specs=[VMEM...]
    all_to_all x2 -> x0, blocking collectives: 38.8 us -> none  [local(): returned = lax.all_to_all(action, AXES, 0, 0, tiled=True)]
    ppermute x16 -> x8, starting transfers between devices: 45.1 us -> 25.9 us  [shifted(): return lax.ppermute(value, AXES, pairs)]
    all_to_all x2 -> x4, starting transfers between devices: 16.7 us -> 34.9 us  [the longest x2 17.9 us: local(): recv = lax.all_to_all(send, AXES, 0, 0, tiled=True)]
    ppermute x16 -> x8, waiting for transfers between devices: 21.3 us -> 12.8 us  [shifted(): return lax.ppermute(value, AXES, pairs)]
    all_to_all x2 -> x4, waiting for transfers between devices: 0.01 us -> 8.3 us  [the longest x2 4.33 us: local(): returned = lax.all_to_all(action, AXES, 0, 0, tiled=True)]
    convert_element_type x1 -> x0, other arithmetic: 4.62 us -> none  [local(): rows = first_recv[:, 6, 0].astype(jnp.int32)]
    unnamed x30 -> x40, local copies, waits for them, and re-layouts: 6.14 us -> 8.79 us
  transfers between devices with their start and end apart: 18 -> 12, of which waited for: 4 -> 8; matrix products, arithmetic and copies ran while one was open for 0% -> 0% of each run, Pallas kernels for 2% -> 4%
where the time goes in v1:
time: 126 us; the launch traced here: 123 us
  starting transfers between devices  60.8 us (48%)
  Pallas kernels  31.7 us (25%)
  waiting for transfers between devices  21.1 us (17%)
  local copies, waits for them, and re-layouts  8.79 us (7%)
    ppermute x8, starting transfers between devices, shifted(): return lax.ppermute(value, AXES, pairs)  25.9 us
    all_to_all x2, starting transfers between devices, local(): recv = lax.all_to_all(send, AXES, 0, 0, tiled=True)  17.9 us
    all_to_all x2, starting transfers between devices, local(): returned = lax.all_to_all(action, AXES, 0, 0, tiled=True)  17 us
    ppermute x8, waiting for transfers between devices, shifted(): return lax.ppermute(value, AXES, pairs)  12.8 us
    pallas_call x1, Pallas kernels, local(): pl.pallas_call(lambda *refs: contact_kernel(False, *refs), in_specs=[VMEM...  10.3 us
    pallas_call x1, Pallas kernels, local(): pl.pallas_call(lambda *refs: contact_kernel(True, *refs), in_specs=[SMEM]...  9.38 us
    unnamed x40, local copies, waits for them, and re-layouts  8.79 us
    all_to_all x2, waiting for transfers between devices, local(): returned = lax.all_to_all(action, AXES, 0, 0, tiled=True)  4.33 us
  transfers between devices with their start and end apart: 12, of which 8 were waited for; matrix products, arithmetic and copies ran while one was open for 0% of the time, Pallas kernels for 4%

profile of v1, /device:TPU:7, one launch (start us, length us, event | category | flops | bytes accessed | tf_op | source)
XLA Modules:
  0.0 123.4 jit_solution(10645330846735243917)
XLA Ops:
  3.2 3.2 %request.1 = (f32[256,8,128]{2,1,0:T(8,128)}, s32[256]{0:T(256)S(1)}, f32[32,8,128]{2,1,0:T(8,128)S(1)}) custom-call(s32[8,32]{1,0:T(8,128)S(1)} %bitcast.20, f32[3,5,32,128]{3,2,1,0:T(8,128)S(1)} %bitcast.11, f32[3,5,32,128]{3,2,1,0:T(8,128)S(1)} %bitcast.15), custom_call_target="tpu_custom_call" | custom-call | tf_op jit(solution)/shard_map/request/pallas_call | solution.py:417
  6.4 10.8 %all-to-all-start = ((f32[256,8,128]{2,1,0:T(8,128)}), f32[256,8,128]{2,1,0:T(8,128)S(1)}, u32[]{:S(2)}, u32[]{:S(2)}) async-start(f32[256,8,128]{2,1,0:T(8,128)} %get-tuple-element.39), calls=%async_computation | async-start | bytes 2097152 | tf_op jit(solution)/shard_map/all_to_all | solution.py:448
  17.3 2.2 %edges_first.1 = (f32[24,128]{1,0:T(8,128)S(1)}, f32[24,128]{1,0:T(8,128)S(1)}, f32[32,128]{1,0:T(8,128)S(1)}, f32[32,128]{1,0:T(8,128)S(1)}, bf16[32,128,48]{2,...) custom-call(s32[2]{0:T(128)S(1)} %add_convert_fusion.refs_0_, ...), custom_call_target="tpu_custom_call" | custom-call | tf_op jit(solution)/shard_map/edges_first/pallas_call | solution.py:459
  19.5 3.1 %collective-permute-start = (f32[32,128]{1,0:T(8,128)S(1)}, f32[32,128]{1,0:T(8,128)S(1)}, u32[]{:S(2)}, u32[]{:S(2)}) collective-permute-start(f32[32,128]{1,0:T(8,128)S(1)} %get-tuple-element.45), channel_id=1, source_target_pairs={{0,1},{1,2},{2,3},{3,4},{4,5},{5,6},{6,7},{7,8},{8,9},{9,10},{10,1... | collective-permute-start | bytes 49160 | tf_op jit(solution)/shard_map/ppermute | solution.py:400
  22.7 4.3 %collective-permute-start.1 = (f32[32,128]{1,0:T(8,128)S(1)}, f32[32,128]{1,0:T(8,128)S(1)}, u32[]{:S(2)}, u32[]{:S(2)}) collective-permute-start(f32[32,128]{1,0:T(8,128)S(1)} %get-tuple-element.46), channel_id=1, source_target_pairs={{1,0},{2,1},{3,2},{4,3},{5,4},{6,5},{7,6},{8,7},{9,8},{10,9},{11,1... | collective-permute-start | bytes 49160 | tf_op jit(solution)/shard_map/ppermute | solution.py:400
  27.0 4.7 %collective-permute-done.refs_5_.refs_4_ = f32[32,128]{1,0:T(8,128)S(1)} collective-permute-done((f32[32,128]{1,0:T(8,128)S(1)}, f32[32,128]{1,0:T(8,128)S(1)}, u32[]{:S(2)}, u32[]{:S(2)}) %collective-permute-start) | collective-permute-done | bytes 16416 | tf_op jit(solution)/shard_map/ppermute | solution.py:400
  31.7 3.2 %all-to-all-done.refs_0_.refs_1_ = f32[256,8,128]{2,1,0:T(8,128)S(1)} async-done(((f32[256,8,128]{2,1,0:T(8,128)}), f32[256,8,128]{2,1,0:T(8,128)S(1)}, u32[]{:S(2)}, u32[]{:S(2)}) %all-to-all-start) | async-done | bytes 1048608 | tf_op jit(solution)/shard_map/all_to_all | solution.py:448
  34.9 10.3 %contact_first.1 = (f32[256,4,128]{2,1,0:T(4,128)}, f32[32,8,128]{2,1,0:T(8,128)S(1)}, f32[32,128]{1,0:T(8,128)S(1)}, f32[32,128]{1,0:T(8,128)S(1)}, s32[2,128]{1,0:T(2,128)S(1)}) custom-call(f32[256,8,128]{2,1,0:T(8,128)S(1)} %all-to-all-done.refs_0_.refs_1_, bf16[32,128,48]{2,1,0:T(8,128)(2,1)S(1)} %get-tuple-element.41.refs_1_, ...), custom_call_target="tpu_custom_call" | custom-call | tf_op jit(solution)/shard_map/contact_first/pallas_call | solution.py:483
  45.7 5.9 %all-to-all-start.1 = ((f32[256,4,128]{2,1,0:T(4,128)}), f32[256,4,128]{2,1,0:T(4,128)S(1)}, u32[]{:S(2)}, u32[]{:S(2)}) async-start(f32[256,4,128]{2,1,0:T(4,128)} %get-tuple-element.48), calls=%async_computation.1 | async-start | bytes 1048576 | tf_op jit(solution)/shard_map/all_to_all | solution.py:492
  51.6 3.7 %collective-permute-start.2 = (f32[32,128]{1,0:T(8,128)S(1)}, f32[32,128]{1,0:T(8,128)S(1)}, u32[]{:S(2)}, u32[]{:S(2)}) collective-permute-start(f32[32,128]{1,0:T(8,128)S(1)} %get-tuple-element.52), channel_id=1, source_target_pairs={{0,16},{1,17},{2,18},{3,19},{4,20},{5,21},{6,22},{7,23},{8,24},{9,... | collective-permute-start | bytes 49160 | tf_op jit(solution)/shard_map/ppermute | solution.py:400
  55.4 1.9 %collective-permute-start.3 = (f32[32,128]{1,0:T(8,128)S(1)}, f32[32,128]{1,0:T(8,128)S(1)}, u32[]{:S(2)}, u32[]{:S(2)}) collective-permute-start(f32[32,128]{1,0:T(8,128)S(1)} %get-tuple-element.53), channel_id=1, source_target_pairs={{16,0},{17,1},{18,2},{19,3},{20,4},{21,5},{22,6},{23,7},{24,8},{25... | collective-permute-start | bytes 49160 | tf_op jit(solution)/shard_map/ppermute | solution.py:400
  57.3 3.6 %collective-permute-done.3.refs_3_ = f32[32,128]{1,0:T(8,128)S(1)} collective-permute-done((f32[32,128]{1,0:T(8,128)S(1)}, f32[32,128]{1,0:T(8,128)S(1)}, u32[]{:S(2)}, u32[]{:S(2)}) %collective-permute-start.3) | collective-permute-done | bytes 16416 | tf_op jit(solution)/shard_map/ppermute | solution.py:400
  62.2 1.7 %all-to-all-done.1.refs_1_ = f32[256,4,128]{2,1,0:T(4,128)S(1)} async-done(((f32[256,4,128]{2,1,0:T(4,128)}), f32[256,4,128]{2,1,0:T(4,128)S(1)}, u32[]{:S(2)}, u32[]{:S(2)}) %all-to-all-start.1) | async-done | bytes 524320 | tf_op jit(solution)/shard_map/all_to_all | solution.py:492
  63.9 2.2 %update.2 = (f32[3,5,32,128]{3,2,1,0:T(8,128)S(1)}, f32[3,5,32,128]{3,2,1,0:T(8,128)S(1)}, f32[256,4,128]{2,1,0:T(4,128)}, f32[32,8,128]{2,1,0:T(8,128)S(1)}) custom-call(s32[256]{0:T(256)S(1)} %get-tuple-element.38.refs_0_, f32[256,4,128]{2,1,0:T(4,128)S(1)} %all-to-all-done.1.refs_1_, f32[32,8,128]{2,1,0:T(8,128)S(1)} %get-tuple-element.49.refs_2_, ...), custom_call_target="tpu_custom_call" | custom-call | tf_op jit(solution)/shard_map/update/pallas_call | solution.py:517
  66.8 7.1 %all-to-all-start.2 = ((f32[256,4,128]{2,1,0:T(4,128)}), f32[256,4,128]{2,1,0:T(4,128)S(1)}, u32[]{:S(2)}, u32[]{:S(2)}) async-start(f32[256,4,128]{2,1,0:T(4,128)} %get-tuple-element.55), calls=%async_computation.2 | async-start | bytes 1048576 | tf_op jit(solution)/shard_map/all_to_all | solution.py:448
  77.1 3.1 %collective-permute-start.4 = (f32[32,128]{1,0:T(8,128)S(1)}, f32[32,128]{1,0:T(8,128)S(1)}, u32[]{:S(2)}, u32[]{:S(2)}) collective-permute-start(f32[32,128]{1,0:T(8,128)S(1)} %get-tuple-element.62), channel_id=1, source_target_pairs={{0,1},{1,2},{2,3},{3,4},{4,5},{5,6},{6,7},{7,8},{8,9},{9,10},{10,1... | collective-permute-start | bytes 49160 | tf_op jit(solution)/shard_map/ppermute | solution.py:400
  80.2 4.3 %collective-permute-start.5 = (f32[32,128]{1,0:T(8,128)S(1)}, f32[32,128]{1,0:T(8,128)S(1)}, u32[]{:S(2)}, u32[]{:S(2)}) collective-permute-start(f32[32,128]{1,0:T(8,128)S(1)} %get-tuple-element.63), channel_id=1, source_target_pairs={{1,0},{2,1},{3,2},{4,3},{5,4},{6,5},{7,6},{8,7},{9,8},{10,9},{11,1... | collective-permute-start | bytes 49160 | tf_op jit(solution)/shard_map/ppermute | solution.py:400
  86.8 9.4 %contact_next.1 = (f32[256,4,128]{2,1,0:T(4,128)S(1)}, f32[32,8,128]{2,1,0:T(8,128)S(1)}, f32[32,128]{1,0:T(8,128)S(1)}, f32[32,128]{1,0:T(8,128)S(1)}) custom-call(s32[2,128]{1,0:T(2,128)S(1)} %copy-done.19, f32[256,8,128]{2,1,0:T(8,128)S(1)} %all-to-all-done.refs_0_.refs_1_, f32[256,4,128]{2,1,0:T(4,128)S(1)} %all-to-all-done.2.refs_2_, ...), custom_call_target="tpu_custom_call" | custom-call | tf_op jit(solution)/shard_map/contact_next/pallas_call | solution.py:473
  97.6 11.1 %all-to-all-start.3 = ((f32[256,4,128]{2,1,0:T(4,128)}), f32[256,4,128]{2,1,0:T(4,128)S(1)}, u32[]{:S(2)}, u32[]{:S(2)}) async-start(f32[256,4,128]{2,1,0:T(4,128)} %copy-done.4), calls=%async_computation.3 | async-start | bytes 1048576 | tf_op jit(solution)/shard_map/all_to_all | solution.py:492
  108.8 3.5 %collective-permute-start.6 = (f32[32,128]{1,0:T(8,128)S(1)}, f32[32,128]{1,0:T(8,128)S(1)}, u32[]{:S(2)}, u32[]{:S(2)}) collective-permute-start(f32[32,128]{1,0:T(8,128)S(1)} %get-tuple-element.69), channel_id=1, source_target_pairs={{0,16},{1,17},{2,18},{3,19},{4,20},{5,21},{6,22},{7,23},{8,24},{9,... | collective-permute-start | bytes 49160 | tf_op jit(solution)/shard_map/ppermute | solution.py:400
  112.3 1.9 %collective-permute-start.7 = (f32[32,128]{1,0:T(8,128)S(1)}, f32[32,128]{1,0:T(8,128)S(1)}, u32[]{:S(2)}, u32[]{:S(2)}) collective-permute-start(f32[32,128]{1,0:T(8,128)S(1)} %get-tuple-element.70), channel_id=1, source_target_pairs={{16,0},{17,1},{18,2},{19,3},{20,4},{21,5},{22,6},{23,7},{24,8},{25... | collective-permute-start | bytes 49160 | tf_op jit(solution)/shard_map/ppermute | solution.py:400
  114.2 3.6 %collective-permute-done.7.refs_4_ = f32[32,128]{1,0:T(8,128)S(1)} collective-permute-done((f32[32,128]{1,0:T(8,128)S(1)}, f32[32,128]{1,0:T(8,128)S(1)}, u32[]{:S(2)}, u32[]{:S(2)}) %collective-permute-start.7) | collective-permute-done | bytes 16416 | tf_op jit(solution)/shard_map/ppermute | solution.py:400
  118.4 2.6 %all-to-all-done.3.refs_1_ = f32[256,4,128]{2,1,0:T(4,128)S(1)} async-done(((f32[256,4,128]{2,1,0:T(4,128)}), f32[256,4,128]{2,1,0:T(4,128)S(1)}, u32[]{:S(2)}, u32[]{:S(2)}) %all-to-all-start.3) | async-done | bytes 524320 | tf_op jit(solution)/shard_map/all_to_all | solution.py:492
  121.7 1.7 %update.3 = (f32[3,5,32,128]{3,2,1,0:T(8,128)}, f32[3,5,32,128]{3,2,1,0:T(8,128)}) custom-call(s32[256]{0:T(256)S(1)} %copy-done.17, f32[256,4,128]{2,1,0:T(4,128)S(1)} %all-to-all-done.3.refs_1_, f32[32,8,128]{2,1,0:T(8,128)S(1)} %copy-done.13, f32[32,8,128]{2,1,0:T(8,128)S(1)} %copy-done.11, f32[3,5,32,128]{3,2,1,0:T(8,128)S(1)} %force_next.1.refs_4_, ...), custom_call_target="tpu_custom_call" | custom-call | tf_op jit(solution)/shard_map/update/pallas_call | solution.py:517
  (50 shorter events, 13.3 us)
Async XLA Ops:
  1.3 0.9 copy-start
  2.3 0.9 copy-start.2
  6.4 57.6 %copy-start.16 = (s32[256]{0:T(256)}, s32[256]{0:T(256)S(1)}, u32[]{:S(2)}) copy-start(s32[256]{0:T(256)S(1)} %get-tuple-element.38.refs_0_) | copy-start | bytes 3076
  6.4 10.9 %copy-start.1 = (f32[3,32,5,128]{3,1,2,0:T(8,128)S(1)}, f32[3,32,5,128]{3,1,2,0:T(8,128)}, u32[]{:S(2)}) copy-start(f32[3,32,5,128]{3,1,2,0:T(8,128)} %param.5) | copy-start | bytes 737284
  6.4 10.9 %copy-start.14 = (f32[32,5,128]{2,0,1:T(8,128)S(1)}, f32[32,5,128]{2,0,1:T(8,128)}, u32[]{:S(2)}) copy-start(f32[32,5,128]{2,0,1:T(8,128)} %param.7) | copy-start | bytes 245764
  6.4 28.5 %all-to-all-start = ((f32[256,8,128]{2,1,0:T(8,128)}), f32[256,8,128]{2,1,0:T(8,128)S(1)}, u32[]{:S(2)}, u32[]{:S(2)}) async-start(f32[256,8,128]{2,1,0:T(8,128)} %get-tuple-element.39), calls=%async_computation | async-start | bytes 2097152 | tf_op jit(solution)/shard_map/all_to_all | solution.py:448
  19.5 12.1 %collective-permute-start = (f32[32,128]{1,0:T(8,128)S(1)}, f32[32,128]{1,0:T(8,128)S(1)}, u32[]{:S(2)}, u32[]{:S(2)}) collective-permute-start(f32[32,128]{1,0:T(8,128)S(1)} %get-tuple-element.45), channel_id=1, source_target_pairs={{0,1},{1,2},{2,3},{3,4},{4,5},{5,6},{6,7},{7,8},{8,9},{9,10},{10,1... | collective-permute-start | bytes 49160 | tf_op jit(solution)/shard_map/ppermute | solution.py:400
  22.7 9.0 %collective-permute-start.1 = (f32[32,128]{1,0:T(8,128)S(1)}, f32[32,128]{1,0:T(8,128)S(1)}, u32[]{:S(2)}, u32[]{:S(2)}) collective-permute-start(f32[32,128]{1,0:T(8,128)S(1)} %get-tuple-element.46), channel_id=1, source_target_pairs={{1,0},{2,1},{3,2},{4,3},{5,4},{6,5},{7,6},{8,7},{9,8},{10,9},{11,1... | collective-permute-start | bytes 49160 | tf_op jit(solution)/shard_map/ppermute | solution.py:400
  45.7 18.2 %all-to-all-start.1 = ((f32[256,4,128]{2,1,0:T(4,128)}), f32[256,4,128]{2,1,0:T(4,128)S(1)}, u32[]{:S(2)}, u32[]{:S(2)}) async-start(f32[256,4,128]{2,1,0:T(4,128)} %get-tuple-element.48), calls=%async_computation.1 | async-start | bytes 1048576 | tf_op jit(solution)/shard_map/all_to_all | solution.py:492
  51.6 12.3 %copy-start.3 = (f32[3,32,5,128]{3,1,2,0:T(8,128)S(1)}, f32[3,32,5,128]{3,1,2,0:T(8,128)}, u32[]{:S(2)}) copy-start(f32[3,32,5,128]{3,1,2,0:T(8,128)} %param.6) | copy-start | bytes 737284
  51.6 5.7 %collective-permute-start.2 = (f32[32,128]{1,0:T(8,128)S(1)}, f32[32,128]{1,0:T(8,128)S(1)}, u32[]{:S(2)}, u32[]{:S(2)}) collective-permute-start(f32[32,128]{1,0:T(8,128)S(1)} %get-tuple-element.52), channel_id=1, source_target_pairs={{0,16},{1,17},{2,18},{3,19},{4,20},{5,21},{6,22},{7,23},{8,24},{9,... | collective-permute-start | bytes 49160 | tf_op jit(solution)/shard_map/ppermute | solution.py:400
  55.4 5.6 %collective-permute-start.3 = (f32[32,128]{1,0:T(8,128)S(1)}, f32[32,128]{1,0:T(8,128)S(1)}, u32[]{:S(2)}, u32[]{:S(2)}) collective-permute-start(f32[32,128]{1,0:T(8,128)S(1)} %get-tuple-element.53), channel_id=1, source_target_pairs={{16,0},{17,1},{18,2},{19,3},{20,4},{21,5},{22,6},{23,7},{24,8},{25... | collective-permute-start | bytes 49160 | tf_op jit(solution)/shard_map/ppermute | solution.py:400
  60.9 3.0 %copy-start.5 = (f32[32,5,128]{2,0,1:T(8,128)S(1)}, f32[32,5,128]{2,0,1:T(8,128)}, u32[]{:S(2)}) copy-start(f32[32,5,128]{2,0,1:T(8,128)} %param.8) | copy-start | bytes 245764
  66.8 19.3 %all-to-all-start.2 = ((f32[256,4,128]{2,1,0:T(4,128)}), f32[256,4,128]{2,1,0:T(4,128)S(1)}, u32[]{:S(2)}, u32[]{:S(2)}) async-start(f32[256,4,128]{2,1,0:T(4,128)} %get-tuple-element.55), calls=%async_computation.2 | async-start | bytes 1048576 | tf_op jit(solution)/shard_map/all_to_all | solution.py:448
  73.9 0.9 copy-start.9
  77.1 7.4 %collective-permute-start.4 = (f32[32,128]{1,0:T(8,128)S(1)}, f32[32,128]{1,0:T(8,128)S(1)}, u32[]{:S(2)}, u32[]{:S(2)}) collective-permute-start(f32[32,128]{1,0:T(8,128)S(1)} %get-tuple-element.62), channel_id=1, source_target_pairs={{0,1},{1,2},{2,3},{3,4},{4,5},{5,6},{6,7},{7,8},{8,9},{9,10},{10,1... | collective-permute-start | bytes 49160 | tf_op jit(solution)/shard_map/ppermute | solution.py:400
  80.2 5.2 %collective-permute-start.5 = (f32[32,128]{1,0:T(8,128)S(1)}, f32[32,128]{1,0:T(8,128)S(1)}, u32[]{:S(2)}, u32[]{:S(2)}) collective-permute-start(f32[32,128]{1,0:T(8,128)S(1)} %get-tuple-element.63), channel_id=1, source_target_pairs={{1,0},{2,1},{3,2},{4,3},{5,4},{6,5},{7,6},{8,7},{9,8},{10,9},{11,1... | collective-permute-start | bytes 49160 | tf_op jit(solution)/shard_map/ppermute | solution.py:400
  96.1 0.8 copy-start.4
  97.6 20.2 %copy-start.7 = (f32[4,2,40,128]{3,2,1,0:T(8,128)S(1)}, f32[4,2,40,128]{3,2,1,0:T(8,128)}, u32[]{:S(2)}) copy-start(f32[4,2,40,128]{3,2,1,0:T(8,128)} %copy-done.6) | copy-start | bytes 491524
  97.6 23.4 %all-to-all-start.3 = ((f32[256,4,128]{2,1,0:T(4,128)}), f32[256,4,128]{2,1,0:T(4,128)S(1)}, u32[]{:S(2)}, u32[]{:S(2)}) async-start(f32[256,4,128]{2,1,0:T(4,128)} %copy-done.4), calls=%async_computation.3 | async-start | bytes 1048576 | tf_op jit(solution)/shard_map/all_to_all | solution.py:492
  108.8 5.4 %collective-permute-start.6 = (f32[32,128]{1,0:T(8,128)S(1)}, f32[32,128]{1,0:T(8,128)S(1)}, u32[]{:S(2)}, u32[]{:S(2)}) collective-permute-start(f32[32,128]{1,0:T(8,128)S(1)} %get-tuple-element.69), channel_id=1, source_target_pairs={{0,16},{1,17},{2,18},{3,19},{4,20},{5,21},{6,22},{7,23},{8,24},{9,... | collective-permute-start | bytes 49160 | tf_op jit(solution)/shard_map/ppermute | solution.py:400
  112.3 5.6 %collective-permute-start.7 = (f32[32,128]{1,0:T(8,128)S(1)}, f32[32,128]{1,0:T(8,128)S(1)}, u32[]{:S(2)}, u32[]{:S(2)}) collective-permute-start(f32[32,128]{1,0:T(8,128)S(1)} %get-tuple-element.70), channel_id=1, source_target_pairs={{16,0},{17,1},{18,2},{19,3},{20,4},{21,5},{22,6},{23,7},{24,8},{25... | collective-permute-start | bytes 49160 | tf_op jit(solution)/shard_map/ppermute | solution.py:400
  117.8 3.2 %copy-start.11 = (f32[32,8,128]{2,1,0:T(8,128)S(1)}, f32[32,8,128]{2,1,0:T(8,128)}, u32[]{:S(2)}) copy-start(f32[32,8,128]{2,1,0:T(8,128)} %copy-done.10) | copy-start | bytes 393220
  117.8 3.2 %copy-start.13 = (f32[32,8,128]{2,1,0:T(8,128)S(1)}, f32[32,8,128]{2,1,0:T(8,128)}, u32[]{:S(2)}) copy-start(f32[32,8,128]{2,1,0:T(8,128)} %copy-done.12) | copy-start | bytes 393220
  (8 other events, 5.2 us)

commit v2 on v1

v2 whole, which is shorter than its diff:
```python
import jax
import jax.numpy as jnp
import numpy as np
from jax import lax
from jax.experimental import pallas as pl
from jax.experimental.pallas import tpu as pltpu
from jax.sharding import PartitionSpec as P

AXES = ("gx", "gy")
NODES = 128
ROWS = 32
DEPTH = 5
FACES = 8
ENTRIES = ROWS * FACES
UNROLL = 64
LAG = 7

time_step = 0.2
stiff_coef = 4.0 / (8.0 * NODES)
damp_coef = 1.0 / (8.0 * NODES)
exponent_scale = float(np.sqrt(np.log2(np.e) / 2.0))
frame_extent = 4.0

f32 = jnp.float32
bf16 = jnp.bfloat16
PARAMS = pltpu.CompilerParams(vmem_limit_bytes=16 * 1024 * 1024)


def sublanes(shape):
    return lax.broadcasted_iota(jnp.int32, shape, 0)


def lanes(shape):
    return lax.broadcasted_iota(jnp.int32, shape, 1)


def split3(value):
    high = value.astype(bf16).astype(f32)
    rest = value - high
    middle = rest.astype(bf16).astype(f32)
    return high, middle, rest - middle


def frame_tile():
    shape = (8, NODES)
    place = (lanes(shape).astype(f32) - (NODES - 1) / 2.0) * (frame_extent / NODES)
    return jnp.where(sublanes(shape) == 1, place, 0.0)


def tile_constants():
    row = sublanes((8, NODES))
    return frame_tile(), (row < 3).astype(f32), (row == 3).astype(f32), (row == 4).astype(f32)


def tile_parts(disp, vel, consts):
    frame, first3, row3, _ = consts
    place = disp + frame
    scaled = (place * exponent_scale) * first3
    half = 0.5 * jnp.sum(scaled * scaled, axis=0, keepdims=True)
    potential = (stiff_coef * place - damp_coef * vel) * first3 + row3
    return scaled, half, potential


def far_factor(scaled, half, consts):
    h, m, l = split3(scaled + half * consts[2] + consts[3])
    return jnp.concatenate([h, m, h, m, l, h], axis=0).astype(bf16)


def near_factor(scaled, half, consts):
    h, m, l = split3(scaled - consts[2] - half * consts[3])
    return jnp.concatenate([h, h, m, m, h, l], axis=0).astype(bf16)


def packed_potential(potential):
    h, m, l = split3(potential)
    return jnp.concatenate([h + pltpu.roll(m, 4, 0), l], axis=0).astype(bf16)


def fold(total):
    total = total[:8] + total[8:]
    return total + pltpu.roll(total, 4, 0)


def request_kernel(facing_hbm, disp_hbm, vel_hbm, send_ref, slot_ref, home_ref, surf_ref, facing_ref, top_ref, count_ref, sems):
    copies = [
        pltpu.make_async_copy(disp_hbm.at[:, DEPTH - 1], top_ref.at[0], sems.at[0]),
        pltpu.make_async_copy(vel_hbm.at[:, DEPTH - 1], top_ref.at[1], sems.at[1]),
        pltpu.make_async_copy(facing_hbm, facing_ref, sems.at[2]),
    ]
    for copy in copies:
        copy.start()

    def clear(i, carry):
        count_ref[i] = 0
        return carry

    lax.fori_loop(0, NODES, clear, 0, unroll=16)
    for copy in copies:
        copy.wait()
    zero = jnp.zeros((ROWS, NODES), f32)
    for c in range(3):
        surf_ref[:, c, :] = top_ref[0, c]
        surf_ref[:, 3 + c, :] = top_ref[1, c]
        if c < 2:
            surf_ref[:, 6 + c, :] = zero
    row6 = (sublanes((8, NODES)) == 6).astype(f32)

    def visit(b, carry):
        tile = surf_ref[b]
        for k in range(FACES):
            name = facing_ref[k, b]
            block = lax.shift_right_logical(name, 4)
            owner = lax.shift_left(lax.shift_right_logical(block, 5), 4) | (name & 15)
            used = count_ref[owner]
            count_ref[owner] = used + 1
            slot = 2 * owner + used
            slot_ref[b * FACES + k] = slot
            home_ref[slot] = b
            send_ref[slot] = tile + row6 * jnp.full((8, NODES), block & 31, jnp.int32).astype(f32)
        return carry

    lax.fori_loop(0, ROWS, visit, 0)


def edge_rows(value, x):
    return [value[c, z, x : x + 1, :] for c in range(value.shape[0]) for z in range(DEPTH)]


def table_kernel(surf_ref, near_ref, exact_ref, pot_ref=None, tail_ref=None):
    consts = tile_constants()
    unit = (lanes((NODES, NODES)) == sublanes((NODES, NODES))).astype(bf16)

    def table(b, carry):
        tile = surf_ref[b]
        scaled, half, potential = tile_parts(tile, pltpu.roll(tile, 5, 0), consts)
        near = near_factor(scaled, half, consts)
        turned = lax.dot_general(unit, near, (((1,), (1,)), ((), ())), preferred_element_type=f32)
        near_ref[b] = turned.astype(bf16)
        exact_ref[b] = potential
        if pot_ref is not None:
            pot_ref[b] = packed_potential(potential)
            tail_ref[b] = (pltpu.roll(tile, 3, 0) * consts[2])[:4]
        return carry

    lax.fori_loop(0, ROWS, table, 0, unroll=4)


def edge_kernel(with_stiff, *refs):
    if with_stiff:
        last_ref, disp_ref, surf_ref, stiff_ref, *refs = refs
        low_row, high_row, low_col, high_col, near_ref, exact_ref, pot_ref, tail_ref, masked_ref = refs
    else:
        disp_ref, surf_ref, low_row, high_row, low_col, high_col, near_ref, exact_ref = refs
    shape = (ROWS, NODES)
    lane = lanes(shape)
    if with_stiff:
        row = sublanes(shape)
        keep = ((row < ROWS - 1) | (last_ref[0] == 0)) & ((lane < NODES - 1) | (last_ref[1] == 0))
        for z in range(DEPTH):
            if z < DEPTH - 1:
                masked_ref[z] = jnp.where(keep, stiff_ref[z], 0.0)
            else:
                masked_ref[z] = jnp.zeros(shape, f32)
    low = jnp.zeros(shape, f32)
    high = jnp.zeros(shape, f32)
    low_row[...] = jnp.zeros((24, NODES), f32)
    high_row[...] = jnp.zeros((24, NODES), f32)
    for c in range(4 if with_stiff else 3):
        for z in range(DEPTH):
            at = c * DEPTH + z
            value = disp_ref[c, z] if c < 3 else masked_ref[z]
            low_row[at : at + 1, :] = value[0:1, :]
            high_row[at : at + 1, :] = value[ROWS - 1 :, :]
            low = jnp.where(lane == at, pltpu.roll(value, at, 1) if at else value, low)
            high = jnp.where(lane == at, pltpu.roll(value, at + 1, 1), high)
    low_col[...] = low
    high_col[...] = high
    if with_stiff:
        table_kernel(surf_ref, near_ref, exact_ref, pot_ref, tail_ref)
    else:
        table_kernel(surf_ref, near_ref, exact_ref)


def extended(center, above, below):
    row = sublanes((8, NODES))
    tail = jnp.where(row == 0, below, jnp.where(row == 7, above, 0.0))
    return jnp.concatenate([center, tail], axis=0)


def force_kernel(with_stiff, disp_ref, *refs):
    if with_stiff:
        stiff_ref, row_lo, row_hi, col_lo, col_hi, force_ref, wide_ref, node_ref = refs
    else:
        wide_in, node_in, row_lo, row_hi, col_lo, col_hi, put = refs
    wide = (ROWS + 8, NODES)
    lane = lanes(wide)
    last = lane == NODES - 1
    left = extended(col_lo[...], row_lo[24:25, :], row_hi[24:25, :])
    right = extended(col_hi[...], row_lo[25:26, :], row_hi[25:26, :])

    def own(c, z):
        value = disp_ref[c, z] if c < 3 else stiff_ref[z]
        at = c * DEPTH + z
        return extended(value, row_lo[at : at + 1, :], row_hi[at : at + 1, :])

    def at_last(cols, at):
        return pltpu.roll(cols, NODES - 1 - at, 1)

    def spread(main, side):
        main = main + pltpu.roll(main, 1, 0)
        side = side + pltpu.roll(side, 1, 0)
        return main + pltpu.roll(jnp.where(last, side, main), 1, 1)

    stiff = []
    if with_stiff:
        total = None
        for z in range(DEPTH - 1):
            main = own(3, z)
            side = at_last(left, 3 * DEPTH + z)
            wide_ref[z, 0] = main
            wide_ref[z, 1] = side
            stiff.append((main * 0.125, side * 0.125))
            out = spread(main, side)[:ROWS]
            node_ref[z] = out if total is None else total + out
            total = out
        node_ref[DEPTH - 1] = total
        node = node_ref
    else:
        for z in range(DEPTH - 1):
            stiff.append((wide_in[z, 0] * 0.125, wide_in[z, 1] * 0.125))
        node = node_in
    for c in range(3):
        boxes = []
        for z in range(DEPTH):
            value = own(c, z)
            turned = pltpu.roll(value, NODES - 1, 1)
            main = value + jnp.where(last, at_last(right, c * DEPTH + z), turned)
            side = at_last(left, c * DEPTH + z) + turned
            boxes.append((main, side))
        total = None
        for z in range(DEPTH):
            out = None
            if z < DEPTH - 1:
                main = boxes[z][0] + boxes[z + 1][0]
                side = boxes[z][1] + boxes[z + 1][1]
                main = main + pltpu.roll(main, ROWS + 7, 0)
                side = side + pltpu.roll(side, ROWS + 7, 0)
                out = spread(main * stiff[z][0], side * stiff[z][1])[:ROWS]
                pull = out if total is None else total + out
            else:
                pull = total
            total = out
            force = pull - disp_ref[c, z] * node[z]
            if with_stiff:
                force_ref[c, z] = force
            else:
                put(c, z, force)


def entry_rows(recv_ref, turn_ref, row_ref, sem):
    shape = (NODES, NODES)
    diagonal = lanes(shape) == sublanes(shape)
    for half in range(ENTRIES // NODES):
        held = recv_ref[half * NODES : (half + 1) * NODES, 6, :]
        picked = jnp.sum(jnp.where(diagonal, held, 0.0), axis=0, keepdims=True)
        turn_ref[half : half + 1, :] = picked.astype(jnp.int32)
    copy = pltpu.make_async_copy(turn_ref, row_ref, sem)
    copy.start()
    copy.wait()


def row_messages(low_row, high_row, col_lo, col_hi, low_out, high_out):
    for side, edge, at in ((low_out, low_row, 0), (high_out, high_row, ROWS - 1)):
        side[:24] = edge[...]
        side[24:25] = col_lo[at : at + 1, :]
        side[25:26] = col_hi[at : at + 1, :]
        side[26:] = jnp.zeros((ROWS - 26, NODES), f32)


def pair_loop(row_of, tile_of, near_ref, loc_ref, pot_ref=None, tail_ref=None, out_ref=None):
    consts = tile_constants()

    def visit(step, carry):
        entries = [step * UNROLL + j for j in range(UNROLL)]
        row = [row_of(step, j) for j in range(UNROLL)]
        held = {}

        def weigh(j):
            scaled, half, potential = tile_parts(*tile_of(entries[j]), consts)
            far = far_factor(scaled, half, consts)
            exponent = jnp.dot(near_ref[row[j]], far, preferred_element_type=f32)
            held[j] = exponent, packed_potential(potential), potential

        def reduce(j):
            exponent, far_pot, potential = held[j]
            weight = jnp.exp2(exponent)
            high = weight.astype(bf16)
            low = (weight - high.astype(f32)).astype(bf16)
            pulled = None
            if out_ref is not None:
                near_pot = pot_ref[row[j]]
                pulled = jnp.dot(
                    jnp.concatenate([near_pot, near_pot], axis=1),
                    jnp.concatenate([high, low], axis=0),
                    preferred_element_type=f32,
                )
            pushed = lax.dot_general(
                jnp.concatenate([far_pot, far_pot], axis=1),
                jnp.concatenate([high, low], axis=1),
                (((1,), (1,)), ((), ())),
                preferred_element_type=f32,
            )
            held[j] = pulled, pushed, potential

        def store(j):
            pulled, pushed, potential = held.pop(j)
            if out_ref is not None:
                pulled = fold(pulled)
                out_ref[entries[j]] = (pulled[3:4] * potential - pulled)[:4] + tail_ref[row[j]]
            loc_ref[row[j]] += pushed[:8] + pushed[8:]

        for t in range(UNROLL + LAG + 1):
            if t < UNROLL:
                weigh(t)
            if 0 <= t - LAG < UNROLL:
                reduce(t - LAG)
            if 0 <= t - LAG - 1 < UNROLL:
                store(t - LAG - 1)
        return carry

    lax.fori_loop(0, ENTRIES // UNROLL, visit, 0)


def split_row(row_ref):
    def row_of(step, j):
        first = step * UNROLL
        return row_ref[first // NODES, first % NODES + j]

    return row_of


def wide_tile(value):
    return jnp.concatenate([value, jnp.zeros((4, NODES), f32)], axis=0)


def contact_first(recv_ref, near_ref, pot_ref, tail_ref, low_row, high_row, col_lo, col_hi, *refs):
    out_ref, loc_ref, low_out, high_out, row_ref, turn_ref, sem = refs
    entry_rows(recv_ref, turn_ref, row_ref, sem)
    row_messages(low_row, high_row, col_lo, col_hi, low_out, high_out)
    loc_ref[...] = jnp.zeros((ROWS, 8, NODES), f32)

    def tile_of(e):
        tile = recv_ref[e]
        return tile, pltpu.roll(tile, 5, 0)

    pair_loop(split_row(row_ref), tile_of, near_ref, loc_ref, pot_ref, tail_ref, out_ref)


def contact_last(row_ref, home_ref, first_ref, x_ref, new_ref, near_ref, loc_ref):
    loc_ref[...] = jnp.zeros((ROWS, 8, NODES), f32)
    row = sublanes((8, NODES))

    def faced(e):
        vel = new_ref[e]
        return first_ref[e] + time_step * vel, vel

    def facing(e):
        tile = new_ref[e]
        vel = pltpu.roll(tile, 4, 0)
        x = pltpu.roll(wide_tile(x_ref[e]), 5, 0)
        y = pltpu.roll(tile, 6, 0)
        z = pltpu.roll(tile, 3, 0)
        disp = jnp.where(row == 0, x, jnp.where(row == 1, y, z))
        return disp + time_step * vel, vel

    pair_loop(split_row(row_ref), faced, near_ref, loc_ref)
    pair_loop(lambda step, j: home_ref[step * UNROLL + j], facing, near_ref, loc_ref)


def local_sum(loc_ref, exact_ref, b):
    total = loc_ref[b]
    total = total + pltpu.roll(total, 4, 0)
    return (total[3:4] * exact_ref[b] - total)[:4]


def update_kernel(
    slot_ref, home_ref, row_ref, ret_ref, loc_ref, exact_ref, force_ref, disp_ref, vel_ref, mass_ref, old_ref, *refs
):
    new_disp, new_vel, send_ref, surf_ref, sum_ref, facing_tile, faced_tile = refs

    def gather(b, carry):
        acc = local_sum(loc_ref, exact_ref, b)
        for k in range(FACES):
            acc = acc + ret_ref[slot_ref[b * FACES + k]]
        sum_ref[b] = acc
        return carry

    lax.fori_loop(0, ROWS, gather, 0, unroll=4)
    for c in range(2):
        surf_ref[:, 6 + c, :] = jnp.zeros((ROWS, NODES), f32)
    for z in reversed(range(DEPTH)):
        mass = time_step * mass_ref[z]
        for c in range(3):
            force = force_ref[c, z]
            if z == DEPTH - 1:
                force = force + sum_ref[:, c, :]
            vel = vel_ref[c, z] + mass * force
            disp = disp_ref[c, z] + time_step * vel
            new_vel[c, z] = vel
            new_disp[c, z] = disp
            if z == DEPTH - 1:
                surf_ref[:, c, :] = disp
                surf_ref[:, 3 + c, :] = vel
    row = sublanes((8, NODES))

    def tiles(b, carry):
        tile = surf_ref[b]
        vel = pltpu.roll(tile, 5, 0)
        old = old_ref[b]
        facing_tile[b] = jnp.where(row < 3, vel, 0.0)
        late = jnp.where(row < 7, pltpu.roll(tile, 1, 0), pltpu.roll(old, 5, 0))
        faced_tile[b] = jnp.where(row < 3, 0.0, jnp.where(row == 3, pltpu.roll(old, 2, 0), late))
        return carry

    lax.fori_loop(0, ROWS, tiles, 0, unroll=8)

    def scatter(i, carry):
        for j in range(16):
            e = i * 16 + j
            r = row_ref[i * 16 // NODES, i * 16 % NODES + j]
            send_ref[e] = facing_tile[home_ref[e]] + faced_tile[r]
        return carry

    lax.fori_loop(0, ENTRIES // 16, scatter, 0)


def final_kernel(
    disp_ref, vel_ref, mass_ref, loc_ref, exact_ref, wide_in, node_in, row_lo, row_hi, col_lo, col_hi, *refs
):
    new_disp, new_vel, sum_ref = refs

    def gather(b, carry):
        sum_ref[b] = local_sum(loc_ref, exact_ref, b)
        return carry

    lax.fori_loop(0, ROWS, gather, 0, unroll=8)

    def put(c, z, force):
        if z == DEPTH - 1:
            force = force + sum_ref[:, c, :]
        vel = vel_ref[c, z] + time_step * mass_ref[z] * force
        new_vel[c, z] = vel
        new_disp[c, z] = disp_ref[c, z] + time_step * vel

    force_kernel(False, disp_ref, wide_in, node_in, row_lo, row_hi, col_lo, col_hi, put)


VMEM = pl.BlockSpec(memory_space=pltpu.VMEM)
SMEM = pl.BlockSpec(memory_space=pltpu.SMEM)
HBM = pl.BlockSpec(memory_space=pltpu.HBM)


def struct(*shape, dtype=f32):
    return jax.ShapeDtypeStruct(shape, dtype)


def shifted(value, count_gx, count_gy, dx, dy):
    pairs = []
    for x in range(count_gx):
        for y in range(count_gy):
            if 0 <= x + dx < count_gx and 0 <= y + dy < count_gy:
                pairs.append((x * count_gy + y, (x + dx) * count_gy + y + dy))
    return lax.ppermute(value, AXES, pairs)


def scalars(value):
    return pltpu.with_memory_space_constraint(value, pltpu.SMEM)


def local(displacement, velocity, stiffness, inverse_mass, facing):
    count_gx = lax.axis_size("gx")
    count_gy = lax.axis_size("gy")
    disp = displacement.transpose(0, 2, 1, 3)
    vel = velocity.transpose(0, 2, 1, 3)
    stiff = stiffness.transpose(1, 0, 2)
    mass = inverse_mass.transpose(1, 0, 2)
    faces = facing.transpose(1, 2, 0).reshape(FACES, ROWS)
    ends = jnp.stack(
        [
            (lax.axis_index("gx") == count_gx - 1).astype(jnp.int32),
            (lax.axis_index("gy") == count_gy - 1).astype(jnp.int32),
        ]
    )
    send, slots, homes, surf = pl.pallas_call(
        request_kernel,
        in_specs=[HBM] * 3,
        out_specs=[VMEM, SMEM, SMEM, VMEM],
        out_shape=[
            struct(ENTRIES, 8, NODES),
            pltpu.SMEM((ENTRIES,), jnp.int32),
            pltpu.SMEM((ENTRIES,), jnp.int32),
            struct(ROWS, 8, NODES),
        ],
        scratch_shapes=[
            pltpu.SMEM((FACES, ROWS), jnp.int32),
            pltpu.VMEM((2, 3, ROWS, NODES), f32),
            pltpu.SMEM((NODES,), jnp.int32),
            pltpu.SemaphoreType.DMA((3,)),
        ],
        compiler_params=PARAMS,
        name="request",
    )(*(pltpu.with_memory_space_constraint(value, pltpu.HBM) for value in (faces, disp, vel)))
    near_shape = struct(ROWS, NODES, 48, dtype=bf16)
    tile_shape = struct(ROWS, 8, NODES)
    small_shape = struct(ROWS, 4, NODES)
    edge_shape = struct(ROWS, NODES)
    edge_shapes = [struct(24, NODES), struct(24, NODES), edge_shape, edge_shape, near_shape, tile_shape]
    field_shape = struct(3, DEPTH, ROWS, NODES)
    entry_shape = struct(ENTRIES, 4, NODES)

    def go(value, dx, dy):
        return shifted(value, count_gx, count_gy, dx, dy)

    def exchange(value):
        return lax.all_to_all(value, AXES, 0, 0, tiled=True)

    def call(kernel, name, in_specs, out_specs, out_shape, scratch=()):
        return pl.pallas_call(
            kernel,
            in_specs=in_specs,
            out_specs=out_specs,
            out_shape=out_shape,
            scratch_shapes=scratch,
            compiler_params=PARAMS,
            name=name,
        )

    first = exchange(send)
    low_row, high_row, low_col, high_col, near, exact, pot, tail, masked = call(
        lambda *refs: edge_kernel(True, *refs),
        "edges_first",
        [SMEM] + [VMEM] * 3,
        [VMEM] * 9,
        edge_shapes + [struct(ROWS, 16, NODES, dtype=bf16), small_shape, struct(DEPTH, ROWS, NODES)],
    )(ends, disp, surf, stiff)
    col_lo = go(high_col, 0, 1)
    col_hi = go(low_col, 0, -1)
    action, reaction, low_out, high_out, rows = call(
        contact_first,
        "contact_first",
        [VMEM] * 8,
        [VMEM] * 4 + [SMEM],
        [entry_shape, tile_shape, edge_shape, edge_shape, pltpu.SMEM((ENTRIES // NODES, NODES), jnp.int32)],
        [pltpu.VMEM((ENTRIES // NODES, NODES), jnp.int32), pltpu.SemaphoreType.DMA(())],
    )(first, near, pot, tail, low_row, high_row, col_lo, col_hi)
    returned = exchange(action)
    row_lo = go(high_out, 1, 0)
    row_hi = go(low_out, -1, 0)
    force, wide, node = call(
        lambda *refs: force_kernel(True, *refs),
        "force_first",
        [VMEM] * 6,
        [VMEM] * 3,
        [field_shape, struct(DEPTH - 1, 2, ROWS + 8, NODES), struct(DEPTH, ROWS, NODES)],
    )(disp, masked, row_lo, row_hi, col_lo, col_hi)
    table = pltpu.VMEM((ROWS, 4, NODES), f32)
    tiles = pltpu.VMEM((ROWS, 8, NODES), f32)
    disp, vel, send, surf = call(
        update_kernel,
        "update_first",
        [SMEM] * 3 + [VMEM] * 8,
        [VMEM] * 4,
        [field_shape, field_shape, struct(ENTRIES, 8, NODES), tile_shape],
        [table, tiles, tiles],
    )(scalars(slots), scalars(homes), scalars(rows), returned, reaction, exact, force, disp, vel, mass, surf)

    news = exchange(send)
    low_row, high_row, low_col, high_col, near, exact = call(
        lambda *refs: edge_kernel(False, *refs), "edges_last", [VMEM] * 2, [VMEM] * 6, edge_shapes
    )(disp, surf)
    col_lo = go(high_col, 0, 1)
    col_hi = go(low_col, 0, -1)
    low_out, high_out = call(row_messages, "rows_last", [VMEM] * 4, [VMEM] * 2, [edge_shape] * 2)(
        low_row, high_row, col_lo, col_hi
    )
    row_lo = go(high_out, 1, 0)
    row_hi = go(low_out, -1, 0)
    (total,) = call(contact_last, "contact_last", [SMEM] * 2 + [VMEM] * 4, [VMEM], [tile_shape])(
        scalars(rows), scalars(homes), first, returned, news, near
    )
    disp, vel = call(final_kernel, "update_last", [VMEM] * 11, [VMEM] * 2, [field_shape] * 2, [table])(
        disp, vel, mass, total, exact, wide, node, row_lo, row_hi, col_lo, col_hi
    )
    return disp.transpose(0, 2, 1, 3), vel.transpose(0, 2, 1, 3)


def solution(mesh):
    in_specs = (
        P(None, "gx", None, "gy"),
        P(None, "gx", None, "gy"),
        P("gx", None, "gy"),
        P("gx", None, "gy"),
        P("gx", "gy", None),
    )
    out_specs = (P(None, "gx", None, "gy"), P(None, "gx", None, "gy"))
    return jax.shard_map(local, mesh=mesh, in_specs=in_specs, out_specs=out_specs, check_vma=False)
```

time: 126 us -> 109 us (0.87); the launches traced: 123 us -> 108 us
  starting transfers between devices: 60.8 us -> 50.3 us
  waiting for transfers between devices: 21.1 us -> 17.1 us
  local copies, waits for them, and re-layouts: 8.79 us -> 5.16 us
  Pallas kernels: 31.7 us -> 34.7 us
    all_to_all x4 -> x3, starting transfers between devices: 34.9 us -> 23.8 us  [exchange(): return lax.all_to_all(value, AXES, 0, 0, tiled=True)]
    unnamed x40 -> x26, local copies, waits for them, and re-layouts: 8.79 us -> 5.16 us
    all_to_all x4 -> x3, waiting for transfers between devices: 8.3 us -> 4.94 us  [exchange(): return lax.all_to_all(value, AXES, 0, 0, tiled=True)]
    pallas_call x9, Pallas kernels: 31.7 us -> 34.7 us  [the longest x1 13.3 us: local(): call(contact_last, 'contact_last', [SMEM] * 2 + [VMEM] * 4, [VMEM], [tile...]
  transfers between devices with their start and end apart: 12 -> 11, of which waited for: 8 -> 5; matrix products, arithmetic and copies ran while one was open for 0% -> 0% of each run, Pallas kernels for 4% -> 16%
where the time goes in v2:
time: 109 us; the launch traced here: 108 us
  starting transfers between devices  50.3 us (46%)
  Pallas kernels  34.7 us (32%)
  waiting for transfers between devices  17.1 us (16%)
  local copies, waits for them, and re-layouts  5.16 us (5%)
    ppermute x8, starting transfers between devices, shifted(): return lax.ppermute(value, AXES, pairs)  26.5 us
    all_to_all x3, starting transfers between devices, exchange(): return lax.all_to_all(value, AXES, 0, 0, tiled=True)  23.8 us
    pallas_call x1, Pallas kernels, local(): call(contact_last, 'contact_last', [SMEM] * 2 + [VMEM] * 4, [VMEM], [tile...  13.3 us
    ppermute x8, waiting for transfers between devices, shifted(): return lax.ppermute(value, AXES, pairs)  12.1 us
    pallas_call x1, Pallas kernels, local(): call(contact_first, 'contact_first', [VMEM] * 8, [VMEM] * 4 + [SMEM], [en...  10.3 us
    unnamed x26, local copies, waits for them, and re-layouts  5.16 us
    all_to_all x3, waiting for transfers between devices, exchange(): return lax.all_to_all(value, AXES, 0, 0, tiled=True)  4.94 us
    pallas_call x1, Pallas kernels, local(): pl.pallas_call(request_kernel, in_specs=[HBM] * 3, out_specs=[VMEM, SMEM,...  3.66 us
  transfers between devices with their start and end apart: 11, of which 5 were waited for; matrix products, arithmetic and copies ran while one was open for 0% of the time, Pallas kernels for 16%

profile of v2, /device:TPU:7, one launch (start us, length us, event | category | flops | bytes accessed | tf_op | source)
XLA Modules:
  0.0 108.1 jit_solution(18287040635758254795)
XLA Ops:
  0.6 3.7 %request.1 = (f32[256,8,128]{2,1,0:T(8,128)}, s32[256]{0:T(256)S(4)}, s32[256]{0:T(256)S(4)}, f32[32,8,128]{2,1,0:T(8,128)S(1)}) custom-call(s32[8,32]{1,0:T(8,128)} %bitcast.20, f32[3,5,32,128]{3,2,1,0:T(8,128)} %bitcast.11, f32[3,5,32,128]{3,2,1,0:T(8,128)} %bitcast.15), custom_call_target="tpu_custom_call" | custom-call | tf_op jit(solution)/shard_map/request/pallas_call | solution.py:494
  4.3 10.8 %all-to-all-start = ((f32[256,8,128]{2,1,0:T(8,128)}), f32[256,8,128]{2,1,0:T(8,128)S(1)}, u32[]{:S(2)}, u32[]{:S(2)}) async-start(f32[256,8,128]{2,1,0:T(8,128)} %get-tuple-element.39), calls=%async_computation | async-start | bytes 2097152 | tf_op jit(solution)/shard_map/all_to_all | solution.py:525
  15.2 2.2 %edges_first.1 = (f32[24,128]{1,0:T(8,128)S(1)}, f32[24,128]{1,0:T(8,128)S(1)}, f32[32,128]{1,0:T(8,128)S(1)}, f32[32,128]{1,0:T(8,128)S(1)}, bf16[32,128,48]{2,...) custom-call(s32[2]{0:T(128)S(1)} %add_convert_fusion.refs_0_, ...), custom_call_target="tpu_custom_call" | custom-call | tf_op jit(solution)/shard_map/edges_first/pallas_call | solution.py:539
  17.5 3.1 %collective-permute-start = (f32[32,128]{1,0:T(8,128)S(1)}, f32[32,128]{1,0:T(8,128)S(1)}, u32[]{:S(2)}, u32[]{:S(2)}) collective-permute-start(f32[32,128]{1,0:T(8,128)S(1)} %get-tuple-element.46), channel_id=1, source_target_pairs={{0,1},{1,2},{2,3},{3,4},{4,5},{5,6},{6,7},{7,8},{8,9},{9,10},{10,1... | collective-permute-start | bytes 49160 | tf_op jit(solution)/shard_map/ppermute | solution.py:473
  20.6 4.3 %collective-permute-start.1 = (f32[32,128]{1,0:T(8,128)S(1)}, f32[32,128]{1,0:T(8,128)S(1)}, u32[]{:S(2)}, u32[]{:S(2)}) collective-permute-start(f32[32,128]{1,0:T(8,128)S(1)} %get-tuple-element.47), channel_id=1, source_target_pairs={{1,0},{2,1},{3,2},{4,3},{5,4},{6,5},{7,6},{8,7},{9,8},{10,9},{11,1... | collective-permute-start | bytes 49160 | tf_op jit(solution)/shard_map/ppermute | solution.py:473
  24.9 4.7 %collective-permute-done.col_lo.refs_4_ = f32[32,128]{1,0:T(8,128)S(1)} collective-permute-done((f32[32,128]{1,0:T(8,128)S(1)}, f32[32,128]{1,0:T(8,128)S(1)}, u32[]{:S(2)}, u32[]{:S(2)}) %collective-permute-start) | collective-permute-done | bytes 16416 | tf_op jit(solution)/shard_map/ppermute | solution.py:473
  29.6 3.2 %all-to-all-done.recv_ref.first_ref = f32[256,8,128]{2,1,0:T(8,128)S(1)} async-done(((f32[256,8,128]{2,1,0:T(8,128)}), f32[256,8,128]{2,1,0:T(8,128)S(1)}, u32[]{:S(2)}, u32[]{:S(2)}) %all-to-all-start) | async-done | bytes 1048608 | tf_op jit(solution)/shard_map/all_to_all | solution.py:525
  32.8 10.3 %contact_first.1 = (f32[256,4,128]{2,1,0:T(4,128)}, f32[32,8,128]{2,1,0:T(8,128)S(1)}, f32[32,128]{1,0:T(8,128)S(1)}, f32[32,128]{1,0:T(8,128)S(1)}, s32[2,128]{1,0:T(2,128)S(4)}) custom-call(f32[256,8,128]{2,1,0:T(8,128)S(1)} %all-to-all-done.recv_ref.first_ref, bf16[32,128,48]{2,1,0:T(8,128)(2,1)S(1)} %get-tuple-element.41.near_ref, ...), custom_call_target="tpu_custom_call" | custom-call | tf_op jit(solution)/shard_map/contact_first/pallas_call | solution.py:548
  43.1 5.9 %all-to-all-start.1 = ((f32[256,4,128]{2,1,0:T(4,128)}), f32[256,4,128]{2,1,0:T(4,128)S(1)}, u32[]{:S(2)}, u32[]{:S(2)}) async-start(f32[256,4,128]{2,1,0:T(4,128)} %get-tuple-element.49), calls=%async_computation.1 | async-start | bytes 1048576 | tf_op jit(solution)/shard_map/all_to_all | solution.py:525
  49.0 3.7 %collective-permute-start.2 = (f32[32,128]{1,0:T(8,128)S(1)}, f32[32,128]{1,0:T(8,128)S(1)}, u32[]{:S(2)}, u32[]{:S(2)}) collective-permute-start(f32[32,128]{1,0:T(8,128)S(1)} %get-tuple-element.53), channel_id=1, source_target_pairs={{0,16},{1,17},{2,18},{3,19},{4,20},{5,21},{6,22},{7,23},{8,24},{9,... | collective-permute-start | bytes 49160 | tf_op jit(solution)/shard_map/ppermute | solution.py:473
  52.7 1.9 %collective-permute-start.3 = (f32[32,128]{1,0:T(8,128)S(1)}, f32[32,128]{1,0:T(8,128)S(1)}, u32[]{:S(2)}, u32[]{:S(2)}) collective-permute-start(f32[32,128]{1,0:T(8,128)S(1)} %get-tuple-element.54), channel_id=1, source_target_pairs={{16,0},{17,1},{18,2},{19,3},{20,4},{21,5},{22,6},{23,7},{24,8},{25... | collective-permute-start | bytes 49160 | tf_op jit(solution)/shard_map/ppermute | solution.py:473
  54.7 3.6 %collective-permute-done.3.refs_3_ = f32[32,128]{1,0:T(8,128)S(1)} collective-permute-done((f32[32,128]{1,0:T(8,128)S(1)}, f32[32,128]{1,0:T(8,128)S(1)}, u32[]{:S(2)}, u32[]{:S(2)}) %collective-permute-start.3) | collective-permute-done | bytes 16416 | tf_op jit(solution)/shard_map/ppermute | solution.py:473
  59.6 1.7 %all-to-all-done.1.ret_ref.x_ref = f32[256,4,128]{2,1,0:T(4,128)S(1)} async-done(((f32[256,4,128]{2,1,0:T(4,128)}), f32[256,4,128]{2,1,0:T(4,128)S(1)}, u32[]{:S(2)}, u32[]{:S(2)}) %all-to-all-start.1) | async-done | bytes 524320 | tf_op jit(solution)/shard_map/all_to_all | solution.py:525
  61.3 1.6 %update_first.1 = (f32[3,5,32,128]{3,2,1,0:T(8,128)S(1)}, f32[3,5,32,128]{3,2,1,0:T(8,128)S(1)}, f32[256,8,128]{2,1,0:T(8,128)S(1)}, f32[32,8,128]{2,1,0:T(8,128)S(1)}) custom-call(s32[256]{0:T(256)S(4)} %get-tuple-element.37.slot_ref, s32[256]{0:T(256)S(4)} %get-tuple-element.38.home_ref, s32[2,128]{1,0:T(2,128)S(4)} %get-tuple-element.48.row_ref, ...), custom_call_target="tpu_custom_call" | custom-call | tf_op jit(solution)/shard_map/update_first/pallas_call | solution.py:568
  64.5 7.1 %all-to-all-start.2 = ((f32[256,8,128]{2,1,0:T(8,128)}), f32[256,8,128]{2,1,0:T(8,128)S(1)}, u32[]{:S(2)}, u32[]{:S(2)}) async-start(f32[256,8,128]{2,1,0:T(8,128)} %copy-done.3), calls=%async_computation.2 | async-start | bytes 2097152 | tf_op jit(solution)/shard_map/all_to_all | solution.py:525
  71.6 1.7 %edges_last.1 = (f32[24,128]{1,0:T(8,128)S(1)}, f32[24,128]{1,0:T(8,128)S(1)}, f32[32,128]{1,0:T(8,128)S(1)}, f32[32,128]{1,0:T(8,128)S(1)}, bf16[32,128,48]{2,1...) custom-call(f32[3,5,32,128]{3,2,1,0:T(8,128)S(1)} %get-tuple-element.56.refs_0_.disp_ref, f32[32,8,128]{2,1,0:T(8,128)S(1)} %copy-done.11), custom_call_target="tpu_custom_call" | custom-call | tf_op jit(solution)/shard_map/edges_last/pallas_call | solution.py:578
  74.9 3.1 %collective-permute-start.4 = (f32[32,128]{1,0:T(8,128)S(1)}, f32[32,128]{1,0:T(8,128)S(1)}, u32[]{:S(2)}, u32[]{:S(2)}) collective-permute-start(f32[32,128]{1,0:T(8,128)S(1)} %get-tuple-element.66), channel_id=1, source_target_pairs={{0,1},{1,2},{2,3},{3,4},{4,5},{5,6},{6,7},{7,8},{8,9},{9,10},{10,1... | collective-permute-start | bytes 49160 | tf_op jit(solution)/shard_map/ppermute | solution.py:473
  78.0 4.3 %collective-permute-start.5 = (f32[32,128]{1,0:T(8,128)S(1)}, f32[32,128]{1,0:T(8,128)S(1)}, u32[]{:S(2)}, u32[]{:S(2)}) collective-permute-start(f32[32,128]{1,0:T(8,128)S(1)} %get-tuple-element.67), channel_id=1, source_target_pairs={{1,0},{2,1},{3,2},{4,3},{5,4},{6,5},{7,6},{8,7},{9,8},{10,9},{11,1... | collective-permute-start | bytes 49160 | tf_op jit(solution)/shard_map/ppermute | solution.py:473
  82.3 3.8 %collective-permute-done.4.col_lo = f32[32,128]{1,0:T(8,128)S(1)} collective-permute-done((f32[32,128]{1,0:T(8,128)S(1)}, f32[32,128]{1,0:T(8,128)S(1)}, u32[]{:S(2)}, u32[]{:S(2)}) %collective-permute-start.4) | collective-permute-done | bytes 16416 | tf_op jit(solution)/shard_map/ppermute | solution.py:473
  86.1 4.1 %collective-permute-start.6 = (f32[32,128]{1,0:T(8,128)S(1)}, f32[32,128]{1,0:T(8,128)S(1)}, u32[]{:S(2)}, u32[]{:S(2)}) collective-permute-start(f32[32,128]{1,0:T(8,128)S(1)} %get-tuple-element.68), channel_id=1, source_target_pairs={{0,16},{1,17},{2,18},{3,19},{4,20},{5,21},{6,22},{7,23},{8,24},{9,... | collective-permute-start | bytes 49160 | tf_op jit(solution)/shard_map/ppermute | solution.py:473
  90.2 1.9 %collective-permute-start.7 = (f32[32,128]{1,0:T(8,128)S(1)}, f32[32,128]{1,0:T(8,128)S(1)}, u32[]{:S(2)}, u32[]{:S(2)}) collective-permute-start(f32[32,128]{1,0:T(8,128)S(1)} %get-tuple-element.69), channel_id=1, source_target_pairs={{16,0},{17,1},{18,2},{19,3},{20,4},{21,5},{22,6},{23,7},{24,8},{25... | collective-permute-start | bytes 49160 | tf_op jit(solution)/shard_map/ppermute | solution.py:473
  92.2 1.2 %copy-done.2 = bf16[32,128,48]{2,1,0:T(8,128)(2,1)S(1)} copy-done((bf16[32,128,48]{2,1,0:T(8,128)(2,1)S(1)}, bf16[32,128,48]{2,1,0:T(8,128)(2,1)}, u32[]{:S(2)}) %copy-start.2) | copy-done | bytes 393240
  93.4 13.3 %contact_last.1.loc_ref = f32[32,8,128]{2,1,0:T(8,128)S(1)} custom-call(s32[2,128]{1,0:T(2,128)S(4)} %get-tuple-element.48.row_ref, s32[256]{0:T(256)S(4)} %get-tuple-element.38.home_ref, f32[256,8,128]{2,1,0:T(8,128)S(1)} %all-to-all-done.recv_ref.first_ref, f32[256,4,128]{2,1,0:T(4,128)S(1)} %all-to-all-done.1.ret_ref.x_ref, ...), custom_call_target="tpu_custom_call" | custom-call | tf_op jit(solution)/shard_map/contact_last/pallas_call | solution.py:588
  106.7 1.4 %update_last.1 = (f32[3,5,32,128]{3,2,1,0:T(8,128)}, f32[3,5,32,128]{3,2,1,0:T(8,128)}) custom-call(f32[3,5,32,128]{3,2,1,0:T(8,128)S(1)} %get-tuple-element.56.refs_0_.disp_ref, f32[3,5,32,128]{3,2,1,0:T(8,128)S(1)} %get-tuple-element.57.vel_ref, f32[5,32,128]{2,1,0:T(8,128)S(1)} %bitcast.18, f32[32,8,128]{2,1,0:T(8,128)S(1)} %contact_last.1.loc_ref, ...), custom_call_target="tpu_custom_call" | custom-call | tf_op jit(solution)/shard_map/update_last/pallas_call | solution.py:591
  (34 shorter events, 4.6 us)
Async XLA Ops:
  4.3 10.9 %copy-start = (f32[3,32,5,128]{3,1,2,0:T(8,128)S(1)}, f32[3,32,5,128]{3,1,2,0:T(8,128)}, u32[]{:S(2)}) copy-start(f32[3,32,5,128]{3,1,2,0:T(8,128)} %param.5) | copy-start | bytes 737284
  4.3 10.9 %copy-start.12 = (f32[32,5,128]{2,0,1:T(8,128)S(1)}, f32[32,5,128]{2,0,1:T(8,128)}, u32[]{:S(2)}) copy-start(f32[32,5,128]{2,0,1:T(8,128)} %param.7) | copy-start | bytes 245764
  4.3 28.5 %all-to-all-start = ((f32[256,8,128]{2,1,0:T(8,128)}), f32[256,8,128]{2,1,0:T(8,128)S(1)}, u32[]{:S(2)}, u32[]{:S(2)}) async-start(f32[256,8,128]{2,1,0:T(8,128)} %get-tuple-element.39), calls=%async_computation | async-start | bytes 2097152 | tf_op jit(solution)/shard_map/all_to_all | solution.py:525
  17.5 12.1 %collective-permute-start = (f32[32,128]{1,0:T(8,128)S(1)}, f32[32,128]{1,0:T(8,128)S(1)}, u32[]{:S(2)}, u32[]{:S(2)}) collective-permute-start(f32[32,128]{1,0:T(8,128)S(1)} %get-tuple-element.46), channel_id=1, source_target_pairs={{0,1},{1,2},{2,3},{3,4},{4,5},{5,6},{6,7},{7,8},{8,9},{9,10},{10,1... | collective-permute-start | bytes 49160 | tf_op jit(solution)/shard_map/ppermute | solution.py:473
  20.6 9.0 %collective-permute-start.1 = (f32[32,128]{1,0:T(8,128)S(1)}, f32[32,128]{1,0:T(8,128)S(1)}, u32[]{:S(2)}, u32[]{:S(2)}) collective-permute-start(f32[32,128]{1,0:T(8,128)S(1)} %get-tuple-element.47), channel_id=1, source_target_pairs={{1,0},{2,1},{3,2},{4,3},{5,4},{6,5},{7,6},{8,7},{9,8},{10,9},{11,1... | collective-permute-start | bytes 49160 | tf_op jit(solution)/shard_map/ppermute | solution.py:473
  43.1 18.2 %all-to-all-start.1 = ((f32[256,4,128]{2,1,0:T(4,128)}), f32[256,4,128]{2,1,0:T(4,128)S(1)}, u32[]{:S(2)}, u32[]{:S(2)}) async-start(f32[256,4,128]{2,1,0:T(4,128)} %get-tuple-element.49), calls=%async_computation.1 | async-start | bytes 1048576 | tf_op jit(solution)/shard_map/all_to_all | solution.py:525
  49.0 12.3 %copy-start.4 = (f32[3,32,5,128]{3,1,2,0:T(8,128)S(1)}, f32[3,32,5,128]{3,1,2,0:T(8,128)}, u32[]{:S(2)}) copy-start(f32[3,32,5,128]{3,1,2,0:T(8,128)} %param.6) | copy-start | bytes 737284
  49.0 5.7 %collective-permute-start.2 = (f32[32,128]{1,0:T(8,128)S(1)}, f32[32,128]{1,0:T(8,128)S(1)}, u32[]{:S(2)}, u32[]{:S(2)}) collective-permute-start(f32[32,128]{1,0:T(8,128)S(1)} %get-tuple-element.53), channel_id=1, source_target_pairs={{0,16},{1,17},{2,18},{3,19},{4,20},{5,21},{6,22},{7,23},{8,24},{9,... | collective-permute-start | bytes 49160 | tf_op jit(solution)/shard_map/ppermute | solution.py:473
  52.7 5.6 %collective-permute-start.3 = (f32[32,128]{1,0:T(8,128)S(1)}, f32[32,128]{1,0:T(8,128)S(1)}, u32[]{:S(2)}, u32[]{:S(2)}) collective-permute-start(f32[32,128]{1,0:T(8,128)S(1)} %get-tuple-element.54), channel_id=1, source_target_pairs={{16,0},{17,1},{18,2},{19,3},{20,4},{21,5},{22,6},{23,7},{24,8},{25... | collective-permute-start | bytes 49160 | tf_op jit(solution)/shard_map/ppermute | solution.py:473
  58.3 3.0 %copy-start.5 = (f32[32,5,128]{2,0,1:T(8,128)S(1)}, f32[32,5,128]{2,0,1:T(8,128)}, u32[]{:S(2)}) copy-start(f32[32,5,128]{2,0,1:T(8,128)} %param.8) | copy-start | bytes 245764
  58.9 0.7 copy-start.6
  62.9 1.0 copy-start.3
  63.9 0.7 copy-start.10
  64.5 7.1 %copy-start.11 = (f32[32,8,128]{2,1,0:T(8,128)S(1)}, f32[32,8,128]{2,1,0:T(8,128)}, u32[]{:S(2)}) copy-start(f32[32,8,128]{2,1,0:T(8,128)} %copy-done.10) | copy-start | bytes 393220
  64.5 27.6 %all-to-all-start.2 = ((f32[256,8,128]{2,1,0:T(8,128)}), f32[256,8,128]{2,1,0:T(8,128)S(1)}, u32[]{:S(2)}, u32[]{:S(2)}) async-start(f32[256,8,128]{2,1,0:T(8,128)} %copy-done.3), calls=%async_computation.2 | async-start | bytes 2097152 | tf_op jit(solution)/shard_map/all_to_all | solution.py:525
  73.3 1.0 copy-start.1
  74.3 0.7 copy-start.8
  74.9 11.2 %collective-permute-start.4 = (f32[32,128]{1,0:T(8,128)S(1)}, f32[32,128]{1,0:T(8,128)S(1)}, u32[]{:S(2)}, u32[]{:S(2)}) collective-permute-start(f32[32,128]{1,0:T(8,128)S(1)} %get-tuple-element.66), channel_id=1, source_target_pairs={{0,1},{1,2},{2,3},{3,4},{4,5},{5,6},{6,7},{7,8},{8,9},{9,10},{10,1... | collective-permute-start | bytes 49160 | tf_op jit(solution)/shard_map/ppermute | solution.py:473
  78.0 8.1 %collective-permute-start.5 = (f32[32,128]{1,0:T(8,128)S(1)}, f32[32,128]{1,0:T(8,128)S(1)}, u32[]{:S(2)}, u32[]{:S(2)}) collective-permute-start(f32[32,128]{1,0:T(8,128)S(1)} %get-tuple-element.67), channel_id=1, source_target_pairs={{1,0},{2,1},{3,2},{4,3},{5,4},{6,5},{7,6},{8,7},{9,8},{10,9},{11,1... | collective-permute-start | bytes 49160 | tf_op jit(solution)/shard_map/ppermute | solution.py:473
  86.1 20.6 %collective-permute-start.6 = (f32[32,128]{1,0:T(8,128)S(1)}, f32[32,128]{1,0:T(8,128)S(1)}, u32[]{:S(2)}, u32[]{:S(2)}) collective-permute-start(f32[32,128]{1,0:T(8,128)S(1)} %get-tuple-element.68), channel_id=1, source_target_pairs={{0,16},{1,17},{2,18},{3,19},{4,20},{5,21},{6,22},{7,23},{8,24},{9,... | collective-permute-start | bytes 49160 | tf_op jit(solution)/shard_map/ppermute | solution.py:473
  90.2 16.5 %collective-permute-start.7 = (f32[32,128]{1,0:T(8,128)S(1)}, f32[32,128]{1,0:T(8,128)S(1)}, u32[]{:S(2)}, u32[]{:S(2)}) collective-permute-start(f32[32,128]{1,0:T(8,128)S(1)} %get-tuple-element.69), channel_id=1, source_target_pairs={{16,0},{17,1},{18,2},{19,3},{20,4},{21,5},{22,6},{23,7},{24,8},{25... | collective-permute-start | bytes 49160 | tf_op jit(solution)/shard_map/ppermute | solution.py:473
  92.2 1.2 %copy-start.2 = (bf16[32,128,48]{2,1,0:T(8,128)(2,1)S(1)}, bf16[32,128,48]{2,1,0:T(8,128)(2,1)}, u32[]{:S(2)}) copy-start(bf16[32,128,48]{2,1,0:T(8,128)(2,1)} %copy-done.1) | copy-start | bytes 1179652
  93.4 13.3 %copy-start.7 = (f32[4,2,40,128]{3,2,1,0:T(8,128)S(1)}, f32[4,2,40,128]{3,2,1,0:T(8,128)}, u32[]{:S(2)}) copy-start(f32[4,2,40,128]{3,2,1,0:T(8,128)} %copy-done.6) | copy-start | bytes 491524
  93.4 13.3 %copy-start.9 = (f32[32,8,128]{2,1,0:T(8,128)S(1)}, f32[32,8,128]{2,1,0:T(8,128)}, u32[]{:S(2)}) copy-start(f32[32,8,128]{2,1,0:T(8,128)} %copy-done.8) | copy-start | bytes 393220

commit v3 on v2

--- a/solution.py
+++ b/solution.py
@@ -12,7 +12,8 @@
 DEPTH = 5
 FACES = 8
 ENTRIES = ROWS * FACES
-UNROLL = 64
+UNROLL = 128
+CHUNKS = 4
 LAG = 7
 
 time_step = 0.2
@@ -119,38 +120,41 @@
             send_ref[slot] = tile + row6 * jnp.full((8, NODES), block & 31, jnp.int32).astype(f32)
         return carry
 
-    lax.fori_loop(0, ROWS, visit, 0)
-
-
-def edge_rows(value, x):
-    return [value[c, z, x : x + 1, :] for c in range(value.shape[0]) for z in range(DEPTH)]
-
-
-def table_kernel(surf_ref, near_ref, exact_ref, pot_ref=None, tail_ref=None):
+    lax.fori_loop(0, ROWS, visit, 0, unroll=4)
+
+
+def near_table(tile, near_ref, b, unit, consts):
+    scaled, half, potential = tile_parts(tile, pltpu.roll(tile, 5, 0), consts)
+    near = near_factor(scaled, half, consts)
+    turned = lax.dot_general(unit, near, (((1,), (1,)), ((), ())), preferred_element_type=f32)
+    near_ref[b] = turned.astype(bf16)
+    return potential
+
+
+def unit_matrix():
+    shape = (NODES, NODES)
+    return (lanes(shape) == sublanes(shape)).astype(bf16)
+
+
+def table_kernel(surf_ref, near_ref, pot_ref, tail_ref):
     consts = tile_constants()
-    unit = (lanes((NODES, NODES)) == sublanes((NODES, NODES))).astype(bf16)
+    unit = unit_matrix()
 
     def table(b, carry):
         tile = surf_ref[b]
-        scaled, half, potential = tile_parts(tile, pltpu.roll(tile, 5, 0), consts)
-        near = near_factor(scaled, half, consts)
-        turned = lax.dot_general(unit, near, (((1,), (1,)), ((), ())), preferred_element_type=f32)
-        near_ref[b] = turned.astype(bf16)
-        exact_ref[b] = potential
-        if pot_ref is not None:
-            pot_ref[b] = packed_potential(potential)
-            tail_ref[b] = (pltpu.roll(tile, 3, 0) * consts[2])[:4]
+        potential = near_table(tile, near_ref, b, unit, consts)
+        pot_ref[b] = packed_potential(potential)
+        tail_ref[b] = (pltpu.roll(tile, 3, 0) * consts[2])[:4]
         return carry
 
-    lax.fori_loop(0, ROWS, table, 0, unroll=4)
+    lax.fori_loop(0, ROWS, table, 0, unroll=16)
 
 
 def edge_kernel(with_stiff, *refs):
     if with_stiff:
-        last_ref, disp_ref, surf_ref, stiff_ref, *refs = refs
-        low_row, high_row, low_col, high_col, near_ref, exact_ref, pot_ref, tail_ref, masked_ref = refs
+        last_ref, disp_ref, surf_ref, stiff_ref, low_row, high_row, low_col, high_col, masked_ref = refs
     else:
-        disp_ref, surf_ref, low_row, high_row, low_col, high_col, near_ref, exact_ref = refs
+        disp_ref, low_row, high_row, low_col, high_col = refs
     shape = (ROWS, NODES)
     lane = lanes(shape)
     if with_stiff:
@@ -175,10 +179,6 @@
             high = jnp.where(lane == at, pltpu.roll(value, at + 1, 1), high)
     low_col[...] = low
     high_col[...] = high
-    if with_stiff:
-        table_kernel(surf_ref, near_ref, exact_ref, pot_ref, tail_ref)
-    else:
-        table_kernel(surf_ref, near_ref, exact_ref)
 
 
 def extended(center, above, below):
@@ -356,9 +356,18 @@
     pair_loop(split_row(row_ref), tile_of, near_ref, loc_ref, pot_ref, tail_ref, out_ref)
 
 
-def contact_last(row_ref, home_ref, first_ref, x_ref, new_ref, near_ref, loc_ref):
+def contact_last(row_ref, home_ref, first_ref, x_ref, new_ref, disp_ref, vel_ref, loc_ref, near_ref, surf_ref):
     loc_ref[...] = jnp.zeros((ROWS, 8, NODES), f32)
     row = sublanes((8, NODES))
+    for c in range(3):
+        surf_ref[:, c, :] = disp_ref[c, DEPTH - 1]
+        surf_ref[:, 3 + c, :] = vel_ref[c, DEPTH - 1]
+        if c < 2:
+            surf_ref[:, 6 + c, :] = jnp.zeros((ROWS, NODES), f32)
+    consts = tile_constants()
+    unit = unit_matrix()
+    for b in range(ROWS):
+        near_table(surf_ref[b], near_ref, b, unit, consts)
 
     def faced(e):
         vel = new_ref[e]
@@ -377,80 +386,85 @@
     pair_loop(lambda step, j: home_ref[step * UNROLL + j], facing, near_ref, loc_ref)
 
 
-def local_sum(loc_ref, exact_ref, b):
-    total = loc_ref[b]
-    total = total + pltpu.roll(total, 4, 0)
-    return (total[3:4] * exact_ref[b] - total)[:4]
-
-
-def update_kernel(
-    slot_ref, home_ref, row_ref, ret_ref, loc_ref, exact_ref, force_ref, disp_ref, vel_ref, mass_ref, old_ref, *refs
-):
-    new_disp, new_vel, send_ref, surf_ref, sum_ref, facing_tile, faced_tile = refs
+def plane_frame(c):
+    if c != 1:
+        return 0.0
+    shape = (ROWS, NODES)
+    return (lanes(shape).astype(f32) - (NODES - 1) / 2.0) * (frame_extent / NODES)
+
+
+def plane_sum(loc_ref, disp, vel, c):
+    weight = loc_ref[:, 3, :] + loc_ref[:, 7, :]
+    potential = stiff_coef * (disp + plane_frame(c)) - damp_coef * vel
+    return weight * potential - (loc_ref[:, c, :] + loc_ref[:, 4 + c, :])
+
+
+def update_kernel(slot_ref, home_ref, row_ref, ret_ref, loc_ref, force_ref, disp_ref, vel_ref, mass_ref, *refs):
+    new_disp, new_vel, send_hbm, send_ref, surf_ref, sum_ref, facing_tile, faced_tile, sems = refs
 
     def gather(b, carry):
-        acc = local_sum(loc_ref, exact_ref, b)
-        for k in range(FACES):
+        acc = ret_ref[slot_ref[b * FACES]]
+        for k in range(1, FACES):
             acc = acc + ret_ref[slot_ref[b * FACES + k]]
         sum_ref[b] = acc
         return carry
 
-    lax.fori_loop(0, ROWS, gather, 0, unroll=4)
-    for c in range(2):
-        surf_ref[:, 6 + c, :] = jnp.zeros((ROWS, NODES), f32)
-    for z in reversed(range(DEPTH)):
+    lax.fori_loop(0, ROWS, gather, 0, unroll=8)
+    last = DEPTH - 1
+    mass = time_step * mass_ref[last]
+    for c in range(3):
+        old, vel = disp_ref[c, last], vel_ref[c, last]
+        vel = vel + mass * (force_ref[c, last] + sum_ref[:, c, :] + plane_sum(loc_ref, old, vel, c))
+        new_vel[c, last] = vel
+        new_disp[c, last] = old + time_step * vel
+        surf_ref[:, c, :] = vel
+        surf_ref[:, 3 + c, :] = old
+    row = sublanes((8, NODES))
+
+    def tiles(b, carry):
+        tile = surf_ref[b]
+        facing_tile[b] = jnp.where(row < 3, tile, 0.0)
+        late = jnp.where(row < 7, pltpu.roll(tile, 4, 0), pltpu.roll(tile, 2, 0))
+        faced_tile[b] = jnp.where(row < 3, 0.0, jnp.where(row == 3, pltpu.roll(tile, 7, 0), late))
+        return carry
+
+    lax.fori_loop(0, ROWS, tiles, 0, unroll=8)
+    size = ENTRIES // CHUNKS
+    copies = []
+    for chunk in range(CHUNKS):
+
+        def scatter(i, carry, chunk=chunk):
+            for j in range(16):
+                e = chunk * size + i * 16 + j
+                at = (chunk * size) % NODES + i * 16 + j
+                r = row_ref[chunk * size // NODES, at]
+                send_ref[e] = facing_tile[home_ref[e]] + faced_tile[r]
+            return carry
+
+        lax.fori_loop(0, size // 16, scatter, 0)
+        part = pl.ds(chunk * size, size)
+        copies.append(pltpu.make_async_copy(send_ref.at[part], send_hbm.at[part], sems.at[chunk]))
+        copies[-1].start()
+    for z in range(DEPTH - 1):
         mass = time_step * mass_ref[z]
         for c in range(3):
-            force = force_ref[c, z]
-            if z == DEPTH - 1:
-                force = force + sum_ref[:, c, :]
-            vel = vel_ref[c, z] + mass * force
-            disp = disp_ref[c, z] + time_step * vel
+            vel = vel_ref[c, z] + mass * force_ref[c, z]
             new_vel[c, z] = vel
-            new_disp[c, z] = disp
-            if z == DEPTH - 1:
-                surf_ref[:, c, :] = disp
-                surf_ref[:, 3 + c, :] = vel
-    row = sublanes((8, NODES))
-
-    def tiles(b, carry):
-        tile = surf_ref[b]
-        vel = pltpu.roll(tile, 5, 0)
-        old = old_ref[b]
-        facing_tile[b] = jnp.where(row < 3, vel, 0.0)
-        late = jnp.where(row < 7, pltpu.roll(tile, 1, 0), pltpu.roll(old, 5, 0))
-        faced_tile[b] = jnp.where(row < 3, 0.0, jnp.where(row == 3, pltpu.roll(old, 2, 0), late))
-        return carry
-
-    lax.fori_loop(0, ROWS, tiles, 0, unroll=8)
-
-    def scatter(i, carry):
-        for j in range(16):
-            e = i * 16 + j
-            r = row_ref[i * 16 // NODES, i * 16 % NODES + j]
-            send_ref[e] = facing_tile[home_ref[e]] + faced_tile[r]
-        return carry
-
-    lax.fori_loop(0, ENTRIES // 16, scatter, 0)
-
-
-def final_kernel(
-    disp_ref, vel_ref, mass_ref, loc_ref, exact_ref, wide_in, node_in, row_lo, row_hi, col_lo, col_hi, *refs
-):
-    new_disp, new_vel, sum_ref = refs
-
-    def gather(b, carry):
-        sum_ref[b] = local_sum(loc_ref, exact_ref, b)
-        return carry
-
-    lax.fori_loop(0, ROWS, gather, 0, unroll=8)
+            new_disp[c, z] = disp_ref[c, z] + time_step * vel
+    for copy in copies:
+        copy.wait()
+
+
+def final_kernel(disp_ref, vel_ref, mass_ref, loc_ref, wide_in, node_in, row_lo, row_hi, col_lo, col_hi, *refs):
+    new_disp, new_vel = refs
 
     def put(c, z, force):
+        disp, vel = disp_ref[c, z], vel_ref[c, z]
         if z == DEPTH - 1:
-            force = force + sum_ref[:, c, :]
-        vel = vel_ref[c, z] + time_step * mass_ref[z] * force
+            force = force + plane_sum(loc_ref, disp, vel, c)
+        vel = vel + time_step * mass_ref[z] * force
         new_vel[c, z] = vel
-        new_disp[c, z] = disp_ref[c, z] + time_step * vel
+        new_disp[c, z] = disp + time_step * vel
 
     force_kernel(False, disp_ref, wide_in, node_in, row_lo, row_hi, col_lo, col_hi, put)
 
@@ -514,7 +528,7 @@
     tile_shape = struct(ROWS, 8, NODES)
     small_shape = struct(ROWS, 4, NODES)
     edge_shape = struct(ROWS, NODES)
-    edge_shapes = [struct(24, NODES), struct(24, NODES), edge_shape, edge_shape, near_shape, tile_shape]
+    edge_shapes = [struct(24, NODES), struct(24, NODES), edge_shape, edge_shape]
     field_shape = struct(3, DEPTH, ROWS, NODES)
     entry_shape = struct(ENTRIES, 4, NODES)
 
@@ -536,15 +550,22 @@
         )
 
     first = exchange(send)
-    low_row, high_row, low_col, high_col, near, exact, pot, tail, masked = call(
+    low_row, high_row, low_col, high_col, masked = call(
         lambda *refs: edge_kernel(True, *refs),
         "edges_first",
         [SMEM] + [VMEM] * 3,
-        [VMEM] * 9,
-        edge_shapes + [struct(ROWS, 16, NODES, dtype=bf16), small_shape, struct(DEPTH, ROWS, NODES)],
+        [VMEM] * 5,
+        edge_shapes + [struct(DEPTH, ROWS, NODES)],
     )(ends, disp, surf, stiff)
     col_lo = go(high_col, 0, 1)
     col_hi = go(low_col, 0, -1)
+    near, pot, tail = call(
+        table_kernel,
+        "tables_first",
+        [VMEM],
+        [VMEM] * 3,
+        [near_shape, struct(ROWS, 16, NODES, dtype=bf16), small_shape],
+    )(surf)
     action, reaction, low_out, high_out, rows = call(
         contact_first,
         "contact_first",
@@ -563,21 +584,27 @@
         [VMEM] * 3,
         [field_shape, struct(DEPTH - 1, 2, ROWS + 8, NODES), struct(DEPTH, ROWS, NODES)],
     )(disp, masked, row_lo, row_hi, col_lo, col_hi)
-    table = pltpu.VMEM((ROWS, 4, NODES), f32)
     tiles = pltpu.VMEM((ROWS, 8, NODES), f32)
-    disp, vel, send, surf = call(
+    disp, vel, send = call(
         update_kernel,
         "update_first",
-        [SMEM] * 3 + [VMEM] * 8,
-        [VMEM] * 4,
-        [field_shape, field_shape, struct(ENTRIES, 8, NODES), tile_shape],
-        [table, tiles, tiles],
-    )(scalars(slots), scalars(homes), scalars(rows), returned, reaction, exact, force, disp, vel, mass, surf)
+        [SMEM] * 3 + [VMEM] * 6,
+        [VMEM] * 2 + [HBM],
+        [field_shape, field_shape, pltpu.HBM((ENTRIES, 8, NODES), f32)],
+        [
+            pltpu.VMEM((ENTRIES, 8, NODES), f32),
+            tiles,
+            pltpu.VMEM((ROWS, 4, NODES), f32),
+            tiles,
+            tiles,
+            pltpu.SemaphoreType.DMA((CHUNKS,)),
+        ],
+    )(scalars(slots), scalars(homes), scalars(rows), returned, reaction, force, disp, vel, mass)
 
     news = exchange(send)
-    low_row, high_row, low_col, high_col, near, exact = call(
-        lambda *refs: edge_kernel(False, *refs), "edges_last", [VMEM] * 2, [VMEM] * 6, edge_shapes
-    )(disp, surf)
+    low_row, high_row, low_col, high_col = call(
+        lambda *refs: edge_kernel(False, *refs), "edges_last", [VMEM], [VMEM] * 4, edge_shapes
+    )(disp)
     col_lo = go(high_col, 0, 1)
     col_hi = go(low_col, 0, -1)
     low_out, high_out = call(row_messages, "rows_last", [VMEM] * 4, [VMEM] * 2, [edge_shape] * 2)(
@@ -585,11 +612,16 @@
     )
     row_lo = go(high_out, 1, 0)
     row_hi = go(low_out, -1, 0)
-    (total,) = call(contact_last, "contact_last", [SMEM] * 2 + [VMEM] * 4, [VMEM], [tile_shape])(
-        scalars(rows), scalars(homes), first, returned, news, near
-    )
-    disp, vel = call(final_kernel, "update_last", [VMEM] * 11, [VMEM] * 2, [field_shape] * 2, [table])(
-        disp, vel, mass, total, exact, wide, node, row_lo, row_hi, col_lo, col_hi
+    (total,) = call(
+        contact_last,
+        "contact_last",
+        [SMEM] * 2 + [VMEM] * 5,
+        [VMEM],
+        [tile_shape],
+        [pltpu.VMEM((ROWS, NODES, 48), bf16), tiles],
+    )(scalars(rows), scalars(homes), first, returned, news, disp, vel)
+    disp, vel = call(final_kernel, "update_last", [VMEM] * 10, [VMEM] * 2, [field_shape] * 2)(
+        disp, vel, mass, total, wide, node, row_lo, row_hi, col_lo, col_hi
     )
     return disp.transpose(0, 2, 1, 3), vel.transpose(0, 2, 1, 3)
 

time: 109 us -> 105 us (0.963)
  local copies, waits for them, and re-layouts: 5.16 us -> 0.66 us
  waiting for transfers between devices: 17.1 us -> 21 us
  Pallas kernels: 34.7 us -> 31.7 us
    unnamed x26 -> x12, local copies, waits for them, and re-layouts: 5.16 us -> 0.66 us
    ppermute x8, waiting for transfers between devices: 12.1 us -> 16.1 us  [shifted(): return lax.ppermute(value, AXES, pairs)]
    pallas_call x1, Pallas kernels: 2.25 us -> 0.77 us  [local(): call(lambda *refs: edge_kernel(True, *refs), 'edges_first', [SMEM] + [VME...]
    pallas_call x4 -> x5, Pallas kernels: 17.9 us -> 16.9 us  [the longest x1 12.6 us: local(): call(contact_last, 'contact_last', [SMEM] * 2 + [VMEM] * 5, [VMEM], [tile...]
  transfers between devices with their start and end apart: 11 -> 11, of which waited for: 5 -> 5; matrix products, arithmetic and copies ran while one was open for 0% -> 0% of each run, Pallas kernels for 16% -> 14%
where the time goes in v3:
time: 105 us
  starting transfers between devices  50.4 us (48%)
  Pallas kernels  31.7 us (30%)
  waiting for transfers between devices  21 us (20%)
    ppermute x8, starting transfers between devices, shifted(): return lax.ppermute(value, AXES, pairs)  26.7 us
    all_to_all x3, starting transfers between devices, exchange(): return lax.all_to_all(value, AXES, 0, 0, tiled=True)  23.8 us
    ppermute x8, waiting for transfers between devices, shifted(): return lax.ppermute(value, AXES, pairs)  16.1 us
    pallas_call x1, Pallas kernels, local(): call(contact_last, 'contact_last', [SMEM] * 2 + [VMEM] * 5, [VMEM], [tile...  12.6 us
    pallas_call x1, Pallas kernels, local(): call(contact_first, 'contact_first', [VMEM] * 8, [VMEM] * 4 + [SMEM], [en...  9.74 us
    all_to_all x3, waiting for transfers between devices, exchange(): return lax.all_to_all(value, AXES, 0, 0, tiled=True)  4.97 us
    pallas_call x1, Pallas kernels, local(): pl.pallas_call(request_kernel, in_specs=[HBM] * 3, out_specs=[VMEM, SMEM,...  3.73 us
  transfers between devices with their start and end apart: 11, of which 5 were waited for; matrix products, arithmetic and copies ran while one was open for 0% of the time, Pallas kernels for 14%

profile of v3, /device:TPU:7, one launch (start us, length us, event | category | flops | bytes accessed | tf_op | source)
XLA Modules:
  0.0 104.8 jit_solution(2132007783692099395)
XLA Ops:
  0.6 3.7 %request.1 = (f32[256,8,128]{2,1,0:T(8,128)}, s32[256]{0:T(256)S(4)}, s32[256]{0:T(256)S(4)}, f32[32,8,128]{2,1,0:T(8,128)S(1)}) custom-call(s32[8,32]{1,0:T(8,128)} %bitcast.20, f32[3,5,32,128]{3,2,1,0:T(8,128)} %bitcast.11, f32[3,5,32,128]{3,2,1,0:T(8,128)} %bitcast.15), custom_call_target="tpu_custom_call" | custom-call | tf_op jit(solution)/shard_map/request/pallas_call | solution.py:508
  4.4 10.8 %all-to-all-start = ((f32[256,8,128]{2,1,0:T(8,128)}), f32[256,8,128]{2,1,0:T(8,128)S(1)}, u32[]{:S(2)}, u32[]{:S(2)}) async-start(f32[256,8,128]{2,1,0:T(8,128)} %get-tuple-element.35), calls=%async_computation | async-start | bytes 2097152 | tf_op jit(solution)/shard_map/all_to_all | solution.py:539
  15.3 0.8 edges_first.1
  16.1 3.1 %collective-permute-start = (f32[32,128]{1,0:T(8,128)S(1)}, f32[32,128]{1,0:T(8,128)S(1)}, u32[]{:S(2)}, u32[]{:S(2)}) collective-permute-start(f32[32,128]{1,0:T(8,128)S(1)} %get-tuple-element.42), channel_id=1, source_target_pairs={{0,1},{1,2},{2,3},{3,4},{4,5},{5,6},{6,7},{7,8},{8,9},{9,10},{10,1... | collective-permute-start | bytes 49160 | tf_op jit(solution)/shard_map/ppermute | solution.py:487
  19.2 4.3 %collective-permute-start.1 = (f32[32,128]{1,0:T(8,128)S(1)}, f32[32,128]{1,0:T(8,128)S(1)}, u32[]{:S(2)}, u32[]{:S(2)}) collective-permute-start(f32[32,128]{1,0:T(8,128)S(1)} %get-tuple-element.43), channel_id=1, source_target_pairs={{1,0},{2,1},{3,2},{4,3},{5,4},{6,5},{7,6},{8,7},{9,8},{10,9},{11,1... | collective-permute-start | bytes 49160 | tf_op jit(solution)/shard_map/ppermute | solution.py:487
  23.5 0.6 tables_first.1
  24.1 5.6 %collective-permute-done.col_lo.refs_4_ = f32[32,128]{1,0:T(8,128)S(1)} collective-permute-done((f32[32,128]{1,0:T(8,128)S(1)}, f32[32,128]{1,0:T(8,128)S(1)}, u32[]{:S(2)}, u32[]{:S(2)}) %collective-permute-start) | collective-permute-done | bytes 16416 | tf_op jit(solution)/shard_map/ppermute | solution.py:487
  29.7 3.2 %all-to-all-done.recv_ref.first_ref = f32[256,8,128]{2,1,0:T(8,128)S(1)} async-done(((f32[256,8,128]{2,1,0:T(8,128)}), f32[256,8,128]{2,1,0:T(8,128)S(1)}, u32[]{:S(2)}, u32[]{:S(2)}) %all-to-all-start) | async-done | bytes 1048608 | tf_op jit(solution)/shard_map/all_to_all | solution.py:539
  32.9 9.7 %contact_first.1 = (f32[256,4,128]{2,1,0:T(4,128)}, f32[32,8,128]{2,1,0:T(8,128)S(1)}, f32[32,128]{1,0:T(8,128)S(1)}, f32[32,128]{1,0:T(8,128)S(1)}, s32[2,128]{1,0:T(2,128)S(4)}) custom-call(f32[256,8,128]{2,1,0:T(8,128)S(1)} %all-to-all-done.recv_ref.first_ref, bf16[32,128,48]{2,1,0:T(8,128)(2,1)S(1)} %get-tuple-element.37.near_ref, ...), custom_call_target="tpu_custom_call" | custom-call | tf_op jit(solution)/shard_map/contact_first/pallas_call | solution.py:569
  42.6 5.9 %all-to-all-start.1 = ((f32[256,4,128]{2,1,0:T(4,128)}), f32[256,4,128]{2,1,0:T(4,128)S(1)}, u32[]{:S(2)}, u32[]{:S(2)}) async-start(f32[256,4,128]{2,1,0:T(4,128)} %get-tuple-element.45), calls=%async_computation.1 | async-start | bytes 1048576 | tf_op jit(solution)/shard_map/all_to_all | solution.py:539
  48.5 3.7 %collective-permute-start.2 = (f32[32,128]{1,0:T(8,128)S(1)}, f32[32,128]{1,0:T(8,128)S(1)}, u32[]{:S(2)}, u32[]{:S(2)}) collective-permute-start(f32[32,128]{1,0:T(8,128)S(1)} %get-tuple-element.48), channel_id=1, source_target_pairs={{0,16},{1,17},{2,18},{3,19},{4,20},{5,21},{6,22},{7,23},{8,24},{9,... | collective-permute-start | bytes 49160 | tf_op jit(solution)/shard_map/ppermute | solution.py:487
  52.3 1.9 %collective-permute-start.3 = (f32[32,128]{1,0:T(8,128)S(1)}, f32[32,128]{1,0:T(8,128)S(1)}, u32[]{:S(2)}, u32[]{:S(2)}) collective-permute-start(f32[32,128]{1,0:T(8,128)S(1)} %get-tuple-element.49), channel_id=1, source_target_pairs={{16,0},{17,1},{18,2},{19,3},{20,4},{21,5},{22,6},{23,7},{24,8},{25... | collective-permute-start | bytes 49160 | tf_op jit(solution)/shard_map/ppermute | solution.py:487
  54.2 3.6 %collective-permute-done.3.refs_3_ = f32[32,128]{1,0:T(8,128)S(1)} collective-permute-done((f32[32,128]{1,0:T(8,128)S(1)}, f32[32,128]{1,0:T(8,128)S(1)}, u32[]{:S(2)}, u32[]{:S(2)}) %collective-permute-start.3) | collective-permute-done | bytes 16416 | tf_op jit(solution)/shard_map/ppermute | solution.py:487
  58.5 0.6 copy-done.4
  59.1 1.8 %all-to-all-done.1.ret_ref.x_ref = f32[256,4,128]{2,1,0:T(4,128)S(1)} async-done(((f32[256,4,128]{2,1,0:T(4,128)}), f32[256,4,128]{2,1,0:T(4,128)S(1)}, u32[]{:S(2)}, u32[]{:S(2)}) %all-to-all-start.1) | async-done | bytes 524320 | tf_op jit(solution)/shard_map/all_to_all | solution.py:539
  60.9 2.1 %update_first.1 = (f32[3,5,32,128]{3,2,1,0:T(8,128)S(1)}, f32[3,5,32,128]{3,2,1,0:T(8,128)S(1)}, f32[256,8,128]{2,1,0:T(8,128)}) custom-call(s32[256]{0:T(256)S(4)} %get-tuple-element.33.slot_ref, s32[256]{0:T(256)S(4)} %get-tuple-element.34.home_ref, s32[2,128]{1,0:T(2,128)S(4)} %get-tuple-element.44.row_ref, ...), custom_call_target="tpu_custom_call" | custom-call | tf_op jit(solution)/shard_map/update_first/pallas_call | solution.py:588
  62.9 7.1 %all-to-all-start.2 = ((f32[256,8,128]{2,1,0:T(8,128)}), f32[256,8,128]{2,1,0:T(8,128)S(1)}, u32[]{:S(2)}, u32[]{:S(2)}) async-start(f32[256,8,128]{2,1,0:T(8,128)} %get-tuple-element.53), calls=%async_computation.2 | async-start | bytes 2097152 | tf_op jit(solution)/shard_map/all_to_all | solution.py:539
  70.2 3.1 %collective-permute-start.4 = (f32[32,128]{1,0:T(8,128)S(1)}, f32[32,128]{1,0:T(8,128)S(1)}, u32[]{:S(2)}, u32[]{:S(2)}) collective-permute-start(f32[32,128]{1,0:T(8,128)S(1)} %get-tuple-element.58), channel_id=1, source_target_pairs={{0,1},{1,2},{2,3},{3,4},{4,5},{5,6},{6,7},{7,8},{8,9},{9,10},{10,1... | collective-permute-start | bytes 49160 | tf_op jit(solution)/shard_map/ppermute | solution.py:487
  73.3 4.3 %collective-permute-start.5 = (f32[32,128]{1,0:T(8,128)S(1)}, f32[32,128]{1,0:T(8,128)S(1)}, u32[]{:S(2)}, u32[]{:S(2)}) collective-permute-start(f32[32,128]{1,0:T(8,128)S(1)} %get-tuple-element.59), channel_id=1, source_target_pairs={{1,0},{2,1},{3,2},{4,3},{5,4},{6,5},{7,6},{8,7},{9,8},{10,9},{11,1... | collective-permute-start | bytes 49160 | tf_op jit(solution)/shard_map/ppermute | solution.py:487
  77.6 6.9 %collective-permute-done.4.col_lo = f32[32,128]{1,0:T(8,128)S(1)} collective-permute-done((f32[32,128]{1,0:T(8,128)S(1)}, f32[32,128]{1,0:T(8,128)S(1)}, u32[]{:S(2)}, u32[]{:S(2)}) %collective-permute-start.4) | collective-permute-done | bytes 16416 | tf_op jit(solution)/shard_map/ppermute | solution.py:487
  84.5 4.1 %collective-permute-start.6 = (f32[32,128]{1,0:T(8,128)S(1)}, f32[32,128]{1,0:T(8,128)S(1)}, u32[]{:S(2)}, u32[]{:S(2)}) collective-permute-start(f32[32,128]{1,0:T(8,128)S(1)} %get-tuple-element.60), channel_id=1, source_target_pairs={{0,16},{1,17},{2,18},{3,19},{4,20},{5,21},{6,22},{7,23},{8,24},{9,... | collective-permute-start | bytes 49160 | tf_op jit(solution)/shard_map/ppermute | solution.py:487
  88.6 2.1 %collective-permute-start.7 = (f32[32,128]{1,0:T(8,128)S(1)}, f32[32,128]{1,0:T(8,128)S(1)}, u32[]{:S(2)}, u32[]{:S(2)}) collective-permute-start(f32[32,128]{1,0:T(8,128)S(1)} %get-tuple-element.61), channel_id=1, source_target_pairs={{16,0},{17,1},{18,2},{19,3},{20,4},{21,5},{22,6},{23,7},{24,8},{25... | collective-permute-start | bytes 49160 | tf_op jit(solution)/shard_map/ppermute | solution.py:487
  90.8 12.6 %contact_last.1.loc_ref = f32[32,8,128]{2,1,0:T(8,128)S(1)} custom-call(s32[2,128]{1,0:T(2,128)S(4)} %get-tuple-element.44.row_ref, s32[256]{0:T(256)S(4)} %get-tuple-element.34.home_ref, f32[256,8,128]{2,1,0:T(8,128)S(1)} %all-to-all-done.recv_ref.first_ref, f32[256,4,128]{2,1,0:T(4,128)S(1)} %all-to-all-done.1.ret_ref.x_ref, ...), custom_call_target="tpu_custom_call" | custom-call | tf_op jit(solution)/shard_map/contact_last/pallas_call | solution.py:615
  103.4 1.3 %update_last.1 = (f32[3,5,32,128]{3,2,1,0:T(8,128)}, f32[3,5,32,128]{3,2,1,0:T(8,128)}) custom-call(f32[3,5,32,128]{3,2,1,0:T(8,128)S(1)} %get-tuple-element.51.disp_ref.refs_0_, f32[3,5,32,128]{3,2,1,0:T(8,128)S(1)} %get-tuple-element.52.vel_ref, f32[5,32,128]{2,1,0:T(8,128)S(1)} %bitcast.18, f32[32,8,128]{2,1,0:T(8,128)S(1)} %contact_last.1.loc_ref, ...), custom_call_target="tpu_custom_call" | custom-call | tf_op jit(solution)/shard_map/update_last/pallas_call | solution.py:623
  (21 shorter events, 0.9 us)
Async XLA Ops:
  4.4 10.9 %copy-start = (f32[3,32,5,128]{3,1,2,0:T(8,128)S(1)}, f32[3,32,5,128]{3,1,2,0:T(8,128)}, u32[]{:S(2)}) copy-start(f32[3,32,5,128]{3,1,2,0:T(8,128)} %param.5) | copy-start | bytes 737284
  4.4 10.9 %copy-start.3 = (f32[32,5,128]{2,0,1:T(8,128)S(1)}, f32[32,5,128]{2,0,1:T(8,128)}, u32[]{:S(2)}) copy-start(f32[32,5,128]{2,0,1:T(8,128)} %param.7) | copy-start | bytes 245764
  4.4 28.5 %all-to-all-start = ((f32[256,8,128]{2,1,0:T(8,128)}), f32[256,8,128]{2,1,0:T(8,128)S(1)}, u32[]{:S(2)}, u32[]{:S(2)}) async-start(f32[256,8,128]{2,1,0:T(8,128)} %get-tuple-element.35), calls=%async_computation | async-start | bytes 2097152 | tf_op jit(solution)/shard_map/all_to_all | solution.py:539
  16.1 13.6 %collective-permute-start = (f32[32,128]{1,0:T(8,128)S(1)}, f32[32,128]{1,0:T(8,128)S(1)}, u32[]{:S(2)}, u32[]{:S(2)}) collective-permute-start(f32[32,128]{1,0:T(8,128)S(1)} %get-tuple-element.42), channel_id=1, source_target_pairs={{0,1},{1,2},{2,3},{3,4},{4,5},{5,6},{6,7},{7,8},{8,9},{9,10},{10,1... | collective-permute-start | bytes 49160 | tf_op jit(solution)/shard_map/ppermute | solution.py:487
  19.2 10.5 %collective-permute-start.1 = (f32[32,128]{1,0:T(8,128)S(1)}, f32[32,128]{1,0:T(8,128)S(1)}, u32[]{:S(2)}, u32[]{:S(2)}) collective-permute-start(f32[32,128]{1,0:T(8,128)S(1)} %get-tuple-element.43), channel_id=1, source_target_pairs={{1,0},{2,1},{3,2},{4,3},{5,4},{6,5},{7,6},{8,7},{9,8},{10,9},{11,1... | collective-permute-start | bytes 49160 | tf_op jit(solution)/shard_map/ppermute | solution.py:487
  42.6 18.2 %all-to-all-start.1 = ((f32[256,4,128]{2,1,0:T(4,128)}), f32[256,4,128]{2,1,0:T(4,128)S(1)}, u32[]{:S(2)}, u32[]{:S(2)}) async-start(f32[256,4,128]{2,1,0:T(4,128)} %get-tuple-element.45), calls=%async_computation.1 | async-start | bytes 1048576 | tf_op jit(solution)/shard_map/all_to_all | solution.py:539
  48.5 12.3 %copy-start.1 = (f32[3,32,5,128]{3,1,2,0:T(8,128)S(1)}, f32[3,32,5,128]{3,1,2,0:T(8,128)}, u32[]{:S(2)}) copy-start(f32[3,32,5,128]{3,1,2,0:T(8,128)} %param.6) | copy-start | bytes 737284
  48.5 5.7 %collective-permute-start.2 = (f32[32,128]{1,0:T(8,128)S(1)}, f32[32,128]{1,0:T(8,128)S(1)}, u32[]{:S(2)}, u32[]{:S(2)}) collective-permute-start(f32[32,128]{1,0:T(8,128)S(1)} %get-tuple-element.48), channel_id=1, source_target_pairs={{0,16},{1,17},{2,18},{3,19},{4,20},{5,21},{6,22},{7,23},{8,24},{9,... | collective-permute-start | bytes 49160 | tf_op jit(solution)/shard_map/ppermute | solution.py:487
  52.3 5.6 %collective-permute-start.3 = (f32[32,128]{1,0:T(8,128)S(1)}, f32[32,128]{1,0:T(8,128)S(1)}, u32[]{:S(2)}, u32[]{:S(2)}) collective-permute-start(f32[32,128]{1,0:T(8,128)S(1)} %get-tuple-element.49), channel_id=1, source_target_pairs={{16,0},{17,1},{18,2},{19,3},{20,4},{21,5},{22,6},{23,7},{24,8},{25... | collective-permute-start | bytes 49160 | tf_op jit(solution)/shard_map/ppermute | solution.py:487
  57.8 3.0 %copy-start.2 = (f32[32,5,128]{2,0,1:T(8,128)S(1)}, f32[32,5,128]{2,0,1:T(8,128)}, u32[]{:S(2)}) copy-start(f32[32,5,128]{2,0,1:T(8,128)} %param.8) | copy-start | bytes 245764
  58.5 0.6 copy-start.4
  62.9 27.8 %all-to-all-start.2 = ((f32[256,8,128]{2,1,0:T(8,128)}), f32[256,8,128]{2,1,0:T(8,128)S(1)}, u32[]{:S(2)}, u32[]{:S(2)}) async-start(f32[256,8,128]{2,1,0:T(8,128)} %get-tuple-element.53), calls=%async_computation.2 | async-start | bytes 2097152 | tf_op jit(solution)/shard_map/all_to_all | solution.py:539
  70.2 14.3 %collective-permute-start.4 = (f32[32,128]{1,0:T(8,128)S(1)}, f32[32,128]{1,0:T(8,128)S(1)}, u32[]{:S(2)}, u32[]{:S(2)}) collective-permute-start(f32[32,128]{1,0:T(8,128)S(1)} %get-tuple-element.58), channel_id=1, source_target_pairs={{0,1},{1,2},{2,3},{3,4},{4,5},{5,6},{6,7},{7,8},{8,9},{9,10},{10,1... | collective-permute-start | bytes 49160 | tf_op jit(solution)/shard_map/ppermute | solution.py:487
  73.3 11.2 %collective-permute-start.5 = (f32[32,128]{1,0:T(8,128)S(1)}, f32[32,128]{1,0:T(8,128)S(1)}, u32[]{:S(2)}, u32[]{:S(2)}) collective-permute-start(f32[32,128]{1,0:T(8,128)S(1)} %get-tuple-element.59), channel_id=1, source_target_pairs={{1,0},{2,1},{3,2},{4,3},{5,4},{6,5},{7,6},{8,7},{9,8},{10,9},{11,1... | collective-permute-start | bytes 49160 | tf_op jit(solution)/shard_map/ppermute | solution.py:487
  84.5 18.9 %collective-permute-start.6 = (f32[32,128]{1,0:T(8,128)S(1)}, f32[32,128]{1,0:T(8,128)S(1)}, u32[]{:S(2)}, u32[]{:S(2)}) collective-permute-start(f32[32,128]{1,0:T(8,128)S(1)} %get-tuple-element.60), channel_id=1, source_target_pairs={{0,16},{1,17},{2,18},{3,19},{4,20},{5,21},{6,22},{7,23},{8,24},{9,... | collective-permute-start | bytes 49160 | tf_op jit(solution)/shard_map/ppermute | solution.py:487
  88.6 14.8 %collective-permute-start.7 = (f32[32,128]{1,0:T(8,128)S(1)}, f32[32,128]{1,0:T(8,128)S(1)}, u32[]{:S(2)}, u32[]{:S(2)}) collective-permute-start(f32[32,128]{1,0:T(8,128)S(1)} %get-tuple-element.61), channel_id=1, source_target_pairs={{16,0},{17,1},{18,2},{19,3},{20,4},{21,5},{22,6},{23,7},{24,8},{25... | collective-permute-start | bytes 49160 | tf_op jit(solution)/shard_map/ppermute | solution.py:487
  90.7 12.7 %copy-start.5 = (f32[5,32,128]{2,1,0:T(8,128)S(1)}, f32[5,32,128]{2,1,0:T(8,128)}, u32[]{:S(2)}) copy-start(f32[5,32,128]{2,1,0:T(8,128)} %copy-done.4) | copy-start | bytes 245764

commit v4 on v3

--- a/solution.py
+++ b/solution.py
@@ -12,7 +12,8 @@
 DEPTH = 5
 FACES = 8
 ENTRIES = ROWS * FACES
-UNROLL = 128
+FIRST_UNROLL = 256
+LAST_UNROLL = 128
 CHUNKS = 4
 LAG = 7
 
@@ -277,12 +278,12 @@
         side[26:] = jnp.zeros((ROWS - 26, NODES), f32)
 
 
-def pair_loop(row_of, tile_of, near_ref, loc_ref, pot_ref=None, tail_ref=None, out_ref=None):
+def pair_loop(unroll, row_of, tile_of, near_ref, loc_ref, pot_ref=None, tail_ref=None, out_ref=None):
     consts = tile_constants()
 
     def visit(step, carry):
-        entries = [step * UNROLL + j for j in range(UNROLL)]
-        row = [row_of(step, j) for j in range(UNROLL)]
+        entries = [step * unroll + j for j in range(unroll)]
+        row = [row_of(step, j) for j in range(unroll)]
         held = {}
 
         def weigh(j):
@@ -319,21 +320,23 @@
                 out_ref[entries[j]] = (pulled[3:4] * potential - pulled)[:4] + tail_ref[row[j]]
             loc_ref[row[j]] += pushed[:8] + pushed[8:]
 
-        for t in range(UNROLL + LAG + 1):
-            if t < UNROLL:
+        for t in range(unroll + LAG + 1):
+            if t < unroll:
                 weigh(t)
-            if 0 <= t - LAG < UNROLL:
+            if 0 <= t - LAG < unroll:
                 reduce(t - LAG)
-            if 0 <= t - LAG - 1 < UNROLL:
+            if 0 <= t - LAG - 1 < unroll:
                 store(t - LAG - 1)
         return carry
 
-    lax.fori_loop(0, ENTRIES // UNROLL, visit, 0)
-
-
-def split_row(row_ref):
+    lax.fori_loop(0, ENTRIES // unroll, visit, 0)
+
+
+def split_row(unroll, row_ref):
     def row_of(step, j):
-        first = step * UNROLL
+        if unroll >= NODES:
+            return row_ref[step * (unroll // NODES) + j // NODES, j % NODES]
+        first = step * unroll
         return row_ref[first // NODES, first % NODES + j]
 
     return row_of
@@ -353,7 +356,7 @@
         tile = recv_ref[e]
         return tile, pltpu.roll(tile, 5, 0)
 
-    pair_loop(split_row(row_ref), tile_of, near_ref, loc_ref, pot_ref, tail_ref, out_ref)
+    pair_loop(FIRST_UNROLL, split_row(FIRST_UNROLL, row_ref), tile_of, near_ref, loc_ref, pot_ref, tail_ref, out_ref)
 
 
 def contact_last(row_ref, home_ref, first_ref, x_ref, new_ref, disp_ref, vel_ref, loc_ref, near_ref, surf_ref):
@@ -382,8 +385,8 @@
         disp = jnp.where(row == 0, x, jnp.where(row == 1, y, z))
         return disp + time_step * vel, vel
 
-    pair_loop(split_row(row_ref), faced, near_ref, loc_ref)
-    pair_loop(lambda step, j: home_ref[step * UNROLL + j], facing, near_ref, loc_ref)
+    pair_loop(LAST_UNROLL, split_row(LAST_UNROLL, row_ref), faced, near_ref, loc_ref)
+    pair_loop(LAST_UNROLL, lambda step, j: home_ref[step * LAST_UNROLL + j], facing, near_ref, loc_ref)
 
 
 def plane_frame(c):

time: 105 us -> 105 us (level)
  no operation moved by 1% of the time
where the time goes in v4:
time: 105 us; the launch traced here: 104 us
  starting transfers between devices  50.3 us (48%)
  Pallas kernels  31.4 us (30%)
  waiting for transfers between devices  21 us (20%)
    ppermute x8, starting transfers between devices, shifted(): return lax.ppermute(value, AXES, pairs)  26.5 us
    all_to_all x3, starting transfers between devices, exchange(): return lax.all_to_all(value, AXES, 0, 0, tiled=True)  23.8 us
    ppermute x8, waiting for transfers between devices, shifted(): return lax.ppermute(value, AXES, pairs)  16.1 us
    pallas_call x1, Pallas kernels, local(): call(contact_last, 'contact_last', [SMEM] * 2 + [VMEM] * 5, [VMEM], [tile...  12.6 us
    pallas_call x1, Pallas kernels, local(): call(contact_first, 'contact_first', [VMEM] * 8, [VMEM] * 4 + [SMEM], [en...  9.44 us
    all_to_all x3, waiting for transfers between devices, exchange(): return lax.all_to_all(value, AXES, 0, 0, tiled=True)  4.97 us
    pallas_call x1, Pallas kernels, local(): pl.pallas_call(request_kernel, in_specs=[HBM] * 3, out_specs=[VMEM, SMEM,...  3.73 us
  transfers between devices with their start and end apart: 11, of which 5 were waited for; matrix products, arithmetic and copies ran while one was open for 0% of the time, Pallas kernels for 14%

profile of v4, /device:TPU:7, one launch (start us, length us, event | category | flops | bytes accessed | tf_op | source)
XLA Modules:
  0.0 104.3 jit_solution(3918476028626937649)
XLA Ops:
  0.6 3.7 %request.1 = (f32[256,8,128]{2,1,0:T(8,128)}, s32[256]{0:T(256)S(4)}, s32[256]{0:T(256)S(4)}, f32[32,8,128]{2,1,0:T(8,128)S(1)}) custom-call(s32[8,32]{1,0:T(8,128)} %bitcast.20, f32[3,5,32,128]{3,2,1,0:T(8,128)} %bitcast.11, f32[3,5,32,128]{3,2,1,0:T(8,128)} %bitcast.15), custom_call_target="tpu_custom_call" | custom-call | tf_op jit(solution)/shard_map/request/pallas_call | solution.py:511
  4.4 10.8 %all-to-all-start = ((f32[256,8,128]{2,1,0:T(8,128)}), f32[256,8,128]{2,1,0:T(8,128)S(1)}, u32[]{:S(2)}, u32[]{:S(2)}) async-start(f32[256,8,128]{2,1,0:T(8,128)} %get-tuple-element.35), calls=%async_computation | async-start | bytes 2097152 | tf_op jit(solution)/shard_map/all_to_all | solution.py:542
  15.3 0.8 edges_first.1
  16.1 3.1 %collective-permute-start = (f32[32,128]{1,0:T(8,128)S(1)}, f32[32,128]{1,0:T(8,128)S(1)}, u32[]{:S(2)}, u32[]{:S(2)}) collective-permute-start(f32[32,128]{1,0:T(8,128)S(1)} %get-tuple-element.42), channel_id=1, source_target_pairs={{0,1},{1,2},{2,3},{3,4},{4,5},{5,6},{6,7},{7,8},{8,9},{9,10},{10,1... | collective-permute-start | bytes 49160 | tf_op jit(solution)/shard_map/ppermute | solution.py:490
  19.2 4.3 %collective-permute-start.1 = (f32[32,128]{1,0:T(8,128)S(1)}, f32[32,128]{1,0:T(8,128)S(1)}, u32[]{:S(2)}, u32[]{:S(2)}) collective-permute-start(f32[32,128]{1,0:T(8,128)S(1)} %get-tuple-element.43), channel_id=1, source_target_pairs={{1,0},{2,1},{3,2},{4,3},{5,4},{6,5},{7,6},{8,7},{9,8},{10,9},{11,1... | collective-permute-start | bytes 49160 | tf_op jit(solution)/shard_map/ppermute | solution.py:490
  23.5 0.6 tables_first.1
  24.1 5.6 %collective-permute-done.col_lo.refs_4_ = f32[32,128]{1,0:T(8,128)S(1)} collective-permute-done((f32[32,128]{1,0:T(8,128)S(1)}, f32[32,128]{1,0:T(8,128)S(1)}, u32[]{:S(2)}, u32[]{:S(2)}) %collective-permute-start) | collective-permute-done | bytes 16416 | tf_op jit(solution)/shard_map/ppermute | solution.py:490
  29.7 3.2 %all-to-all-done.recv_ref.first_ref = f32[256,8,128]{2,1,0:T(8,128)S(1)} async-done(((f32[256,8,128]{2,1,0:T(8,128)}), f32[256,8,128]{2,1,0:T(8,128)S(1)}, u32[]{:S(2)}, u32[]{:S(2)}) %all-to-all-start) | async-done | bytes 1048608 | tf_op jit(solution)/shard_map/all_to_all | solution.py:542
  32.9 9.4 %contact_first.1 = (f32[256,4,128]{2,1,0:T(4,128)}, f32[32,8,128]{2,1,0:T(8,128)S(1)}, f32[32,128]{1,0:T(8,128)S(1)}, f32[32,128]{1,0:T(8,128)S(1)}, s32[2,128]{1,0:T(2,128)S(4)}) custom-call(f32[256,8,128]{2,1,0:T(8,128)S(1)} %all-to-all-done.recv_ref.first_ref, bf16[32,128,48]{2,1,0:T(8,128)(2,1)S(1)} %get-tuple-element.37.near_ref, ...), custom_call_target="tpu_custom_call" | custom-call | tf_op jit(solution)/shard_map/contact_first/pallas_call | solution.py:572
  42.3 5.9 %all-to-all-start.1 = ((f32[256,4,128]{2,1,0:T(4,128)}), f32[256,4,128]{2,1,0:T(4,128)S(1)}, u32[]{:S(2)}, u32[]{:S(2)}) async-start(f32[256,4,128]{2,1,0:T(4,128)} %get-tuple-element.45), calls=%async_computation.1 | async-start | bytes 1048576 | tf_op jit(solution)/shard_map/all_to_all | solution.py:542
  48.2 3.7 %collective-permute-start.2 = (f32[32,128]{1,0:T(8,128)S(1)}, f32[32,128]{1,0:T(8,128)S(1)}, u32[]{:S(2)}, u32[]{:S(2)}) collective-permute-start(f32[32,128]{1,0:T(8,128)S(1)} %get-tuple-element.48), channel_id=1, source_target_pairs={{0,16},{1,17},{2,18},{3,19},{4,20},{5,21},{6,22},{7,23},{8,24},{9,... | collective-permute-start | bytes 49160 | tf_op jit(solution)/shard_map/ppermute | solution.py:490
  52.0 1.9 %collective-permute-start.3 = (f32[32,128]{1,0:T(8,128)S(1)}, f32[32,128]{1,0:T(8,128)S(1)}, u32[]{:S(2)}, u32[]{:S(2)}) collective-permute-start(f32[32,128]{1,0:T(8,128)S(1)} %get-tuple-element.49), channel_id=1, source_target_pairs={{16,0},{17,1},{18,2},{19,3},{20,4},{21,5},{22,6},{23,7},{24,8},{25... | collective-permute-start | bytes 49160 | tf_op jit(solution)/shard_map/ppermute | solution.py:490
  53.9 3.6 %collective-permute-done.3.refs_3_ = f32[32,128]{1,0:T(8,128)S(1)} collective-permute-done((f32[32,128]{1,0:T(8,128)S(1)}, f32[32,128]{1,0:T(8,128)S(1)}, u32[]{:S(2)}, u32[]{:S(2)}) %collective-permute-start.3) | collective-permute-done | bytes 16416 | tf_op jit(solution)/shard_map/ppermute | solution.py:490
  58.2 0.6 copy-done.4
  58.8 1.8 %all-to-all-done.1.ret_ref.x_ref = f32[256,4,128]{2,1,0:T(4,128)S(1)} async-done(((f32[256,4,128]{2,1,0:T(4,128)}), f32[256,4,128]{2,1,0:T(4,128)S(1)}, u32[]{:S(2)}, u32[]{:S(2)}) %all-to-all-start.1) | async-done | bytes 524320 | tf_op jit(solution)/shard_map/all_to_all | solution.py:542
  60.6 2.1 %update_first.1 = (f32[3,5,32,128]{3,2,1,0:T(8,128)S(1)}, f32[3,5,32,128]{3,2,1,0:T(8,128)S(1)}, f32[256,8,128]{2,1,0:T(8,128)}) custom-call(s32[256]{0:T(256)S(4)} %get-tuple-element.33.slot_ref, s32[256]{0:T(256)S(4)} %get-tuple-element.34.home_ref, s32[2,128]{1,0:T(2,128)S(4)} %get-tuple-element.44.row_ref, ...), custom_call_target="tpu_custom_call" | custom-call | tf_op jit(solution)/shard_map/update_first/pallas_call | solution.py:591
  62.6 7.1 %all-to-all-start.2 = ((f32[256,8,128]{2,1,0:T(8,128)}), f32[256,8,128]{2,1,0:T(8,128)S(1)}, u32[]{:S(2)}, u32[]{:S(2)}) async-start(f32[256,8,128]{2,1,0:T(8,128)} %get-tuple-element.53), calls=%async_computation.2 | async-start | bytes 2097152 | tf_op jit(solution)/shard_map/all_to_all | solution.py:542
  69.9 3.1 %collective-permute-start.4 = (f32[32,128]{1,0:T(8,128)S(1)}, f32[32,128]{1,0:T(8,128)S(1)}, u32[]{:S(2)}, u32[]{:S(2)}) collective-permute-start(f32[32,128]{1,0:T(8,128)S(1)} %get-tuple-element.58), channel_id=1, source_target_pairs={{0,1},{1,2},{2,3},{3,4},{4,5},{5,6},{6,7},{7,8},{8,9},{9,10},{10,1... | collective-permute-start | bytes 49160 | tf_op jit(solution)/shard_map/ppermute | solution.py:490
  73.0 4.3 %collective-permute-start.5 = (f32[32,128]{1,0:T(8,128)S(1)}, f32[32,128]{1,0:T(8,128)S(1)}, u32[]{:S(2)}, u32[]{:S(2)}) collective-permute-start(f32[32,128]{1,0:T(8,128)S(1)} %get-tuple-element.59), channel_id=1, source_target_pairs={{1,0},{2,1},{3,2},{4,3},{5,4},{6,5},{7,6},{8,7},{9,8},{10,9},{11,1... | collective-permute-start | bytes 49160 | tf_op jit(solution)/shard_map/ppermute | solution.py:490
  77.3 6.9 %collective-permute-done.4.col_lo = f32[32,128]{1,0:T(8,128)S(1)} collective-permute-done((f32[32,128]{1,0:T(8,128)S(1)}, f32[32,128]{1,0:T(8,128)S(1)}, u32[]{:S(2)}, u32[]{:S(2)}) %collective-permute-start.4) | collective-permute-done | bytes 16416 | tf_op jit(solution)/shard_map/ppermute | solution.py:490
  84.2 4.1 %collective-permute-start.6 = (f32[32,128]{1,0:T(8,128)S(1)}, f32[32,128]{1,0:T(8,128)S(1)}, u32[]{:S(2)}, u32[]{:S(2)}) collective-permute-start(f32[32,128]{1,0:T(8,128)S(1)} %get-tuple-element.60), channel_id=1, source_target_pairs={{0,16},{1,17},{2,18},{3,19},{4,20},{5,21},{6,22},{7,23},{8,24},{9,... | collective-permute-start | bytes 49160 | tf_op jit(solution)/shard_map/ppermute | solution.py:490
  88.3 1.9 %collective-permute-start.7 = (f32[32,128]{1,0:T(8,128)S(1)}, f32[32,128]{1,0:T(8,128)S(1)}, u32[]{:S(2)}, u32[]{:S(2)}) collective-permute-start(f32[32,128]{1,0:T(8,128)S(1)} %get-tuple-element.61), channel_id=1, source_target_pairs={{16,0},{17,1},{18,2},{19,3},{20,4},{21,5},{22,6},{23,7},{24,8},{25... | collective-permute-start | bytes 49160 | tf_op jit(solution)/shard_map/ppermute | solution.py:490
  90.3 12.6 %contact_last.1.loc_ref = f32[32,8,128]{2,1,0:T(8,128)S(1)} custom-call(s32[2,128]{1,0:T(2,128)S(4)} %get-tuple-element.44.row_ref, s32[256]{0:T(256)S(4)} %get-tuple-element.34.home_ref, f32[256,8,128]{2,1,0:T(8,128)S(1)} %all-to-all-done.recv_ref.first_ref, f32[256,4,128]{2,1,0:T(4,128)S(1)} %all-to-all-done.1.ret_ref.x_ref, ...), custom_call_target="tpu_custom_call" | custom-call | tf_op jit(solution)/shard_map/contact_last/pallas_call | solution.py:618
  103.0 1.3 %update_last.1 = (f32[3,5,32,128]{3,2,1,0:T(8,128)}, f32[3,5,32,128]{3,2,1,0:T(8,128)}) custom-call(f32[3,5,32,128]{3,2,1,0:T(8,128)S(1)} %get-tuple-element.51.disp_ref.refs_0_, f32[3,5,32,128]{3,2,1,0:T(8,128)S(1)} %get-tuple-element.52.vel_ref, f32[5,32,128]{2,1,0:T(8,128)S(1)} %bitcast.18, f32[32,8,128]{2,1,0:T(8,128)S(1)} %contact_last.1.loc_ref, ...), custom_call_target="tpu_custom_call" | custom-call | tf_op jit(solution)/shard_map/update_last/pallas_call | solution.py:626
  (21 shorter events, 0.9 us)
Async XLA Ops:
  4.4 10.9 %copy-start = (f32[3,32,5,128]{3,1,2,0:T(8,128)S(1)}, f32[3,32,5,128]{3,1,2,0:T(8,128)}, u32[]{:S(2)}) copy-start(f32[3,32,5,128]{3,1,2,0:T(8,128)} %param.5) | copy-start | bytes 737284
  4.4 10.9 %copy-start.3 = (f32[32,5,128]{2,0,1:T(8,128)S(1)}, f32[32,5,128]{2,0,1:T(8,128)}, u32[]{:S(2)}) copy-start(f32[32,5,128]{2,0,1:T(8,128)} %param.7) | copy-start | bytes 245764
  4.4 28.5 %all-to-all-start = ((f32[256,8,128]{2,1,0:T(8,128)}), f32[256,8,128]{2,1,0:T(8,128)S(1)}, u32[]{:S(2)}, u32[]{:S(2)}) async-start(f32[256,8,128]{2,1,0:T(8,128)} %get-tuple-element.35), calls=%async_computation | async-start | bytes 2097152 | tf_op jit(solution)/shard_map/all_to_all | solution.py:542
  16.1 13.6 %collective-permute-start = (f32[32,128]{1,0:T(8,128)S(1)}, f32[32,128]{1,0:T(8,128)S(1)}, u32[]{:S(2)}, u32[]{:S(2)}) collective-permute-start(f32[32,128]{1,0:T(8,128)S(1)} %get-tuple-element.42), channel_id=1, source_target_pairs={{0,1},{1,2},{2,3},{3,4},{4,5},{5,6},{6,7},{7,8},{8,9},{9,10},{10,1... | collective-permute-start | bytes 49160 | tf_op jit(solution)/shard_map/ppermute | solution.py:490
  19.2 10.5 %collective-permute-start.1 = (f32[32,128]{1,0:T(8,128)S(1)}, f32[32,128]{1,0:T(8,128)S(1)}, u32[]{:S(2)}, u32[]{:S(2)}) collective-permute-start(f32[32,128]{1,0:T(8,128)S(1)} %get-tuple-element.43), channel_id=1, source_target_pairs={{1,0},{2,1},{3,2},{4,3},{5,4},{6,5},{7,6},{8,7},{9,8},{10,9},{11,1... | collective-permute-start | bytes 49160 | tf_op jit(solution)/shard_map/ppermute | solution.py:490
  42.3 18.2 %all-to-all-start.1 = ((f32[256,4,128]{2,1,0:T(4,128)}), f32[256,4,128]{2,1,0:T(4,128)S(1)}, u32[]{:S(2)}, u32[]{:S(2)}) async-start(f32[256,4,128]{2,1,0:T(4,128)} %get-tuple-element.45), calls=%async_computation.1 | async-start | bytes 1048576 | tf_op jit(solution)/shard_map/all_to_all | solution.py:542
  48.2 12.3 %copy-start.1 = (f32[3,32,5,128]{3,1,2,0:T(8,128)S(1)}, f32[3,32,5,128]{3,1,2,0:T(8,128)}, u32[]{:S(2)}) copy-start(f32[3,32,5,128]{3,1,2,0:T(8,128)} %param.6) | copy-start | bytes 737284
  48.2 5.7 %collective-permute-start.2 = (f32[32,128]{1,0:T(8,128)S(1)}, f32[32,128]{1,0:T(8,128)S(1)}, u32[]{:S(2)}, u32[]{:S(2)}) collective-permute-start(f32[32,128]{1,0:T(8,128)S(1)} %get-tuple-element.48), channel_id=1, source_target_pairs={{0,16},{1,17},{2,18},{3,19},{4,20},{5,21},{6,22},{7,23},{8,24},{9,... | collective-permute-start | bytes 49160 | tf_op jit(solution)/shard_map/ppermute | solution.py:490
  52.0 5.6 %collective-permute-start.3 = (f32[32,128]{1,0:T(8,128)S(1)}, f32[32,128]{1,0:T(8,128)S(1)}, u32[]{:S(2)}, u32[]{:S(2)}) collective-permute-start(f32[32,128]{1,0:T(8,128)S(1)} %get-tuple-element.49), channel_id=1, source_target_pairs={{16,0},{17,1},{18,2},{19,3},{20,4},{21,5},{22,6},{23,7},{24,8},{25... | collective-permute-start | bytes 49160 | tf_op jit(solution)/shard_map/ppermute | solution.py:490
  57.5 3.0 %copy-start.2 = (f32[32,5,128]{2,0,1:T(8,128)S(1)}, f32[32,5,128]{2,0,1:T(8,128)}, u32[]{:S(2)}) copy-start(f32[32,5,128]{2,0,1:T(8,128)} %param.8) | copy-start | bytes 245764
  58.2 0.6 copy-start.4
  62.6 27.6 %all-to-all-start.2 = ((f32[256,8,128]{2,1,0:T(8,128)}), f32[256,8,128]{2,1,0:T(8,128)S(1)}, u32[]{:S(2)}, u32[]{:S(2)}) async-start(f32[256,8,128]{2,1,0:T(8,128)} %get-tuple-element.53), calls=%async_computation.2 | async-start | bytes 2097152 | tf_op jit(solution)/shard_map/all_to_all | solution.py:542
  69.9 14.3 %collective-permute-start.4 = (f32[32,128]{1,0:T(8,128)S(1)}, f32[32,128]{1,0:T(8,128)S(1)}, u32[]{:S(2)}, u32[]{:S(2)}) collective-permute-start(f32[32,128]{1,0:T(8,128)S(1)} %get-tuple-element.58), channel_id=1, source_target_pairs={{0,1},{1,2},{2,3},{3,4},{4,5},{5,6},{6,7},{7,8},{8,9},{9,10},{10,1... | collective-permute-start | bytes 49160 | tf_op jit(solution)/shard_map/ppermute | solution.py:490
  73.0 11.2 %collective-permute-start.5 = (f32[32,128]{1,0:T(8,128)S(1)}, f32[32,128]{1,0:T(8,128)S(1)}, u32[]{:S(2)}, u32[]{:S(2)}) collective-permute-start(f32[32,128]{1,0:T(8,128)S(1)} %get-tuple-element.59), channel_id=1, source_target_pairs={{1,0},{2,1},{3,2},{4,3},{5,4},{6,5},{7,6},{8,7},{9,8},{10,9},{11,1... | collective-permute-start | bytes 49160 | tf_op jit(solution)/shard_map/ppermute | solution.py:490
  84.2 18.7 %collective-permute-start.6 = (f32[32,128]{1,0:T(8,128)S(1)}, f32[32,128]{1,0:T(8,128)S(1)}, u32[]{:S(2)}, u32[]{:S(2)}) collective-permute-start(f32[32,128]{1,0:T(8,128)S(1)} %get-tuple-element.60), channel_id=1, source_target_pairs={{0,16},{1,17},{2,18},{3,19},{4,20},{5,21},{6,22},{7,23},{8,24},{9,... | collective-permute-start | bytes 49160 | tf_op jit(solution)/shard_map/ppermute | solution.py:490
  88.3 14.6 %collective-permute-start.7 = (f32[32,128]{1,0:T(8,128)S(1)}, f32[32,128]{1,0:T(8,128)S(1)}, u32[]{:S(2)}, u32[]{:S(2)}) collective-permute-start(f32[32,128]{1,0:T(8,128)S(1)} %get-tuple-element.61), channel_id=1, source_target_pairs={{16,0},{17,1},{18,2},{19,3},{20,4},{21,5},{22,6},{23,7},{24,8},{25... | collective-permute-start | bytes 49160 | tf_op jit(solution)/shard_map/ppermute | solution.py:490
  90.3 12.7 %copy-start.5 = (f32[5,32,128]{2,1,0:T(8,128)S(1)}, f32[5,32,128]{2,1,0:T(8,128)}, u32[]{:S(2)}) copy-start(f32[5,32,128]{2,1,0:T(8,128)} %copy-done.4) | copy-start | bytes 245764

commit v5 on v4

--- a/solution.py
+++ b/solution.py
@@ -278,7 +278,7 @@
         side[26:] = jnp.zeros((ROWS - 26, NODES), f32)
 
 
-def pair_loop(unroll, row_of, tile_of, near_ref, loc_ref, pot_ref=None, tail_ref=None, out_ref=None):
+def pair_loop(steps, unroll, row_of, tile_of, near_ref, loc_ref, pot_ref=None, tail_ref=None, out_ref=None):
     consts = tile_constants()
 
     def visit(step, carry):
@@ -287,7 +287,7 @@
         held = {}
 
         def weigh(j):
-            scaled, half, potential = tile_parts(*tile_of(entries[j]), consts)
+            scaled, half, potential = tile_parts(*tile_of(step, j), consts)
             far = far_factor(scaled, half, consts)
             exponent = jnp.dot(near_ref[row[j]], far, preferred_element_type=f32)
             held[j] = exponent, packed_potential(potential), potential
@@ -329,7 +329,7 @@
                 store(t - LAG - 1)
         return carry
 
-    lax.fori_loop(0, ENTRIES // unroll, visit, 0)
+    lax.fori_loop(0, steps, visit, 0)
 
 
 def split_row(unroll, row_ref):
@@ -352,11 +352,11 @@
     row_messages(low_row, high_row, col_lo, col_hi, low_out, high_out)
     loc_ref[...] = jnp.zeros((ROWS, 8, NODES), f32)
 
-    def tile_of(e):
-        tile = recv_ref[e]
+    def tile_of(step, j):
+        tile = recv_ref[step * FIRST_UNROLL + j]
         return tile, pltpu.roll(tile, 5, 0)
 
-    pair_loop(FIRST_UNROLL, split_row(FIRST_UNROLL, row_ref), tile_of, near_ref, loc_ref, pot_ref, tail_ref, out_ref)
+    pair_loop(ENTRIES // FIRST_UNROLL, FIRST_UNROLL, split_row(FIRST_UNROLL, row_ref), tile_of, near_ref, loc_ref, pot_ref, tail_ref, out_ref)
 
 
 def contact_last(row_ref, home_ref, first_ref, x_ref, new_ref, disp_ref, vel_ref, loc_ref, near_ref, surf_ref):
@@ -385,8 +385,19 @@
         disp = jnp.where(row == 0, x, jnp.where(row == 1, y, z))
         return disp + time_step * vel, vel
 
-    pair_loop(LAST_UNROLL, split_row(LAST_UNROLL, row_ref), faced, near_ref, loc_ref)
-    pair_loop(LAST_UNROLL, lambda step, j: home_ref[step * LAST_UNROLL + j], facing, near_ref, loc_ref)
+    faced_row = split_row(LAST_UNROLL, row_ref)
+
+    def row_of(step, j):
+        if j < LAST_UNROLL:
+            return faced_row(step, j)
+        return home_ref[step * LAST_UNROLL + j - LAST_UNROLL]
+
+    def tile_of(step, j):
+        if j < LAST_UNROLL:
+            return faced(step * LAST_UNROLL + j)
+        return facing(step * LAST_UNROLL + j - LAST_UNROLL)
+
+    pair_loop(ENTRIES // LAST_UNROLL, 2 * LAST_UNROLL, row_of, tile_of, near_ref, loc_ref)
 
 
 def plane_frame(c):

time: 105 us -> 104 us (level)
  no operation moved by 1% of the time
where the time goes in v5:
time: 104 us
  starting transfers between devices  50.3 us (48%)
  Pallas kernels  30.8 us (30%)
  waiting for transfers between devices  21 us (20%)
    ppermute x8, starting transfers between devices, shifted(): return lax.ppermute(value, AXES, pairs)  26.5 us
    all_to_all x3, starting transfers between devices, exchange(): return lax.all_to_all(value, AXES, 0, 0, tiled=True)  23.8 us
    ppermute x8, waiting for transfers between devices, shifted(): return lax.ppermute(value, AXES, pairs)  16.1 us
    pallas_call x1, Pallas kernels, local(): call(contact_last, 'contact_last', [SMEM] * 2 + [VMEM] * 5, [VMEM], [tile...  12.1 us
    pallas_call x1, Pallas kernels, local(): call(contact_first, 'contact_first', [VMEM] * 8, [VMEM] * 4 + [SMEM], [en...  9.44 us
    all_to_all x3, waiting for transfers between devices, exchange(): return lax.all_to_all(value, AXES, 0, 0, tiled=True)  4.97 us
    pallas_call x1, Pallas kernels, local(): pl.pallas_call(request_kernel, in_specs=[HBM] * 3, out_specs=[VMEM, SMEM,...  3.73 us
  transfers between devices with their start and end apart: 11, of which 5 were waited for; matrix products, arithmetic and copies ran while one was open for 0% of the time, Pallas kernels for 14%

profile of v5, /device:TPU:7, one launch (start us, length us, event | category | flops | bytes accessed | tf_op | source)
XLA Modules:
  0.0 103.7 jit_solution(9802542881867603742)
XLA Ops:
  0.6 3.7 %request.1 = (f32[256,8,128]{2,1,0:T(8,128)}, s32[256]{0:T(256)S(4)}, s32[256]{0:T(256)S(4)}, f32[32,8,128]{2,1,0:T(8,128)S(1)}) custom-call(s32[8,32]{1,0:T(8,128)} %bitcast.20, f32[3,5,32,128]{3,2,1,0:T(8,128)} %bitcast.11, f32[3,5,32,128]{3,2,1,0:T(8,128)} %bitcast.15), custom_call_target="tpu_custom_call" | custom-call | tf_op jit(solution)/shard_map/request/pallas_call | solution.py:522
  4.4 10.8 %all-to-all-start = ((f32[256,8,128]{2,1,0:T(8,128)}), f32[256,8,128]{2,1,0:T(8,128)S(1)}, u32[]{:S(2)}, u32[]{:S(2)}) async-start(f32[256,8,128]{2,1,0:T(8,128)} %get-tuple-element.35), calls=%async_computation | async-start | bytes 2097152 | tf_op jit(solution)/shard_map/all_to_all | solution.py:553
  15.3 0.8 edges_first.1
  16.1 3.1 %collective-permute-start = (f32[32,128]{1,0:T(8,128)S(1)}, f32[32,128]{1,0:T(8,128)S(1)}, u32[]{:S(2)}, u32[]{:S(2)}) collective-permute-start(f32[32,128]{1,0:T(8,128)S(1)} %get-tuple-element.42), channel_id=1, source_target_pairs={{0,1},{1,2},{2,3},{3,4},{4,5},{5,6},{6,7},{7,8},{8,9},{9,10},{10,1... | collective-permute-start | bytes 49160 | tf_op jit(solution)/shard_map/ppermute | solution.py:501
  19.2 4.3 %collective-permute-start.1 = (f32[32,128]{1,0:T(8,128)S(1)}, f32[32,128]{1,0:T(8,128)S(1)}, u32[]{:S(2)}, u32[]{:S(2)}) collective-permute-start(f32[32,128]{1,0:T(8,128)S(1)} %get-tuple-element.43), channel_id=1, source_target_pairs={{1,0},{2,1},{3,2},{4,3},{5,4},{6,5},{7,6},{8,7},{9,8},{10,9},{11,1... | collective-permute-start | bytes 49160 | tf_op jit(solution)/shard_map/ppermute | solution.py:501
  23.5 0.6 tables_first.1
  24.1 5.6 %collective-permute-done.col_lo.refs_4_ = f32[32,128]{1,0:T(8,128)S(1)} collective-permute-done((f32[32,128]{1,0:T(8,128)S(1)}, f32[32,128]{1,0:T(8,128)S(1)}, u32[]{:S(2)}, u32[]{:S(2)}) %collective-permute-start) | collective-permute-done | bytes 16416 | tf_op jit(solution)/shard_map/ppermute | solution.py:501
  29.7 3.2 %all-to-all-done.recv_ref.first_ref = f32[256,8,128]{2,1,0:T(8,128)S(1)} async-done(((f32[256,8,128]{2,1,0:T(8,128)}), f32[256,8,128]{2,1,0:T(8,128)S(1)}, u32[]{:S(2)}, u32[]{:S(2)}) %all-to-all-start) | async-done | bytes 1048608 | tf_op jit(solution)/shard_map/all_to_all | solution.py:553
  32.9 9.4 %contact_first.1 = (f32[256,4,128]{2,1,0:T(4,128)}, f32[32,8,128]{2,1,0:T(8,128)S(1)}, f32[32,128]{1,0:T(8,128)S(1)}, f32[32,128]{1,0:T(8,128)S(1)}, s32[2,128]{1,0:T(2,128)S(4)}) custom-call(f32[256,8,128]{2,1,0:T(8,128)S(1)} %all-to-all-done.recv_ref.first_ref, bf16[32,128,48]{2,1,0:T(8,128)(2,1)S(1)} %get-tuple-element.37.near_ref, ...), custom_call_target="tpu_custom_call" | custom-call | tf_op jit(solution)/shard_map/contact_first/pallas_call | solution.py:583
  42.3 5.9 %all-to-all-start.1 = ((f32[256,4,128]{2,1,0:T(4,128)}), f32[256,4,128]{2,1,0:T(4,128)S(1)}, u32[]{:S(2)}, u32[]{:S(2)}) async-start(f32[256,4,128]{2,1,0:T(4,128)} %get-tuple-element.45), calls=%async_computation.1 | async-start | bytes 1048576 | tf_op jit(solution)/shard_map/all_to_all | solution.py:553
  48.2 3.7 %collective-permute-start.2 = (f32[32,128]{1,0:T(8,128)S(1)}, f32[32,128]{1,0:T(8,128)S(1)}, u32[]{:S(2)}, u32[]{:S(2)}) collective-permute-start(f32[32,128]{1,0:T(8,128)S(1)} %get-tuple-element.48), channel_id=1, source_target_pairs={{0,16},{1,17},{2,18},{3,19},{4,20},{5,21},{6,22},{7,23},{8,24},{9,... | collective-permute-start | bytes 49160 | tf_op jit(solution)/shard_map/ppermute | solution.py:501
  52.0 1.9 %collective-permute-start.3 = (f32[32,128]{1,0:T(8,128)S(1)}, f32[32,128]{1,0:T(8,128)S(1)}, u32[]{:S(2)}, u32[]{:S(2)}) collective-permute-start(f32[32,128]{1,0:T(8,128)S(1)} %get-tuple-element.49), channel_id=1, source_target_pairs={{16,0},{17,1},{18,2},{19,3},{20,4},{21,5},{22,6},{23,7},{24,8},{25... | collective-permute-start | bytes 49160 | tf_op jit(solution)/shard_map/ppermute | solution.py:501
  53.9 3.6 %collective-permute-done.3.refs_3_ = f32[32,128]{1,0:T(8,128)S(1)} collective-permute-done((f32[32,128]{1,0:T(8,128)S(1)}, f32[32,128]{1,0:T(8,128)S(1)}, u32[]{:S(2)}, u32[]{:S(2)}) %collective-permute-start.3) | collective-permute-done | bytes 16416 | tf_op jit(solution)/shard_map/ppermute | solution.py:501
  58.2 0.6 copy-done.4
  58.8 1.8 %all-to-all-done.1.ret_ref.x_ref = f32[256,4,128]{2,1,0:T(4,128)S(1)} async-done(((f32[256,4,128]{2,1,0:T(4,128)}), f32[256,4,128]{2,1,0:T(4,128)S(1)}, u32[]{:S(2)}, u32[]{:S(2)}) %all-to-all-start.1) | async-done | bytes 524320 | tf_op jit(solution)/shard_map/all_to_all | solution.py:553
  60.6 2.1 %update_first.1 = (f32[3,5,32,128]{3,2,1,0:T(8,128)S(1)}, f32[3,5,32,128]{3,2,1,0:T(8,128)S(1)}, f32[256,8,128]{2,1,0:T(8,128)}) custom-call(s32[256]{0:T(256)S(4)} %get-tuple-element.33.slot_ref, s32[256]{0:T(256)S(4)} %get-tuple-element.34.home_ref, s32[2,128]{1,0:T(2,128)S(4)} %get-tuple-element.44.row_ref, ...), custom_call_target="tpu_custom_call" | custom-call | tf_op jit(solution)/shard_map/update_first/pallas_call | solution.py:602
  62.6 7.1 %all-to-all-start.2 = ((f32[256,8,128]{2,1,0:T(8,128)}), f32[256,8,128]{2,1,0:T(8,128)S(1)}, u32[]{:S(2)}, u32[]{:S(2)}) async-start(f32[256,8,128]{2,1,0:T(8,128)} %get-tuple-element.53), calls=%async_computation.2 | async-start | bytes 2097152 | tf_op jit(solution)/shard_map/all_to_all | solution.py:553
  69.9 3.1 %collective-permute-start.4 = (f32[32,128]{1,0:T(8,128)S(1)}, f32[32,128]{1,0:T(8,128)S(1)}, u32[]{:S(2)}, u32[]{:S(2)}) collective-permute-start(f32[32,128]{1,0:T(8,128)S(1)} %get-tuple-element.58), channel_id=1, source_target_pairs={{0,1},{1,2},{2,3},{3,4},{4,5},{5,6},{6,7},{7,8},{8,9},{9,10},{10,1... | collective-permute-start | bytes 49160 | tf_op jit(solution)/shard_map/ppermute | solution.py:501
  73.0 4.3 %collective-permute-start.5 = (f32[32,128]{1,0:T(8,128)S(1)}, f32[32,128]{1,0:T(8,128)S(1)}, u32[]{:S(2)}, u32[]{:S(2)}) collective-permute-start(f32[32,128]{1,0:T(8,128)S(1)} %get-tuple-element.59), channel_id=1, source_target_pairs={{1,0},{2,1},{3,2},{4,3},{5,4},{6,5},{7,6},{8,7},{9,8},{10,9},{11,1... | collective-permute-start | bytes 49160 | tf_op jit(solution)/shard_map/ppermute | solution.py:501
  77.3 6.9 %collective-permute-done.4.col_lo = f32[32,128]{1,0:T(8,128)S(1)} collective-permute-done((f32[32,128]{1,0:T(8,128)S(1)}, f32[32,128]{1,0:T(8,128)S(1)}, u32[]{:S(2)}, u32[]{:S(2)}) %collective-permute-start.4) | collective-permute-done | bytes 16416 | tf_op jit(solution)/shard_map/ppermute | solution.py:501
  84.2 4.1 %collective-permute-start.6 = (f32[32,128]{1,0:T(8,128)S(1)}, f32[32,128]{1,0:T(8,128)S(1)}, u32[]{:S(2)}, u32[]{:S(2)}) collective-permute-start(f32[32,128]{1,0:T(8,128)S(1)} %get-tuple-element.60), channel_id=1, source_target_pairs={{0,16},{1,17},{2,18},{3,19},{4,20},{5,21},{6,22},{7,23},{8,24},{9,... | collective-permute-start | bytes 49160 | tf_op jit(solution)/shard_map/ppermute | solution.py:501
  88.3 1.9 %collective-permute-start.7 = (f32[32,128]{1,0:T(8,128)S(1)}, f32[32,128]{1,0:T(8,128)S(1)}, u32[]{:S(2)}, u32[]{:S(2)}) collective-permute-start(f32[32,128]{1,0:T(8,128)S(1)} %get-tuple-element.61), channel_id=1, source_target_pairs={{16,0},{17,1},{18,2},{19,3},{20,4},{21,5},{22,6},{23,7},{24,8},{25... | collective-permute-start | bytes 49160 | tf_op jit(solution)/shard_map/ppermute | solution.py:501
  90.3 12.1 %contact_last.1.loc_ref = f32[32,8,128]{2,1,0:T(8,128)S(1)} custom-call(s32[2,128]{1,0:T(2,128)S(4)} %get-tuple-element.44.row_ref, s32[256]{0:T(256)S(4)} %get-tuple-element.34.home_ref, f32[256,8,128]{2,1,0:T(8,128)S(1)} %all-to-all-done.recv_ref.first_ref, f32[256,4,128]{2,1,0:T(4,128)S(1)} %all-to-all-done.1.ret_ref.x_ref, ...), custom_call_target="tpu_custom_call" | custom-call | tf_op jit(solution)/shard_map/contact_last/pallas_call | solution.py:629
  102.4 1.3 %update_last.1 = (f32[3,5,32,128]{3,2,1,0:T(8,128)}, f32[3,5,32,128]{3,2,1,0:T(8,128)}) custom-call(f32[3,5,32,128]{3,2,1,0:T(8,128)S(1)} %get-tuple-element.51.disp_ref.refs_0_, f32[3,5,32,128]{3,2,1,0:T(8,128)S(1)} %get-tuple-element.52.vel_ref, f32[5,32,128]{2,1,0:T(8,128)S(1)} %bitcast.18, f32[32,8,128]{2,1,0:T(8,128)S(1)} %contact_last.1.loc_ref, ...), custom_call_target="tpu_custom_call" | custom-call | tf_op jit(solution)/shard_map/update_last/pallas_call | solution.py:637
  (21 shorter events, 0.9 us)
Async XLA Ops:
  4.4 10.9 %copy-start = (f32[3,32,5,128]{3,1,2,0:T(8,128)S(1)}, f32[3,32,5,128]{3,1,2,0:T(8,128)}, u32[]{:S(2)}) copy-start(f32[3,32,5,128]{3,1,2,0:T(8,128)} %param.5) | copy-start | bytes 737284
  4.4 10.9 %copy-start.3 = (f32[32,5,128]{2,0,1:T(8,128)S(1)}, f32[32,5,128]{2,0,1:T(8,128)}, u32[]{:S(2)}) copy-start(f32[32,5,128]{2,0,1:T(8,128)} %param.7) | copy-start | bytes 245764
  4.4 28.5 %all-to-all-start = ((f32[256,8,128]{2,1,0:T(8,128)}), f32[256,8,128]{2,1,0:T(8,128)S(1)}, u32[]{:S(2)}, u32[]{:S(2)}) async-start(f32[256,8,128]{2,1,0:T(8,128)} %get-tuple-element.35), calls=%async_computation | async-start | bytes 2097152 | tf_op jit(solution)/shard_map/all_to_all | solution.py:553
  16.1 13.6 %collective-permute-start = (f32[32,128]{1,0:T(8,128)S(1)}, f32[32,128]{1,0:T(8,128)S(1)}, u32[]{:S(2)}, u32[]{:S(2)}) collective-permute-start(f32[32,128]{1,0:T(8,128)S(1)} %get-tuple-element.42), channel_id=1, source_target_pairs={{0,1},{1,2},{2,3},{3,4},{4,5},{5,6},{6,7},{7,8},{8,9},{9,10},{10,1... | collective-permute-start | bytes 49160 | tf_op jit(solution)/shard_map/ppermute | solution.py:501
  19.2 10.5 %collective-permute-start.1 = (f32[32,128]{1,0:T(8,128)S(1)}, f32[32,128]{1,0:T(8,128)S(1)}, u32[]{:S(2)}, u32[]{:S(2)}) collective-permute-start(f32[32,128]{1,0:T(8,128)S(1)} %get-tuple-element.43), channel_id=1, source_target_pairs={{1,0},{2,1},{3,2},{4,3},{5,4},{6,5},{7,6},{8,7},{9,8},{10,9},{11,1... | collective-permute-start | bytes 49160 | tf_op jit(solution)/shard_map/ppermute | solution.py:501
  42.3 18.2 %all-to-all-start.1 = ((f32[256,4,128]{2,1,0:T(4,128)}), f32[256,4,128]{2,1,0:T(4,128)S(1)}, u32[]{:S(2)}, u32[]{:S(2)}) async-start(f32[256,4,128]{2,1,0:T(4,128)} %get-tuple-element.45), calls=%async_computation.1 | async-start | bytes 1048576 | tf_op jit(solution)/shard_map/all_to_all | solution.py:553
  48.2 12.3 %copy-start.1 = (f32[3,32,5,128]{3,1,2,0:T(8,128)S(1)}, f32[3,32,5,128]{3,1,2,0:T(8,128)}, u32[]{:S(2)}) copy-start(f32[3,32,5,128]{3,1,2,0:T(8,128)} %param.6) | copy-start | bytes 737284
  48.2 5.7 %collective-permute-start.2 = (f32[32,128]{1,0:T(8,128)S(1)}, f32[32,128]{1,0:T(8,128)S(1)}, u32[]{:S(2)}, u32[]{:S(2)}) collective-permute-start(f32[32,128]{1,0:T(8,128)S(1)} %get-tuple-element.48), channel_id=1, source_target_pairs={{0,16},{1,17},{2,18},{3,19},{4,20},{5,21},{6,22},{7,23},{8,24},{9,... | collective-permute-start | bytes 49160 | tf_op jit(solution)/shard_map/ppermute | solution.py:501
  52.0 5.6 %collective-permute-start.3 = (f32[32,128]{1,0:T(8,128)S(1)}, f32[32,128]{1,0:T(8,128)S(1)}, u32[]{:S(2)}, u32[]{:S(2)}) collective-permute-start(f32[32,128]{1,0:T(8,128)S(1)} %get-tuple-element.49), channel_id=1, source_target_pairs={{16,0},{17,1},{18,2},{19,3},{20,4},{21,5},{22,6},{23,7},{24,8},{25... | collective-permute-start | bytes 49160 | tf_op jit(solution)/shard_map/ppermute | solution.py:501
  57.5 3.0 %copy-start.2 = (f32[32,5,128]{2,0,1:T(8,128)S(1)}, f32[32,5,128]{2,0,1:T(8,128)}, u32[]{:S(2)}) copy-start(f32[32,5,128]{2,0,1:T(8,128)} %param.8) | copy-start | bytes 245764
  58.2 0.6 copy-start.4
  62.6 27.6 %all-to-all-start.2 = ((f32[256,8,128]{2,1,0:T(8,128)}), f32[256,8,128]{2,1,0:T(8,128)S(1)}, u32[]{:S(2)}, u32[]{:S(2)}) async-start(f32[256,8,128]{2,1,0:T(8,128)} %get-tuple-element.53), calls=%async_computation.2 | async-start | bytes 2097152 | tf_op jit(solution)/shard_map/all_to_all | solution.py:553
  69.9 14.3 %collective-permute-start.4 = (f32[32,128]{1,0:T(8,128)S(1)}, f32[32,128]{1,0:T(8,128)S(1)}, u32[]{:S(2)}, u32[]{:S(2)}) collective-permute-start(f32[32,128]{1,0:T(8,128)S(1)} %get-tuple-element.58), channel_id=1, source_target_pairs={{0,1},{1,2},{2,3},{3,4},{4,5},{5,6},{6,7},{7,8},{8,9},{9,10},{10,1... | collective-permute-start | bytes 49160 | tf_op jit(solution)/shard_map/ppermute | solution.py:501
  73.0 11.2 %collective-permute-start.5 = (f32[32,128]{1,0:T(8,128)S(1)}, f32[32,128]{1,0:T(8,128)S(1)}, u32[]{:S(2)}, u32[]{:S(2)}) collective-permute-start(f32[32,128]{1,0:T(8,128)S(1)} %get-tuple-element.59), channel_id=1, source_target_pairs={{1,0},{2,1},{3,2},{4,3},{5,4},{6,5},{7,6},{8,7},{9,8},{10,9},{11,1... | collective-permute-start | bytes 49160 | tf_op jit(solution)/shard_map/ppermute | solution.py:501
  84.2 18.2 %collective-permute-start.6 = (f32[32,128]{1,0:T(8,128)S(1)}, f32[32,128]{1,0:T(8,128)S(1)}, u32[]{:S(2)}, u32[]{:S(2)}) collective-permute-start(f32[32,128]{1,0:T(8,128)S(1)} %get-tuple-element.60), channel_id=1, source_target_pairs={{0,16},{1,17},{2,18},{3,19},{4,20},{5,21},{6,22},{7,23},{8,24},{9,... | collective-permute-start | bytes 49160 | tf_op jit(solution)/shard_map/ppermute | solution.py:501
  88.3 14.0 %collective-permute-start.7 = (f32[32,128]{1,0:T(8,128)S(1)}, f32[32,128]{1,0:T(8,128)S(1)}, u32[]{:S(2)}, u32[]{:S(2)}) collective-permute-start(f32[32,128]{1,0:T(8,128)S(1)} %get-tuple-element.61), channel_id=1, source_target_pairs={{16,0},{17,1},{18,2},{19,3},{20,4},{21,5},{22,6},{23,7},{24,8},{25... | collective-permute-start | bytes 49160 | tf_op jit(solution)/shard_map/ppermute | solution.py:501
  90.3 12.1 %copy-start.5 = (f32[5,32,128]{2,1,0:T(8,128)S(1)}, f32[5,32,128]{2,1,0:T(8,128)}, u32[]{:S(2)}) copy-start(f32[5,32,128]{2,1,0:T(8,128)} %copy-done.4) | copy-start | bytes 245764
